TPU v7x, 32 devices: a whole 2x2x4 slice. The times are simulated.
32 devices in a mesh: tower: 2 (over x), crops: 16 (over z, y, core).
Axes of the slice: x: 2, y: 2, z: 4, core: 2. Of those that a mesh axis runs over, the one named last changes fastest.
Arguments:
- features: bfloat16 [2, 2048, 13, 13, 384], P('tower', 'crops'), may hold values from -6 to 6
- conv_weight: bfloat16 [2, 3, 3, 384, 256], P('tower'), may hold values from -0.109375 to 0.109375
- conv_bias: float32 [2, 256], P('tower'), may hold values from -3 to 3
- fc_weight: bfloat16 [2, 9216, 4096], P('tower', 'crops'), may hold values from -0.0625 to 0.0625
- fc_bias: float32 [2, 4096], P('tower'), may hold values from -3 to 3
- stitch_pool: float32 [2, 2, 256], P('tower'), may hold values from 0.2 to 1
- stitch_fc: float32 [2, 2, 4096], P('tower'), may hold values from 0.2 to 1
- cotangent: bfloat16 [2, 2048, 4096], P('tower', 'crops'), may hold values from -6 to 6
- crop_counts: int32 [512], P('crops'), may hold values from 1 to 4
- slot_image: int32 [2048], P('crops'), may hold values from 0 to 31, as said below
- slot_mask: int32 [2048], P('crops'), may hold values from 0 to 1, as said below
Outputs:
- output: bfloat16 [2, 2048, 4096], P('tower', 'crops')
- grad_features: bfloat16 [2, 2048, 13, 13, 384], P('tower', 'crops')
- grad_conv_weight: float32 [2, 3, 3, 384, 256], P('tower')
- grad_conv_bias: float32 [2, 256], P('tower')
- grad_fc_weight: float32 [2, 9216, 4096], P('tower', 'crops')
- grad_fc_bias: float32 [2, 4096], P('tower')
- grad_stitch_pool: float32 [2, 2, 256], P('tower')
- grad_stitch_fc: float32 [2, 2, 4096], P('tower')
Inputs may be any that keep to these rules, and one draw needn't show every extreme that they name: Within each device's 128 slots the numbers never fall; slot_image names one of that device's 32 images, and the first and last slot of each device name images 0 and 31. `slot_mask`: each device's live slots come first; every device has at least 64 live slots, and in every draw some device has all 128 live.
All inputs are finite; a program needn't handle non-finite values.
Results may differ from a plain program's by a relative error of at most 0.0082.
Values may be sent and summed in bfloat16 or wider, within the bound.
No kernel may reach another device: no remote copies, remote signals or barrier semaphores. Data moves between devices by JAX's collectives and lax.ppermute only.
A program may use at most 704 MiB of HBM per device.

v0:
```python
import jax
import jax.numpy as jnp
from jax import lax
from jax.sharding import PartitionSpec as P


def partner(block, axis, distance):
    count = lax.axis_size(axis)
    route = []
    for low in range(count):
        high = low | 1 << distance
        if high != low and high < count:
            route += [(low, high), (high, low)]
    return lax.ppermute(block, axis, route)


def smooth_gelu(argument):
    return jax.nn.gelu(argument, approximate=True)


def smooth_pool(activity):
    extent = activity.shape[1]
    stride_span = 2 * ((extent - 3) // 2 + 1) - 1
    summed = jnp.zeros(
        (activity.shape[0], (extent - 3) // 2 + 1, (extent - 3) // 2 + 1, activity.shape[3]),
        jnp.float32,
    )
    for row_shift in range(3):
        for col_shift in range(3):
            window = activity[
                :,
                row_shift : row_shift + stride_span : 2,
                col_shift : col_shift + stride_span : 2,
                :,
            ]
            summed = summed + jnp.exp(window)
    return jnp.log(summed)


def conv_apply(inputs, kernel):
    extent = inputs.shape[1]
    padded = jnp.pad(inputs, ((0, 0), (1, 1), (1, 1), (0, 0)))
    summed = jnp.zeros(inputs.shape[:3] + (kernel.shape[3],), jnp.float32)
    for row_shift in range(3):
        for col_shift in range(3):
            window = padded[:, row_shift : row_shift + extent, col_shift : col_shift + extent, :]
            summed = summed + jnp.einsum(
                "bhwc,cd->bhwd",
                window,
                kernel[row_shift, col_shift],
                preferred_element_type=jnp.float32,
            )
    return summed


def conv_back(inputs, kernel, grad_pre):
    extent = inputs.shape[1]
    padded = jnp.pad(inputs, ((0, 0), (1, 1), (1, 1), (0, 0)))
    kernel_rows = []
    grad_padded = jnp.zeros((inputs.shape[0], extent + 2, extent + 2, inputs.shape[3]), jnp.float32)
    for row_shift in range(3):
        for col_shift in range(3):
            window = padded[:, row_shift : row_shift + extent, col_shift : col_shift + extent, :]
            kernel_rows.append(
                jnp.einsum("bhwc,bhwd->cd", window, grad_pre, preferred_element_type=jnp.float32)
            )
            backed = jnp.einsum(
                "bhwd,cd->bhwc",
                grad_pre,
                kernel[row_shift, col_shift],
                preferred_element_type=jnp.float32,
            )
            grad_padded = grad_padded + jnp.pad(
                backed, ((0, 0), (row_shift, 2 - row_shift), (col_shift, 2 - col_shift), (0, 0))
            )
    grad_kernel = jnp.stack(kernel_rows).reshape(kernel.shape)
    return (grad_kernel, grad_padded[:, 1 : extent + 1, 1 : extent + 1, :])


def body(
    features,
    conv_weight,
    conv_bias,
    fc_weight,
    fc_bias,
    stitch_pool,
    stitch_fc,
    cotangent,
    crop_counts,
    slot_image,
    slot_mask,
):
    is_first = lax.axis_index("tower") == 0
    inputs = features[0]
    kernel = conv_weight[0]
    pre_conv = conv_apply(inputs, kernel) + conv_bias[0]
    activity, gelu_conv_back = jax.vjp(smooth_gelu, pre_conv)
    pool_exact, pool_pullback = jax.vjp(smooth_pool, activity)
    pooled = pool_exact.astype(jnp.bfloat16)
    partner_pool = partner(pooled, "tower", 0)
    row_pool = stitch_pool[0]
    self_pool = jnp.where(is_first, row_pool[0], row_pool[1])
    cross_pool = jnp.where(is_first, row_pool[1], row_pool[0])
    slot_count = pooled.shape[0]
    mixed = (
        self_pool * pooled.astype(jnp.float32) + cross_pool * partner_pool.astype(jnp.float32)
    ).astype(jnp.bfloat16)
    mixed = mixed.reshape(slot_count, -1)
    weight_rows = fc_weight[0]
    columns = mixed
    pre_fc = jnp.dot(
        columns,
        lax.all_gather(weight_rows, "crops", axis=0, tiled=True),
        preferred_element_type=jnp.float32,
    )
    pre_fc = pre_fc + fc_bias[0]
    hidden_exact, gelu_fc_back = jax.vjp(smooth_gelu, pre_fc)
    hidden = hidden_exact.astype(jnp.bfloat16)
    partner_hidden = partner(hidden, "tower", 0)
    row_fc = stitch_fc[0]
    self_fc = jnp.where(is_first, row_fc[0], row_fc[1])
    cross_fc = jnp.where(is_first, row_fc[1], row_fc[0])
    stitched = self_fc * hidden.astype(jnp.float32) + cross_fc * partner_hidden.astype(jnp.float32)
    live_slots = slot_mask.astype(jnp.float32)
    output = (stitched * live_slots[:, None]).astype(jnp.bfloat16)
    image_ids = jnp.arange(crop_counts.shape[0], dtype=jnp.int32)
    matches = (slot_image[:, None] == image_ids[None, :]).astype(jnp.float32)
    per_slot = jnp.sum(matches * crop_counts.astype(jnp.float32)[None, :], axis=1)
    scaling = live_slots / per_slot
    grad_out = cotangent[0].astype(jnp.float32) * scaling[:, None]
    grad_self_fc = jnp.sum(hidden.astype(jnp.float32) * grad_out, axis=0)
    grad_cross_fc = jnp.sum(partner_hidden.astype(jnp.float32) * grad_out, axis=0)
    grad_row_fc = jnp.where(
        is_first, jnp.stack([grad_self_fc, grad_cross_fc]), jnp.stack([grad_cross_fc, grad_self_fc])
    )
    sent_fc = (cross_fc * grad_out).astype(jnp.bfloat16)
    back_fc = partner(sent_fc, "tower", 0)
    grad_hidden = self_fc * grad_out + back_fc.astype(jnp.float32)
    grad_pre_fc = gelu_fc_back(grad_hidden)[0].astype(jnp.bfloat16)
    grad_fc_bias = jnp.sum(grad_pre_fc.astype(jnp.float32), axis=0)
    grad_mixed = lax.dot_general(
        grad_pre_fc,
        lax.all_gather(weight_rows, "crops", axis=0, tiled=True),
        (((1,), (1,)), ((), ())),
        preferred_element_type=jnp.float32,
    )
    columns = mixed
    grad_fc_weight = lax.psum_scatter(
        lax.dot_general(
            columns, grad_pre_fc, (((0,), (0,)), ((), ())), preferred_element_type=jnp.float32
        ),
        "crops",
        scatter_dimension=0,
        tiled=True,
    )
    grad_mixed = grad_mixed.reshape(pooled.shape)
    grad_self_pool = jnp.sum(pooled.astype(jnp.float32) * grad_mixed, axis=(0, 1, 2))
    grad_cross_pool = jnp.sum(partner_pool.astype(jnp.float32) * grad_mixed, axis=(0, 1, 2))
    grad_row_pool = jnp.where(
        is_first,
        jnp.stack([grad_self_pool, grad_cross_pool]),
        jnp.stack([grad_cross_pool, grad_self_pool]),
    )
    sent_pool = (cross_pool * grad_mixed).astype(jnp.bfloat16)
    back_pool = partner(sent_pool, "tower", 0)
    grad_pooled = self_pool * grad_mixed + back_pool.astype(jnp.float32)
    grad_activity = pool_pullback(grad_pooled)[0]
    grad_pre_conv = gelu_conv_back(grad_activity)[0].astype(jnp.bfloat16)
    grad_conv_bias = jnp.sum(grad_pre_conv.astype(jnp.float32), axis=(0, 1, 2))
    grad_kernel, grad_inputs = conv_back(inputs, kernel, grad_pre_conv)
    summed_kernel, summed_conv_bias, summed_fc_bias, summed_pool, summed_fc = lax.psum(
        (grad_kernel, grad_conv_bias, grad_fc_bias, grad_row_pool, grad_row_fc), "crops"
    )
    return (
        output[None],
        grad_inputs.astype(jnp.bfloat16)[None],
        summed_kernel[None],
        summed_conv_bias[None],
        grad_fc_weight[None],
        summed_fc_bias[None],
        summed_pool[None],
        summed_fc[None],
    )


def solution(mesh):
    placed = (
        P("tower", "crops", None, None, None),
        P("tower", None, None, None, None),
        P("tower", None),
        P("tower", "crops", None),
        P("tower", None),
        P("tower", None, None),
        P("tower", None, None),
        P("tower", "crops", None),
        P("crops"),
        P("crops"),
        P("crops"),
    )
    return jax.shard_map(
        body,
        mesh=mesh,
        in_specs=placed,
        out_specs=(
            P("tower", "crops", None),
            P("tower", "crops", None, None, None),
            P("tower", None, None, None, None),
            P("tower", None),
            P("tower", "crops", None),
            P("tower", None),
            P("tower", None, None),
            P("tower", None, None),
        ),
        check_vma=False,
    )
```

profile of v0, /device:TPU:1, one launch (start us, length us, event | category | flops | bytes accessed | tf_op | source)
XLA Modules:
  0.0 2450.4 jit_solution(2233461885350318876)
XLA Ops:
  121.4 79.2 %multiply_multiply_fusion.2 = (f32[128,13,13,256]{3,0,2,1:T(8,128)}, f32[128,13,13,256]{3,0,2,1:T(8,128)}) fusion(f32[256]{0:T(256)S(1)} %bitcast.314, f32[128,13,13,256]{3,0,2,1:T(8,128)} %fusion.26, f32[128,13,13,256]{3,0,2,1:T(8,128)} %fusion.28, f32[128,13,13,256]{3,0,2,1:T(8,128)} %fusion.30, f32[128,13,13,256]{3,0,2,1:T(8,128)} %fusion.32, ...), kind=kOutput, calls=%fused_computation.22 | convolution fusion | flops 4347166720 | bytes 238322688 | tf_op jit(solution)/shard_map/bhwc,cd->bhwd/dot_general | solution.py:47
  222.8 49.4 %collective-permute-done = bf16[128,6,6,256]{3,0,2,1:T(8,128)(2,1)} collective-permute-done((bf16[128,6,6,256]{3,0,2,1:T(8,128)(2,1)S(1)}, bf16[128,6,6,256]{3,0,2,1:T(8,128)(2,1)}, u32[]{:S(2)}, u32[]{:S(2)}) %collective-permute-start) | collective-permute-done | bytes 2359328 | tf_op jit(solution)/shard_map/ppermute | solution.py:14
  294.6 83.1 %all-gather.3.cloned.1.call-done = bf16[1,9216,4096]{2,1,0:T(8,128)(2,1)} async-done(((bf16[1,576,4096]{2,1,0:T(8,128)(2,1)}), bf16[1,9216,4096]{2,1,0:T(8,128)(2,1)}) %all-gather.3.cloned.1.call-update) | async-done | bytes 75497488 | tf_op jit(solution)/shard_map/all_gather | solution.py:113
  377.8 28.4 %convert_reduce_fusion.1 = (f32[4096]{0:T(1024)}, bf16[128,4096]{1,0:T(8,128)(2,1)S(1)}, bf16[128,4096]{1,0:T(8,128)(2,1)}) fusion(bf16[128,4096]{1,0:T(8,128)(2,1)} %collective-permute-done.2, f32[128]{0:T(128)S(1)} %convert_divide_fusion, bf16[1,128,4096]{2,1,0:T(8,128)(2,1)S(1)} %copy-done.7, f32[4096]{0:T(1024)S(1)} %bitcast.315, ...), kind=kOutput, calls=%fused_computation.114 | convolution fusion | flops 9679400960 | bytes 82100736 | tf_op jit(solution)/shard_map/dot_general | solution.py:111
  406.1 31.2 %fusion = f32[128,9216]{0,1:T(8,128)} fusion(bf16[128,4096]{1,0:T(8,128)(2,1)S(1)} %get-tuple-element.17, bf16[1,9216,4096]{2,1,0:T(8,128)(2,1)} %all-gather.3.cloned.1.call-done), kind=kOutput, calls=%fused_computation | convolution fusion | flops 9663676416 | bytes 81264640 | tf_op jit(solution)/shard_map/dot_general | solution.py:141
  449.8 51.4 %collective-permute-done.3 = bf16[128,6,6,256]{3,0,2,1:T(8,128)(2,1)S(1)} collective-permute-done((bf16[128,6,6,256]{3,0,2,1:T(8,128)(2,1)S(1)}, bf16[128,6,6,256]{3,0,2,1:T(8,128)(2,1)S(1)}, u32[]{:S(2)}, u32[]{:S(2)}) %collective-permute-start.3) | collective-permute-done | bytes 2359328 | tf_op jit(solution)/shard_map/ppermute | solution.py:14
  508.3 27.2 %fusion.64 = (f32[128,6,6,256]{3,0,2,1:T(8,128)}, f32[128,6,6,256]{3,0,2,1:T(8,128)}, f32[128,6,6,256]{3,0,2,1:T(8,128)}, f32[128,6,6,256]{3,0,2,1:T(8,128)}, f3...) fusion(f32[128,6,6,256]{3,0,2,1:T(8,128)} %get-tuple-element.21, ...), kind=kLoop, calls=%fused_computation.90 | loop fusion | flops 9437184 | bytes 80216064 | tf_op jit(solution)/shard_map/transpose(jvp())/mul | solution.py:36
  535.5 27.3 %pad.69 = f32[128,13,13,256]{3,0,2,1:T(8,128)} pad(f32[128,6,6,256]{3,0,2,1:T(8,128)} %get-tuple-element.24, f32[]{:T(128)} %constant.29.clone.1), padding=0_0_0x2_0_1x2_0_1x0_0_0 | pad | bytes 26869764 | tf_op jit(solution)/shard_map/transpose(jvp())/pad | solution.py:30
  562.8 27.2 %pad.70 = f32[128,13,13,256]{3,0,2,1:T(8,128)} pad(f32[128,6,6,256]{3,0,2,1:T(8,128)} %get-tuple-element.20, f32[]{:T(128)} %constant.29.clone.1), padding=0_0_0x2_0_1x1_1_1x0_0_0 | pad | bytes 26869764 | tf_op jit(solution)/shard_map/transpose(jvp())/pad | solution.py:30
  590.0 27.3 %pad.76 = f32[128,13,13,256]{3,0,2,1:T(8,128)} pad(f32[128,6,6,256]{3,0,2,1:T(8,128)} %get-tuple-element.25, f32[]{:T(128)} %constant.29.clone.1), padding=0_0_0x0_2_1x1_1_1x0_0_0 | pad | bytes 26869764 | tf_op jit(solution)/shard_map/transpose(jvp())/pad | solution.py:30
  617.2 27.3 %pad.75 = f32[128,13,13,256]{3,0,2,1:T(8,128)} pad(f32[128,6,6,256]{3,0,2,1:T(8,128)} %get-tuple-element.26, f32[]{:T(128)} %constant.29.clone.1), padding=0_0_0x0_2_1x2_0_1x0_0_0 | pad | bytes 26869764 | tf_op jit(solution)/shard_map/transpose(jvp())/pad | solution.py:30
  644.5 27.4 %pad.74 = f32[128,13,13,256]{3,0,2,1:T(8,128)} pad(f32[128,6,6,256]{3,0,2,1:T(8,128)} %get-tuple-element.27, f32[]{:T(128)} %constant.29.clone.1), padding=0_0_0x1_1_1x0_2_1x0_0_0 | pad | bytes 26869764 | tf_op jit(solution)/shard_map/transpose(jvp())/pad | solution.py:30
  671.9 27.3 %pad.73 = f32[128,13,13,256]{3,0,2,1:T(8,128)} pad(f32[128,6,6,256]{3,0,2,1:T(8,128)} %get-tuple-element.28, f32[]{:T(128)} %constant.29.clone.1), padding=0_0_0x1_1_1x1_1_1x0_0_0 | pad | bytes 26869764 | tf_op jit(solution)/shard_map/transpose(jvp())/pad | solution.py:30
  699.2 27.2 %pad.72 = f32[128,13,13,256]{3,0,2,1:T(8,128)} pad(f32[128,6,6,256]{3,0,2,1:T(8,128)} %get-tuple-element.29, f32[]{:T(128)} %constant.29.clone.1), padding=0_0_0x1_1_1x2_0_1x0_0_0 | pad | bytes 26869764 | tf_op jit(solution)/shard_map/transpose(jvp())/pad | solution.py:30
  726.4 27.3 %pad.71 = f32[128,13,13,256]{3,0,2,1:T(8,128)} pad(f32[128,6,6,256]{3,0,2,1:T(8,128)} %get-tuple-element.30, f32[]{:T(128)} %constant.29.clone.1), padding=0_0_0x2_0_1x0_2_1x0_0_0 | pad | bytes 26869764 | tf_op jit(solution)/shard_map/transpose(jvp())/pad | solution.py:30
  753.7 27.4 %pad.77 = f32[128,13,13,256]{3,0,2,1:T(8,128)} pad(f32[128,6,6,256]{3,0,2,1:T(8,128)} %get-tuple-element.31, f32[]{:T(128)} %constant.29.clone.1), padding=0_0_0x0_2_1x0_2_1x0_0_0 | pad | bytes 26869764 | tf_op jit(solution)/shard_map/transpose(jvp())/pad | solution.py:30
  781.0 74.6 %convert_reduce_fusion = (f32[256]{0:T(256)}, bf16[128,13,13,256]{3,0,2,1:T(8,128)(2,1)}) fusion(f32[128,13,13,256]{3,0,2,1:T(8,128)} %get-tuple-element.40, f32[128,13,13,256]{3,0,2,1:T(8,128)} %pad.77, f32[128,13,13,256]{3,0,2,1:T(8,128)} %pad.76, f32[128,13,13,256]{3,0,2,1:T(8,128)} %pad.75, f32[128,13,13,256]{3,0,2,1:T(8,128)} %pad.74, ...), kind=kLoop, calls=%fused_computation.20 | loop fusion | flops 166133504 | bytes 232588288 | tf_op jit(solution)/shard_map/reduce_sum | solution.py:169
  957.8 52.2 %fusion.151 = f32[9216,4096]{1,0:T(8,128)} fusion(bf16[128,9216]{0,1:T(8,128)(2,1)S(1)} %bitcast.294, bf16[128,4096]{1,0:T(8,128)(2,1)S(1)} %copy-done.6), kind=kOutput, calls=%fused_computation.164 | convolution fusion | flops 9663676416 | bytes 154402816 | tf_op jit(solution)/shard_map/dot_general | solution.py:149
  1011.5 22.6 collective-permute-done.1
  1037.3 57.4 %all-reduce.19 = (f32[1,256]{1,0:T(1,128)}, f32[1,4096]{1,0:T(1,128)}, f32[1,2,256]{2,1,0:T(2,128)}, f32[1,2,4096]{2,1,0:T(2,128)}) all-reduce(f32[1,256]{1,0:T(1,128)S(1)} %bitcast.329, f32[1,4096]{1,0:T(1,128)S(1)} %bitcast.319, f32[1,2,256]{2,1,0:T(2,128)S(1)} %fusion.148, ...), channel_id=1, replica_groups=mesh['tower'=2,'crops'=16] {'crops'}, use_global_device_ids=true, to_apply=%region_3.4 | all-reduce | flops 13056 | bytes 104448 | tf_op jit(solution)/shard_map/psum | solution.py:171
  1094.7 24.5 fusion.144
  1119.2 24.6 %fusion.141 = f32[128,13,13,384]{3,0,2,1:T(8,128)} fusion(bf16[128,13,13,256]{3,0,2,1:T(8,128)(2,1)} %get-tuple-element.19, bf16[3,3,384,256]{3,2,1,0:T(8,128)(2,1)S(1)} %bitcast.306), kind=kOutput, calls=%fused_computation.147 | convolution fusion | flops 4253024256 | bytes 44498944 | tf_op jit(solution)/shard_map/bhwd,cd->bhwc/dot_general | solution.py:67
  1143.7 24.5 fusion.140
  1168.2 24.9 %fusion.139 = f32[128,13,13,384]{3,0,2,1:T(8,128)} fusion(bf16[128,13,13,256]{3,0,2,1:T(8,128)(2,1)} %get-tuple-element.19, bf16[3,3,384,256]{3,2,1,0:T(8,128)(2,1)S(1)} %bitcast.308), kind=kOutput, calls=%fused_computation.145 | convolution fusion | flops 4253024256 | bytes 44498944 | tf_op jit(solution)/shard_map/bhwd,cd->bhwc/dot_general | solution.py:67
  1193.1 24.6 %fusion.138 = f32[128,13,13,384]{3,0,2,1:T(8,128)} fusion(bf16[128,13,13,256]{3,0,2,1:T(8,128)(2,1)} %get-tuple-element.19, bf16[3,3,384,256]{3,2,1,0:T(8,128)(2,1)S(1)} %bitcast.309), kind=kOutput, calls=%fused_computation.144 | convolution fusion | flops 4253024256 | bytes 44498944 | tf_op jit(solution)/shard_map/bhwd,cd->bhwc/dot_general | solution.py:67
  1217.7 72.4 %pad_add_fusion = f32[128,15,15,384]{3,0,2,1:T(8,128)} fusion(f32[128,13,13,384]{3,0,2,1:T(8,128)} %fusion.141, f32[128,13,13,384]{3,0,2,1:T(8,128)} %fusion.140, f32[128,13,13,384]{3,0,2,1:T(8,128)} %fusion.139, f32[128,13,13,384]{3,0,2,1:T(8,128)} %fusion.138), kind=kLoop, calls=%fused_computation.4 | loop fusion | flops 33177600 | bytes 177143808 | tf_op jit(solution)/shard_map/add | solution.py:73
  1290.1 23.4 fusion.146
  1313.5 23.3 fusion.145
  1336.8 23.5 fusion.143
  1360.4 23.0 fusion.142
  1383.4 67.7 %fusion.48 = bf16[1,128,13,13,384]{4,1,3,2,0:T(8,128)(2,1)} fusion(f32[128,15,15,384]{3,0,2,1:T(8,128)} %fusion.146, f32[128,15,15,384]{3,0,2,1:T(8,128)} %fusion.145, f32[128,13,13,384]{3,0,2,1:T(8,128)} %fusion.144, f32[128,15,15,384]{3,0,2,1:T(8,128)} %fusion.143, f32[128,15,15,384]{3,0,2,1:T(8,128)} %fusion.142, f32[128,15,15,384]{3,0,2,1:T(8,128)} %pad_add_fusion), kind=kLoop, calls=%fused_computation.59 | loop fusion | flops 49840128 | bytes 215973888 | tf_op jit(solution)/shard_map/broadcast_in_dim | solution.py:176
  1451.1 988.6 %reduce-scatter.2.cloned.1.call-done = f32[576,4096]{1,0:T(8,128)} async-done(((f32[9216,4096]{1,0:T(8,128)}), f32[576,4096]{1,0:T(8,128)}) %reduce-scatter.2.cloned.1.call-update) | async-done | bytes 9437200 | tf_op jit(solution)/shard_map/reduce_scatter | solution.py:148
  (122 shorter events, 289.0 us)
Async XLA Ops:
  7.2 370.6 %all-gather.3.cloned.1.call-start = ((), (), s32[]{:S(2)}) async-start(), calls=%async_computation.3 | async-start | bytes 80216064 | tf_op jit(solution)/shard_map/all_gather | solution.py:113
  7.9 1443.2 %all-reduce.22.cloned.1.call-start = ((), (), s32[]{:S(2)}) async-start(), calls=%async_computation.1 | async-start | bytes 7077888 | tf_op jit(solution)/shard_map/psum | solution.py:171
  200.7 20.4 copy-start.26
  200.7 20.5 copy-start.27
  200.7 20.5 copy-start.17
  200.7 20.5 copy-start.7
  200.7 22.0 copy-start.24
  219.3 52.9 %copy-start.3 = (bf16[128,6,6,256]{3,0,2,1:T(8,128)(2,1)}, bf16[128,6,6,256]{3,0,2,1:T(8,128)(2,1)S(1)}, u32[]{:S(2)}) copy-start(bf16[128,6,6,256]{3,0,2,1:T(8,128)(2,1)S(1)} %get-tuple-element.22) | copy-start | bytes 7077892
  219.3 158.5 %copy-start.18 = (f32[1,4096]{1,0:T(1,128)S(1)}, f32[1,4096]{1,0:T(1,128)}, u32[]{:S(2)}) copy-start(f32[1,4096]{1,0:T(1,128)} %param.15) | copy-start | bytes 49156
  219.3 52.9 %collective-permute-start = (bf16[128,6,6,256]{3,0,2,1:T(8,128)(2,1)S(1)}, bf16[128,6,6,256]{3,0,2,1:T(8,128)(2,1)}, u32[]{:S(2)}, u32[]{:S(2)}) collective-permute-start(bf16[128,6,6,256]{3,0,2,1:T(8,128)(2,1)S(1)} %get-tuple-element.22), channel_id=1, source_target_pairs={{0,16},{16,0},{1,17},{17,1},{2,18},{18,2},{3,19},{19,3},{4,20},{20... | collective-permute-start | bytes 7077896 | tf_op jit(solution)/shard_map/ppermute | solution.py:14
  221.2 184.9 %copy-start.19 = (f32[128]{0:T(128)}, f32[128]{0:T(128)S(1)}, u32[]{:S(2)}) copy-start(f32[128]{0:T(128)S(1)} %convert_divide_fusion) | copy-start | bytes 1540
  221.2 50.9 %copy-start.14 = (f32[1,1,4096]{2,1,0:T(1,128)}, f32[1,1,4096]{2,1,0:T(1,128)S(1)}, u32[]{:S(2)}) copy-start(f32[1,1,4096]{2,1,0:T(1,128)S(1)} %get-tuple-element.36) | copy-start | bytes 49156
  221.2 184.9 %copy-start.12 = (f32[1,1,4096]{2,1,0:T(1,128)}, f32[1,1,4096]{2,1,0:T(1,128)S(1)}, u32[]{:S(2)}) copy-start(f32[1,1,4096]{2,1,0:T(1,128)S(1)} %get-tuple-element.35) | copy-start | bytes 49156
  222.6 72.1 %collective-permute-start.2 = (bf16[128,4096]{1,0:T(8,128)(2,1)}, bf16[128,4096]{1,0:T(8,128)(2,1)}, u32[]{:S(2)}, u32[]{:S(2)}) collective-permute-start(bf16[128,4096]{1,0:T(8,128)(2,1)} %fusion.82), channel_id=1, source_target_pairs={{0,16},{16,0},{1,17},{17,1},{2,18},{18,2},{3,19},{19,3},{4,20},{20... | collective-permute-start | bytes 3145736 | tf_op jit(solution)/shard_map/ppermute | solution.py:14
  279.6 126.5 %copy-start.1 = (bf16[128,6,6,256]{0,3,2,1:T(8,128)(2,1)}, bf16[128,6,6,256]{0,3,2,1:T(8,128)(2,1)S(1)}, u32[]{:S(2)}) copy-start(bf16[128,6,6,256]{0,3,2,1:T(8,128)(2,1)S(1)} %copy.45) | copy-start | bytes 7077892
  406.1 31.2 %copy-start.5 = (bf16[128,4096]{1,0:T(8,128)(2,1)}, bf16[128,4096]{1,0:T(8,128)(2,1)S(1)}, u32[]{:S(2)}) copy-start(bf16[128,4096]{1,0:T(8,128)(2,1)S(1)} %get-tuple-element.17) | copy-start | bytes 3145732
  406.1 37.2 %copy-start.4 = (bf16[128,6,6,256]{3,0,2,1:T(8,128)(2,1)S(1)}, bf16[128,6,6,256]{3,0,2,1:T(8,128)(2,1)}, u32[]{:S(2)}) copy-start(bf16[128,6,6,256]{3,0,2,1:T(8,128)(2,1)} %copy-done.3) | copy-start | bytes 7077892
  443.3 57.8 %copy-start = (f32[128,6,6,256]{3,0,2,1:T(8,128)S(1)}, f32[128,6,6,256]{3,0,2,1:T(8,128)}, u32[]{:S(2)}) copy-start(f32[128,6,6,256]{3,0,2,1:T(8,128)} %copy.47) | copy-start | bytes 14155780
  448.6 52.6 %collective-permute-start.3 = (bf16[128,6,6,256]{3,0,2,1:T(8,128)(2,1)S(1)}, bf16[128,6,6,256]{3,0,2,1:T(8,128)(2,1)S(1)}, u32[]{:S(2)}, u32[]{:S(2)}) collective-permute-start(bf16[128,6,6,256]{3,0,2,1:T(8,128)(2,1)S(1)} %get-tuple-element.32), channel_id=1, source_target_pairs={{0,16},{16,0},{1,17},{17,1},{2,18},{18,2},{3,19},{19,3},{4,20},{20... | collective-permute-start | bytes 7077896 | tf_op jit(solution)/shard_map/ppermute | solution.py:14
  855.6 27.4 %slice-start = ((s8[16613376]{0:T(1024)(128)(4,1)}), s8[4194304]{0:T(1024)(128)(4,1)S(1)}, s32[]{:S(2)}) async-start(s8[16613376]{0:T(1024)(128)(4,1)} %bitcast.289), calls=%async_computation.4 | async-start | bytes 8388608
  855.6 27.4 %slice-start.1 = ((s8[16613376]{0:T(1024)(128)(4,1)}), s8[4194304]{0:T(1024)(128)(4,1)S(1)}, s32[]{:S(2)}) async-start(s8[16613376]{0:T(1024)(128)(4,1)} %bitcast.289), calls=%async_computation.5 | async-start | bytes 8388608
  913.3 27.5 %slice-start.4 = ((s8[16613376]{0:T(1024)(128)(4,1)}), s8[4194304]{0:T(1024)(128)(4,1)S(1)}, s32[]{:S(2)}) async-start(s8[16613376]{0:T(1024)(128)(4,1)} %bitcast.291), calls=%async_computation.8 | async-start | bytes 8388608
  913.3 27.5 %slice-start.5 = ((s8[16613376]{0:T(1024)(128)(4,1)}), s8[4194304]{0:T(1024)(128)(4,1)S(1)}, s32[]{:S(2)}) async-start(s8[16613376]{0:T(1024)(128)(4,1)} %bitcast.291), calls=%async_computation.9 | async-start | bytes 8388608
  957.8 1481.9 %reduce-scatter.2.cloned.1.call-start = ((), (), s32[]{:S(2)}) async-start(), calls=%async_computation.2 | async-start | bytes 160432128 | tf_op jit(solution)/shard_map/reduce_scatter | solution.py:148
  1010.1 24.0 copy-start.8
  1010.1 24.0 copy-start.13
  1010.1 24.0 copy-start.15
  1010.1 23.9 copy-start.20
  1010.1 27.2 %copy-start.16 = (f32[4096]{0:T(1024)S(1)}, f32[4096]{0:T(1024)}, u32[]{:S(2)}) copy-start(f32[4096]{0:T(1024)} %get-tuple-element.16) | copy-start | bytes 49156
  1010.1 27.1 %copy-start.23 = (f32[256]{0:T(256)S(1)}, f32[256]{0:T(256)}, u32[]{:S(2)}) copy-start(f32[256]{0:T(256)} %get-tuple-element.18) | copy-start | bytes 3076
  1010.1 84.6 %copy-start.10 = (bf16[1,3,3,384,256]{4,3,2,1,0:T(8,128)(2,1)S(1)}, bf16[1,3,3,384,256]{4,3,2,1,0:T(8,128)(2,1)}, u32[]{:S(2)}) copy-start(bf16[1,3,3,384,256]{4,3,2,1,0:T(8,128)(2,1)} %param.12) | copy-start | bytes 5308420
  1010.2 23.9 collective-permute-start.1
  (12 other events, 127.2 us)
Sparse Core Ops, SparseCore 0:
  9.6 368.1 all-gather.2
  957.9 105.1 all-reduce.21
  1067.8 1371.7 reduce-scatter.1
where the time goes:
time: 2460 us; the launch traced here: 2450 us
  waiting for transfers between devices  1210 us (49%)
  matrix products  623 us (25%)
  other arithmetic  281 us (11%)
  local copies, waits for them, and re-layouts  259 us (11%)
  blocking collectives  57.4 us (2%)
    reduce_scatter x1, waiting for transfers between devices, body(): lax.psum_scatter(lax.dot_general(columns, grad_pre_fc, (((0,), (0,)), (()...  989 us
    pad x9, local copies, waits for them, and re-layouts, smooth_pool(): activity[:, row_shift:row_shift + stride_span:2, col_shift:col_shift + st...  246 us
    dot_general x9, matrix products, conv_apply(): jnp.einsum('bhwc,cd->bhwd', window, kernel[row_shift, col_shift], preferr...  193 us
    ppermute x4, waiting for transfers between devices, partner(): return lax.ppermute(block, axis, route)  138 us
    dot_general x5, matrix products, conv_back(): jnp.einsum('bhwd,cd->bhwc', grad_pre, kernel[row_shift, col_shift], prefe...  123 us
    dot_general x9, matrix products, conv_back(): jnp.einsum('bhwc,bhwd->cd', window, grad_pre, preferred_element_type=jnp....  102 us
    pad x4, matrix products, conv_back(): jnp.pad(backed, ((0, 0), (row_shift, 2 - row_shift), (col_shift, 2 - col_...  93.3 us
    all_gather x1, waiting for transfers between devices, body(): lax.all_gather(weight_rows, 'crops', axis=0, tiled=True)  83.1 us
  transfers between devices with their start and end apart: 7, of which 6 were waited for; matrix products, arithmetic and copies ran while one was open for 26% of the time, Pallas kernels for 0%

commit v1 on v0

v1 whole, which is shorter than its diff:
```python
import functools

import jax
import jax.numpy as jnp
from jax import lax
from jax.experimental import pallas as pl
from jax.experimental.pallas import tpu as pltpu
from jax.sharding import PartitionSpec as P

CHUNKS = 4
BF16 = jnp.bfloat16
F32 = jnp.float32
CONV_DIMS = ("NHWC", "HWIO", "NHWC")
VMEM_LIMIT = 48 * 1024 * 1024


def swap_crops(block, mask):
    count = lax.axis_size("crops")
    return lax.ppermute(block, "crops", [(i, i ^ mask) for i in range(count)])


def swap_tower(block):
    return lax.ppermute(block, "tower", [(0, 1), (1, 0)])


def pick(stack, index):
    return lax.dynamic_index_in_dim(stack, index, 0, keepdims=False)


def pool_kernel(e_ref, pooled_ref, inv_ref):
    extent = e_ref.shape[0]
    width = e_ref.shape[3]
    out = (extent - 3) // 2 + 1

    def columns(row):
        cells = [e_ref[row, col].astype(F32) for col in range(extent)]
        return [cells[2 * j] + cells[2 * j + 1] + cells[2 * j + 2] for j in range(out)]

    top = columns(0)
    for i in range(out):
        middle = columns(2 * i + 1)
        bottom = columns(2 * i + 2)
        for j in range(out):
            total = top[j] + middle[j] + bottom[j]
            lanes = pl.ds((i * out + j) * width, width)
            pooled_ref[:, lanes] = jnp.log(total).astype(pooled_ref.dtype)
            inv_ref[:, lanes] = 2.0 / total
        top = bottom


def pool_forward(e):
    extent, _, slots, width = e.shape
    out = (extent - 3) // 2 + 1
    block = 16
    flat = out * out * width
    return pl.pallas_call(
        pool_kernel,
        grid=(slots // block,),
        in_specs=[pl.BlockSpec((extent, extent, block, width), lambda s: (0, 0, s, 0))],
        out_specs=[
            pl.BlockSpec((block, flat), lambda s: (s, 0)),
            pl.BlockSpec((block, flat), lambda s: (s, 0)),
        ],
        out_shape=[
            jax.ShapeDtypeStruct((slots, flat), BF16),
            jax.ShapeDtypeStruct((slots, flat), F32),
        ],
        compiler_params=pltpu.CompilerParams(vmem_limit_bytes=VMEM_LIMIT),
        cost_estimate=pl.CostEstimate(
            flops=4 * e.size, bytes_accessed=2 * e.size + 6 * slots * flat, transcendentals=0
        ),
        name="pool_forward",
    )(e)


def pool_back_kernel(slope_ref, grad_ref, back_ref, inv_ref, self_ref, g_ref, bias_ref):
    extent = slope_ref.shape[0]
    width = slope_ref.shape[3]
    out = (extent - 3) // 2 + 1
    coef = self_ref[0:1, :]

    @pl.when(pl.program_id(0) == 0)
    def _():
        bias_ref[...] = jnp.zeros_like(bias_ref)

    def window_row(i):
        row = []
        for j in range(out):
            lanes = pl.ds((i * out + j) * width, width)
            grad = coef * grad_ref[:, lanes].astype(F32) + back_ref[:, lanes].astype(F32)
            row.append(grad * inv_ref[:, lanes])
        return row

    sums = jnp.zeros((slope_ref.shape[2], width), F32)
    above = None
    current = window_row(0)
    for row in range(extent):
        if row % 2 == 0:
            if row == 0:
                rows = current
            elif row == extent - 1:
                rows = current
            else:
                above, current = current, window_row(row // 2)
                rows = [a + b for a, b in zip(above, current)]
        else:
            rows = current
        for col in range(extent):
            if col % 2 == 1:
                spread = rows[col // 2]
            elif col == 0:
                spread = rows[0]
            elif col == extent - 1:
                spread = rows[out - 1]
            else:
                spread = rows[col // 2 - 1] + rows[col // 2]
            grad = (slope_ref[row, col].astype(F32) * spread).astype(g_ref.dtype)
            g_ref[row, col] = grad
            sums = sums + grad.astype(F32)
    bias_ref[...] += sums


def pool_backward(slope, grad_mixed, back_pool, inv, self_pool):
    extent, _, slots, width = slope.shape
    block = 16
    flat = grad_mixed.shape[1]
    rows = pl.BlockSpec((block, flat), lambda s: (s, 0))
    grid_block = pl.BlockSpec((extent, extent, block, width), lambda s: (0, 0, s, 0))
    return pl.pallas_call(
        pool_back_kernel,
        grid=(slots // block,),
        in_specs=[grid_block, rows, rows, rows, pl.BlockSpec((1, width), lambda s: (0, 0))],
        out_specs=[grid_block, pl.BlockSpec((block, width), lambda s: (0, 0))],
        out_shape=[
            jax.ShapeDtypeStruct(slope.shape, BF16),
            jax.ShapeDtypeStruct((block, width), F32),
        ],
        compiler_params=pltpu.CompilerParams(vmem_limit_bytes=VMEM_LIMIT),
        cost_estimate=pl.CostEstimate(
            flops=4 * slope.size, bytes_accessed=4 * slope.size + 8 * slots * flat, transcendentals=0
        ),
        name="pool_backward",
    )(slope, grad_mixed, back_pool, inv, self_pool[None])


def gelu_parts(v):
    root = 0.7978845608028654
    cubic = 0.044715
    tanh = jnp.tanh(root * (v + cubic * (v * v * v)))
    half = 0.5 * (1.0 + tanh)
    slope = half + 0.5 * v * (1.0 - tanh * tanh) * (root * (1.0 + 3.0 * cubic * (v * v)))
    return v * half, slope


def conv_forward(inputs, kernel, bias):
    pre_conv = lax.conv_general_dilated(
        inputs, kernel, (1, 1), ((1, 1), (1, 1)), dimension_numbers=CONV_DIMS, preferred_element_type=F32
    )
    activity, slope = gelu_parts(pre_conv + bias)
    e = jnp.exp(activity)
    return e.astype(BF16), ((0.5 * e) * slope).astype(BF16)


def conv_grad_inputs(grad_pre, kernel):
    turned = jnp.flip(kernel, (0, 1)).swapaxes(2, 3)
    return lax.conv_general_dilated(
        grad_pre, turned, (1, 1), ((1, 1), (1, 1)), dimension_numbers=CONV_DIMS, preferred_element_type=F32
    ).astype(BF16)


def conv_grad_kernel(inputs, grad_pre):
    dims = lax.ConvDimensionNumbers(lhs_spec=(3, 0, 1, 2), rhs_spec=(3, 0, 1, 2), out_spec=(2, 3, 0, 1))
    return lax.conv_general_dilated(
        inputs, grad_pre, (1, 1), ((1, 1), (1, 1)), dimension_numbers=dims, preferred_element_type=F32
    )


def sum_small(vector):
    step = 1
    while step < lax.axis_size("crops"):
        vector = vector + swap_crops(vector, step)
        step *= 2
    return vector


def sum_kernel(rows, outer, mid, core):
    width = rows.shape[1]
    outer_count = lax.axis_size("crops") // 4
    for mask, side in ((1, core), (2, mid)):
        halves = rows.reshape(2, -1, width)
        got = swap_crops(pick(halves, 1 - side).astype(BF16), mask)
        rows = pick(halves, side) + got.astype(F32)
    parts = rows.reshape(outer_count, -1, width)
    total = pick(parts, outer)
    for k in range(1, outer_count):
        total = total + swap_crops(pick(parts, outer ^ k).astype(BF16), 4 * k).astype(F32)
    total = total.astype(BF16)
    stack = jnp.stack([total] + [swap_crops(total, 4 * k) for k in range(1, outer_count)])
    rows = jnp.concatenate([pick(stack, outer ^ k) for k in range(outer_count)])
    for mask, side in ((2, mid), (1, core)):
        got = swap_crops(rows, mask)
        rows = jnp.where(side == 0, jnp.concatenate([rows, got]), jnp.concatenate([got, rows]))
    return rows.astype(F32)


def body(
    features,
    conv_weight,
    conv_bias,
    fc_weight,
    fc_bias,
    stitch_pool,
    stitch_fc,
    cotangent,
    crop_counts,
    slot_image,
    slot_mask,
):
    is_first = lax.axis_index("tower") == 0
    place = lax.axis_index("crops")
    core, mid, outer = place & 1, (place >> 1) & 1, place >> 2
    outer_count = lax.axis_size("crops") // 4
    own_rows = fc_weight[0]
    other_rows = swap_crops(own_rows, 2)
    block = own_rows.shape[0]
    units = own_rows.shape[1]

    row_pool = stitch_pool[0]
    self_pool = jnp.where(is_first, row_pool[0], row_pool[1])
    cross_pool = jnp.where(is_first, row_pool[1], row_pool[0])
    row_fc = stitch_fc[0]
    self_fc = jnp.where(is_first, row_fc[0], row_fc[1])
    cross_fc = jnp.where(is_first, row_fc[1], row_fc[0])

    live_slots = slot_mask.astype(F32)
    image_ids = jnp.arange(crop_counts.shape[0], dtype=jnp.int32)
    matches = (slot_image[:, None] == image_ids[None, :]).astype(F32)
    per_slot = jnp.sum(matches * crop_counts.astype(F32)[None, :], axis=1)
    scaling = live_slots / per_slot
    sent_fc = (cross_fc * (cotangent[0].astype(F32) * scaling[:, None])).astype(BF16)
    back_fc = swap_tower(sent_fc)

    inputs = features[0]
    kernel = conv_weight[0]
    slots = inputs.shape[0] // CHUNKS
    width = kernel.shape[3]
    cells = outer_count * 4 * block // width
    self_flat = jnp.tile(self_pool, cells)
    cross_flat = jnp.tile(cross_pool, cells)

    def column_block(array, o, m, c):
        start = ((o * 2 + m) * 2 + c) * block
        return array[:, start : start + block]

    def spread_rows(mixed):
        keep, give = [], []
        for o in range(outer_count):
            parts = [[column_block(mixed, o, m, c) for c in range(2)] for m in range(2)]
            own = [jnp.where(mid == 0, parts[0][c], parts[1][c]) for c in range(2)]
            far = [jnp.where(mid == 0, parts[1][c], parts[0][c]) for c in range(2)]
            keep.append(
                jnp.concatenate([jnp.where(core == 0, own[0], own[1]), jnp.where(core == 0, far[0], far[1])], axis=1)
            )
            give.append(
                jnp.concatenate([jnp.where(core == 0, own[1], own[0]), jnp.where(core == 0, far[1], far[0])], axis=1)
            )
        got = swap_crops(jnp.stack(give), 1)
        blocks = jnp.stack([jnp.stack(keep), got], axis=1)
        arrived = [pick(blocks, outer)]
        for k in range(1, outer_count):
            arrived.append(swap_crops(pick(blocks, outer ^ k), 4 * k))
        return jnp.stack(arrived)

    def join_rows(columns):
        arrived = [columns[0]] + [swap_crops(columns[k], 4 * k) for k in range(1, outer_count)]
        stack = jnp.stack(arrived)
        own_core = stack[:, 0]
        far_core = swap_crops(stack[:, 1], 1)
        pieces = []
        for o in range(outer_count):
            here, there = pick(own_core, outer ^ o), pick(far_core, outer ^ o)
            by_core = [jnp.where(core == 0, here, there), jnp.where(core == 0, there, here)]
            for m in range(2):
                for c in range(2):
                    first, second = by_core[c][:, :block], by_core[c][:, block:]
                    pieces.append(jnp.where(mid == m, first, second))
        return jnp.concatenate(pieces, axis=1)

    outputs, grads_in = [], []
    hidden_self = hidden_cross = fc_bias_sum = 0.0
    pool_self = pool_cross = conv_bias_sum = 0.0
    kernel_sum = 0.0
    stage = []
    for n in range(CHUNKS):
        part = inputs[n * slots : (n + 1) * slots]
        e, slope = conv_forward(part, kernel, conv_bias[0])
        pooled, inv = pool_forward(jnp.transpose(e, (1, 2, 0, 3)))
        partner_pool = swap_tower(pooled)
        mixed = (self_flat * pooled.astype(F32) + cross_flat * partner_pool.astype(F32)).astype(BF16)
        columns = spread_rows(mixed)
        flat = columns.reshape(-1, 2 * block)
        partial = jnp.dot(flat[:, :block], own_rows, preferred_element_type=F32) + jnp.dot(
            flat[:, block:], other_rows, preferred_element_type=F32
        )
        partial = partial.astype(BF16).reshape(outer_count, 2, slots, units)
        chip = (partial[:, 0].astype(F32) + swap_crops(partial[:, 1], 1).astype(F32)).astype(BF16)
        pre_fc = chip[0].astype(F32)
        for k in range(1, outer_count):
            pre_fc = pre_fc + swap_crops(chip[k], 4 * k).astype(F32)
        pre_fc = pre_fc + fc_bias[0]
        hidden, slope_fc = gelu_parts(pre_fc)
        hidden = hidden.astype(BF16)
        rows = slice(n * slots, (n + 1) * slots)
        grad_out = cotangent[0][rows].astype(F32) * scaling[rows, None]
        grad_pre_fc = ((self_fc * grad_out + back_fc[rows].astype(F32)) * slope_fc).astype(BF16)
        fc_bias_sum = fc_bias_sum + jnp.sum(grad_pre_fc.astype(F32), axis=0)
        around = jnp.stack([grad_pre_fc] + [swap_crops(grad_pre_fc, 4 * k) for k in range(1, outer_count)])
        gathered = jnp.stack([around, swap_crops(around, 1)], axis=1).reshape(-1, units)
        turned = (((1,), (1,)), ((), ()))
        grad_columns = jnp.concatenate(
            [
                lax.dot_general(gathered, own_rows, turned, preferred_element_type=F32).astype(BF16),
                lax.dot_general(gathered, other_rows, turned, preferred_element_type=F32).astype(BF16),
            ],
            axis=1,
        )
        grad_mixed = join_rows(grad_columns.reshape(outer_count, 2, slots, 2 * block))
        wide = grad_mixed.astype(F32)
        pool_self = pool_self + jnp.sum(pooled.astype(F32) * wide, axis=0)
        pool_cross = pool_cross + jnp.sum(partner_pool.astype(F32) * wide, axis=0)
        back_pool = swap_tower((cross_flat * wide).astype(BF16))
        grad_pre, bias_rows = pool_backward(
            jnp.transpose(slope, (1, 2, 0, 3)), grad_mixed, back_pool, inv, self_pool
        )
        conv_bias_sum = conv_bias_sum + jnp.sum(bias_rows, axis=0)
        grad_pre = jnp.transpose(grad_pre, (2, 0, 1, 3))
        kernel_sum = kernel_sum + conv_grad_kernel(part, grad_pre)
        grads_in.append(conv_grad_inputs(grad_pre, kernel))
        partner_hidden = swap_tower(hidden)
        stitched = self_fc * hidden.astype(F32) + cross_fc * partner_hidden.astype(F32)
        outputs.append((stitched * live_slots[rows, None]).astype(BF16))
        hidden_self = hidden_self + jnp.sum(hidden.astype(F32) * grad_out, axis=0)
        hidden_cross = hidden_cross + jnp.sum(partner_hidden.astype(F32) * grad_out, axis=0)
        stage.append((flat, gathered))

    all_columns = jnp.concatenate([s[0] for s in stage])
    all_grads = jnp.concatenate([s[1] for s in stage])
    lead = (((0,), (0,)), ((), ()))
    far_term = lax.dot_general(all_columns[:, block:], all_grads, lead, preferred_element_type=F32).astype(BF16)
    grad_fc_weight = lax.dot_general(
        all_columns[:, :block], all_grads, lead, preferred_element_type=F32
    ) + swap_crops(far_term, 2).astype(F32)

    pool_self = jnp.sum(pool_self.reshape(cells, width), axis=0)
    pool_cross = jnp.sum(pool_cross.reshape(cells, width), axis=0)
    small = sum_small(
        jnp.concatenate([conv_bias_sum, pool_self, pool_cross, fc_bias_sum, hidden_self, hidden_cross])[None]
    )[0]
    cuts = [width, 2 * width, 3 * width, 3 * width + units, 3 * width + 2 * units]
    conv_bias_sum, pool_self, pool_cross, fc_bias_sum, hidden_self, hidden_cross = jnp.split(small, cuts)
    grad_row_pool = jnp.where(
        is_first, jnp.stack([pool_self, pool_cross]), jnp.stack([pool_cross, pool_self])
    )
    grad_row_fc = jnp.where(
        is_first, jnp.stack([hidden_self, hidden_cross]), jnp.stack([hidden_cross, hidden_self])
    )
    summed_kernel = sum_kernel(kernel_sum.reshape(-1, width), outer, mid, core).reshape(kernel.shape)
    return (
        jnp.concatenate(outputs)[None],
        jnp.concatenate(grads_in)[None],
        summed_kernel[None],
        conv_bias_sum[None],
        grad_fc_weight[None],
        fc_bias_sum[None],
        grad_row_pool[None],
        grad_row_fc[None],
    )


def solution(mesh):
    placed = (
        P("tower", "crops", None, None, None),
        P("tower", None, None, None, None),
        P("tower", None),
        P("tower", "crops", None),
        P("tower", None),
        P("tower", None, None),
        P("tower", None, None),
        P("tower", "crops", None),
        P("crops"),
        P("crops"),
        P("crops"),
    )
    return jax.shard_map(
        body,
        mesh=mesh,
        in_specs=placed,
        out_specs=(
            P("tower", "crops", None),
            P("tower", "crops", None, None, None),
            P("tower", None, None, None, None),
            P("tower", None),
            P("tower", "crops", None),
            P("tower", None),
            P("tower", None, None),
            P("tower", None, None),
        ),
        check_vma=False,
    )
```

time: 2460 us -> 794 us (0.32)
  waiting for transfers between devices: 1210 us -> 189 us
  matrix products: 623 us -> 250 us
  local copies, waits for them, and re-layouts: 259 us -> 54.9 us
  other arithmetic: 281 us -> 101 us
  starting transfers between devices: 4.55 us -> 160 us
  blocking collectives: 57.4 us -> 0 us
    reduce_scatter x1 -> x0, waiting for transfers between devices: 989 us -> none  [body(): lax.psum_scatter(lax.dot_general(columns, grad_pre_fc, (((0,), (0,)), (()...]
    dot_general x26 -> x18, matrix products: 530 us -> 52.9 us  [the longest x4 15.6 us: body(): lax.dot_general(gathered, own_rows, turned, preferred_element_type=F32)]
    pad x9 -> x0, local copies, waits for them, and re-layouts: 246 us -> none  [smooth_pool(): activity[:, row_shift:row_shift + stride_span:2, col_shift:col_shift + st...]
    conv_general_dilated x0 -> x12, matrix products: none -> 198 us  [the longest x4 83 us: conv_forward(): lax.conv_general_dilated(inputs, kernel, (1, 1), ((1, 1), (1, 1)), dimens...]
    ppermute x4 -> x93, starting transfers between devices: 4.43 us -> 160 us  [the longest x80 149 us: swap_crops(): return lax.ppermute(block, 'crops', [(i, i ^ mask) for i in range(count)])]
    pad x4 -> x0, matrix products: 93.3 us -> none  [conv_back(): jnp.pad(backed, ((0, 0), (row_shift, 2 - row_shift), (col_shift, 2 - col_...]
    all_gather x1 -> x0, waiting for transfers between devices: 83.1 us -> none  [body(): lax.all_gather(weight_rows, 'crops', axis=0, tiled=True)]
    add x1 -> x8, other arithmetic: 72.4 us -> 2.55 us  [the longest x1 1.44 us: body(): pool_self = pool_self + jnp.sum(pooled.astype(F32) * wide, axis=0)]
  transfers between devices with their start and end apart: 7 -> 93, of which waited for: 6 -> 24; matrix products, arithmetic and copies ran while one was open for 26% -> 48% of each run, Pallas kernels for 0% -> 3%
where the time goes in v1:
time: 794 us; the launch traced here: 783 us
  matrix products  250 us (31%)
  waiting for transfers between devices  189 us (24%)
  starting transfers between devices  160 us (20%)
  other arithmetic  101 us (13%)
  local copies, waits for them, and re-layouts  54.9 us (7%)
  Pallas kernels  24.3 us (3%)
    ppermute x80, waiting for transfers between devices, swap_crops(): return lax.ppermute(block, 'crops', [(i, i ^ mask) for i in range(count)])  153 us
    ppermute x80, starting transfers between devices, swap_crops(): return lax.ppermute(block, 'crops', [(i, i ^ mask) for i in range(count)])  149 us
    conv_general_dilated x4, matrix products, conv_forward(): lax.conv_general_dilated(inputs, kernel, (1, 1), ((1, 1), (1, 1)), dimens...  83 us
    conv_general_dilated x4, matrix products, conv_grad_inputs(): lax.conv_general_dilated(grad_pre, turned, (1, 1), ((1, 1), (1, 1)), dime...  60.7 us
    conv_general_dilated x4, matrix products, conv_grad_kernel(): lax.conv_general_dilated(inputs, grad_pre, (1, 1), ((1, 1), (1, 1)), dime...  53.8 us
    ppermute x13, waiting for transfers between devices, swap_tower(): return lax.ppermute(block, 'tower', [(0, 1), (1, 0)])  36 us
    select_n x32, other arithmetic, join_rows(): pieces.append(jnp.where(mid == m, first, second))  19.2 us
    slice x12, local copies, waits for them, and re-layouts, join_rows(): columns[k]  18.4 us
  transfers between devices with their start and end apart: 93, of which 24 were waited for; matrix products, arithmetic and copies ran while one was open for 48% of the time, Pallas kernels for 3%

profile of v1, /device:TPU:1, one launch (start us, length us, event | category | flops | bytes accessed | tf_op | source)
XLA Modules:
  0.0 783.4 jit_solution(4212870742545361708)
XLA Ops:
  9.6 17.2 %fusion.58 = f32[13,13,32,256]{3,2,1,0:T(8,128)S(1)} fusion(bf16[1,128,13,13,384]{4,1,3,2,0:T(8,128)(2,1)} %param.11, bf16[1,3,3,384,256]{4,3,2,1,0:T(8,128)(2,1)S(1)} %copy-done), kind=kOutput, calls=%fused_computation.82 | convolution fusion | flops 8613003264 | bytes 11460608 | tf_op jit(solution)/shard_map/conv_general_dilated | solution.py:156
  26.8 12.7 %fusion.50 = f32[13,13,32,256]{3,2,1,0:T(8,128)} fusion(bf16[1,128,13,13,384]{4,1,3,2,0:T(8,128)(2,1)S(1)} %bitcast.696, bf16[1,3,3,384,256]{4,3,2,1,0:T(8,128)(2,1)S(1)} %copy-done), kind=kOutput, calls=%fused_computation.74 | convolution fusion | flops 8613003264 | bytes 11460608 | tf_op jit(solution)/shard_map/conv_general_dilated | solution.py:156
  39.6 13.4 %fusion.54 = f32[13,13,32,256]{3,2,1,0:T(8,128)} fusion(bf16[1,128,13,13,384]{4,1,3,2,0:T(8,128)(2,1)S(1)} %bitcast.696, bf16[1,3,3,384,256]{4,3,2,1,0:T(8,128)(2,1)S(1)} %copy-done), kind=kOutput, calls=%fused_computation.78 | convolution fusion | flops 8613003264 | bytes 11460608 | tf_op jit(solution)/shard_map/conv_general_dilated | solution.py:156
  52.9 39.8 %fusion.9 = (bf16[13,13,32,256]{3,2,1,0:T(8,128)(2,1)}, bf16[13,13,32,256]{3,2,1,0:T(8,128)(2,1)S(1)}, bf16[13,13,32,256]{3,2,1,0:T(8,128)(2,1)S(1)}, bf16[13,13...) fusion(f32[256]{0:T(256)S(1)} %bitcast.697, ...), kind=kOutput, calls=%fused_computation.21 | convolution fusion | flops 8734834688 | bytes 44688384 | tf_op jit(solution)/shard_map/conv_general_dilated | solution.py:156
  98.6 9.6 %pool_forward.7 = (bf16[32,9216]{1,0:T(8,128)(2,1)S(1)}, f32[32,9216]{1,0:T(8,128)S(1)}) custom-call(bf16[13,13,32,256]{3,2,1,0:T(8,128)(2,1)S(1)} %get-tuple-element.345.e_ref), custom_call_target="tpu_custom_call" | custom-call | flops 5537792 | bytes 4538368 | tf_op jit(solution)/shard_map/pool_forward/pallas_call | solution.py:56
  115.9 5.4 collective-permute-done.11
  121.3 12.6 %collective-permute-done.21 = bf16[32,9216]{1,0:T(8,128)(2,1)} collective-permute-done((bf16[32,9216]{1,0:T(8,128)(2,1)S(1)}, bf16[32,9216]{1,0:T(8,128)(2,1)}, u32[]{:S(2)}, u32[]{:S(2)}) %collective-permute-start.21) | collective-permute-done | bytes 589856 | tf_op jit(solution)/shard_map/ppermute | solution.py:23
  133.9 12.6 %collective-permute-done.31 = bf16[32,9216]{1,0:T(8,128)(2,1)} collective-permute-done((bf16[32,9216]{1,0:T(8,128)(2,1)S(1)}, bf16[32,9216]{1,0:T(8,128)(2,1)}, u32[]{:S(2)}, u32[]{:S(2)}) %collective-permute-start.31) | collective-permute-done | bytes 589856 | tf_op jit(solution)/shard_map/ppermute | solution.py:23
  172.6 9.2 %collective-permute-start.13 = (bf16[2,32,1152]{2,1,0:T(8,128)(2,1)S(1)}, bf16[2,32,1152]{2,1,0:T(8,128)(2,1)S(1)}, u32[]{:S(2)}, u32[]{:S(2)}) collective-permute-start(bf16[2,32,1152]{2,1,0:T(8,128)(2,1)S(1)} %get-tuple-element.198), channel_id=1, source_target_pairs={{0,4},{1,5},{2,6},{3,7},{4,0},{5,1},{6,2},{7,3},{8,12},{9,13},{10,... | collective-permute-start | bytes 442376 | tf_op jit(solution)/shard_map/ppermute | solution.py:19
  189.3 5.9 collective-permute-done.14
  197.1 8.4 %collective-permute-done.3 = bf16[2,32,1152]{2,1,0:T(8,128)(2,1)S(1)} collective-permute-done((bf16[2,32,1152]{2,1,0:T(8,128)(2,1)S(1)}, bf16[2,32,1152]{2,1,0:T(8,128)(2,1)S(1)}, u32[]{:S(2)}, u32[]{:S(2)}) %collective-permute-start.3) | collective-permute-done | bytes 147488 | tf_op jit(solution)/shard_map/ppermute | solution.py:19
  245.5 10.2 %collective-permute-done.8 = bf16[32,4096]{1,0:T(8,128)(2,1)S(1)} collective-permute-done((bf16[32,4096]{1,0:T(8,128)(2,1)S(1)}, bf16[32,4096]{1,0:T(8,128)(2,1)S(1)}, u32[]{:S(2)}, u32[]{:S(2)}) %collective-permute-start.8) | collective-permute-done | bytes 262176 | tf_op jit(solution)/shard_map/ppermute | solution.py:19
  262.4 10.5 %collective-permute-start.37 = (bf16[32,4096]{1,0:T(8,128)(2,1)S(1)}, bf16[32,4096]{1,0:T(8,128)(2,1)S(1)}, u32[]{:S(2)}, u32[]{:S(2)}) collective-permute-start(bf16[32,4096]{1,0:T(8,128)(2,1)S(1)} %get-tuple-element.111), channel_id=1, source_target_pairs={{0,4},{1,5},{2,6},{3,7},{4,0},{5,1},{6,2},{7,3},{8,12},{9,13},{10,... | collective-permute-start | bytes 786440 | tf_op jit(solution)/shard_map/ppermute | solution.py:19
  272.9 16.6 %collective-permute-done.18 = bf16[32,4096]{1,0:T(8,128)(2,1)S(1)} collective-permute-done((bf16[32,4096]{1,0:T(8,128)(2,1)S(1)}, bf16[32,4096]{1,0:T(8,128)(2,1)S(1)}, u32[]{:S(2)}, u32[]{:S(2)}) %collective-permute-start.18) | collective-permute-done | bytes 262176 | tf_op jit(solution)/shard_map/ppermute | solution.py:19
  295.7 21.9 %collective-permute-done.28 = bf16[32,4096]{1,0:T(8,128)(2,1)S(1)} collective-permute-done((bf16[32,4096]{1,0:T(8,128)(2,1)S(1)}, bf16[32,4096]{1,0:T(8,128)(2,1)S(1)}, u32[]{:S(2)}, u32[]{:S(2)}) %collective-permute-start.28) | collective-permute-done | bytes 262176 | tf_op jit(solution)/shard_map/ppermute | solution.py:19
  320.0 14.8 %collective-permute-start.51 = (bf16[32,4096]{1,0:T(8,128)(2,1)S(1)}, bf16[32,4096]{1,0:T(8,128)(2,1)S(1)}, u32[]{:S(2)}, u32[]{:S(2)}) collective-permute-start(bf16[32,4096]{1,0:T(8,128)(2,1)S(1)} %get-tuple-element.85), channel_id=1, source_target_pairs={{0,4},{1,5},{2,6},{3,7},{4,0},{5,1},{6,2},{7,3},{8,12},{9,13},{10,... | collective-permute-start | bytes 786440 | tf_op jit(solution)/shard_map/ppermute | solution.py:19
  345.2 17.4 %collective-permute-done.52 = bf16[32,4096]{1,0:T(8,128)(2,1)S(1)} collective-permute-done((bf16[32,4096]{1,0:T(8,128)(2,1)S(1)}, bf16[32,4096]{1,0:T(8,128)(2,1)S(1)}, u32[]{:S(2)}, u32[]{:S(2)}) %collective-permute-start.52) | collective-permute-done | bytes 262176 | tf_op jit(solution)/shard_map/ppermute | solution.py:19
  375.3 32.2 %collective-permute-done.70 = bf16[32,4096]{1,0:T(8,128)(2,1)S(1)} collective-permute-done((bf16[32,4096]{1,0:T(8,128)(2,1)S(1)}, bf16[32,4096]{1,0:T(8,128)(2,1)S(1)}, u32[]{:S(2)}, u32[]{:S(2)}) %collective-permute-start.70) | collective-permute-done | bytes 262176 | tf_op jit(solution)/shard_map/ppermute | solution.py:19
  419.1 5.6 collective-permute-start.63
  495.1 7.5 convolution_convert_fusion
  526.7 5.5 collective-permute-done.74
  589.8 13.2 %fusion.56 = f32[3,3,384,256]{3,2,1,0:T(8,128)} fusion(bf16[13,13,32,256]{3,2,1,0:T(8,128)(2,1)S(1)} %get-tuple-element.31, bf16[1,128,13,13,384]{4,1,3,2,0:T(8,128)(2,1)} %param.11), kind=kOutput, calls=%fused_computation.80 | convolution fusion | flops 8613003264 | bytes 10461184 | tf_op jit(solution)/shard_map/conv_general_dilated | solution.py:173
  605.9 14.1 %fusion.60 = f32[3,3,384,256]{3,2,1,0:T(8,128)} fusion(bf16[13,13,32,256]{3,2,1,0:T(8,128)(2,1)S(1)} %get-tuple-element.29, bf16[1,128,13,13,384]{4,1,3,2,0:T(8,128)(2,1)} %param.11), kind=kOutput, calls=%fused_computation.84 | convolution fusion | flops 8613003264 | bytes 10461184 | tf_op jit(solution)/shard_map/conv_general_dilated | solution.py:173
  620.1 15.3 %convolution_convert_fusion.3 = bf16[32,13,13,384]{3,0,2,1:T(8,128)(2,1)} fusion(bf16[13,13,32,256]{3,2,1,0:T(8,128)(2,1)S(1)} %get-tuple-element.31, bf16[1,3,3,384,256]{4,3,2,1,0:T(8,128)(2,1)S(1)} %copy-done), kind=kOutput, calls=%fused_computation.99 | convolution fusion | flops 8615079936 | bytes 8691712 | tf_op jit(solution)/shard_map/conv_general_dilated | solution.py:166
  649.6 13.8 %fusion.52 = f32[3,3,384,256]{3,2,1,0:T(8,128)S(1)} fusion(bf16[13,13,32,256]{3,2,1,0:T(8,128)(2,1)} %copy-done.15, bf16[1,128,13,13,384]{4,1,3,2,0:T(8,128)(2,1)} %param.11), kind=kOutput, calls=%fused_computation.76 | convolution fusion | flops 8613003264 | bytes 10461184 | tf_op jit(solution)/shard_map/conv_general_dilated | solution.py:173
  663.5 12.6 %add_add_fusion = f32[3,3,384,256]{3,2,1,0:T(8,128)S(1)} fusion(f32[3,3,384,256]{3,2,1,0:T(8,128)S(1)} %fusion.52, f32[3,3,384,256]{3,2,1,0:T(8,128)S(1)} %copy-done.64, f32[3,3,384,256]{3,2,1,0:T(8,128)S(1)} %copy-done.63, bf16[13,13,32,256]{3,2,1,0:T(8,128)(2,1)S(1)} %copy-done.18, bf16[1,128,13,13,384]{4,1,3,2,0:T(8,128)(2,1)} %param.11), kind=kOutput, calls=%fused_computation.96 | convolution fusion | flops 8615657472 | bytes 21078016 | tf_op jit(solution)/shard_map/conv_general_dilated | solution.py:173
  676.3 15.1 %convolution_convert_fusion.4 = bf16[32,13,13,384]{3,0,2,1:T(8,128)(2,1)} fusion(bf16[13,13,32,256]{3,2,1,0:T(8,128)(2,1)S(1)} %copy-done.20, bf16[1,3,3,384,256]{4,3,2,1,0:T(8,128)(2,1)S(1)} %copy-done), kind=kOutput, calls=%fused_computation.100 | convolution fusion | flops 8615079936 | bytes 8691712 | tf_op jit(solution)/shard_map/conv_general_dilated | solution.py:166
  693.5 9.9 %collective-permute-done.79 = bf16[864,256]{1,0:T(8,128)(2,1)S(1)} collective-permute-done((bf16[864,256]{1,0:T(8,128)(2,1)S(1)}, bf16[864,256]{1,0:T(8,128)(2,1)S(1)}, u32[]{:S(2)}, u32[]{:S(2)}) %collective-permute-start.79) | collective-permute-done | bytes 442400 | tf_op jit(solution)/shard_map/ppermute | solution.py:19
  707.2 15.1 %convolution_convert_fusion.1 = bf16[32,13,13,384]{3,0,2,1:T(8,128)(2,1)} fusion(bf16[13,13,32,256]{3,2,1,0:T(8,128)(2,1)S(1)} %copy-done.18, bf16[1,3,3,384,256]{4,3,2,1,0:T(8,128)(2,1)S(1)} %copy-done), kind=kOutput, calls=%fused_computation.97 | convolution fusion | flops 8615079936 | bytes 8691712 | tf_op jit(solution)/shard_map/conv_general_dilated | solution.py:166
  727.6 15.2 %convolution_convert_fusion.2 = bf16[32,13,13,384]{3,0,2,1:T(8,128)(2,1)} fusion(bf16[13,13,32,256]{3,2,1,0:T(8,128)(2,1)S(1)} %copy-done.16, bf16[1,3,3,384,256]{4,3,2,1,0:T(8,128)(2,1)S(1)} %copy-done), kind=kOutput, calls=%fused_computation.98 | convolution fusion | flops 8615079936 | bytes 8691712 | tf_op jit(solution)/shard_map/conv_general_dilated | solution.py:166
  745.5 16.5 %maximum_bitcast_fusion = bf16[1,128,13,13,384]{4,1,3,2,0:T(8,128)(2,1)} fusion(bf16[32,13,13,384]{3,0,2,1:T(8,128)(2,1)} %convolution_convert_fusion.1, bf16[32,13,13,384]{3,0,2,1:T(8,128)(2,1)} %convolution_convert_fusion.2, bf16[32,13,13,384]{3,0,2,1:T(8,128)(2,1)S(1)} %copy-done.23, bf16[32,13,13,384]{3,0,2,1:T(8,128)(2,1)} %convolution_convert_fusion.4), kind=kLoop, calls=%fused_computation | loop fusion | flops 66453504 | bytes 33226752 | tf_op jit(solution)/shard_map/broadcast_in_dim | solution.py:370
  773.8 9.2 %add_bitcast_fusion = f32[1,576,4096]{2,1,0:T(8,128)} fusion(bf16[576,4096]{1,0:T(8,128)(2,1)} %collective-permute-done.92, bf16[256,4096]{1,0:T(8,128)(2,1)S(1)} %bitcast.623, bf16[256,4096]{1,0:T(8,128)(2,1)S(1)} %bitcast.619, bf16[256,4096]{1,0:T(8,128)(2,1)S(1)} %bitcast.615, bf16[256,4096]{1,0:T(8,128)(2,1)S(1)} %bitcast.611, ...), kind=kOutput, calls=%fused_computation.1 | convolution fusion | flops 4870111232 | bytes 23855104 | tf_op jit(solution)/shard_map/dot_general | solution.py:350
  (579 shorter events, 341.0 us)
Async XLA Ops:
  7.6 228.7 %collective-permute-start.41 = (bf16[128,4096]{1,0:T(8,128)(2,1)}, bf16[128,4096]{1,0:T(8,128)(2,1)}, u32[]{:S(2)}, u32[]{:S(2)}) collective-permute-start(bf16[128,4096]{1,0:T(8,128)(2,1)} %fusion.73), channel_id=1, source_target_pairs={{0,16},{16,0},{1,17},{17,1},{2,18},{18,2},{3,19},{19,3},{4,20},{20... | collective-permute-start | bytes 3145736 | tf_op jit(solution)/shard_map/ppermute | solution.py:23
  98.5 35.4 %collective-permute-start.21 = (bf16[32,9216]{1,0:T(8,128)(2,1)S(1)}, bf16[32,9216]{1,0:T(8,128)(2,1)}, u32[]{:S(2)}, u32[]{:S(2)}) collective-permute-start(bf16[32,9216]{1,0:T(8,128)(2,1)S(1)} %get-tuple-element.26), channel_id=1, source_target_pairs={{0,16},{16,0},{1,17},{17,1},{2,18},{18,2},{3,19},{19,3},{4,20},{20... | collective-permute-start | bytes 1769480 | tf_op jit(solution)/shard_map/ppermute | solution.py:23
  109.2 37.4 %collective-permute-start.31 = (bf16[32,9216]{1,0:T(8,128)(2,1)S(1)}, bf16[32,9216]{1,0:T(8,128)(2,1)}, u32[]{:S(2)}, u32[]{:S(2)}) collective-permute-start(bf16[32,9216]{1,0:T(8,128)(2,1)S(1)} %get-tuple-element.27), channel_id=1, source_target_pairs={{0,16},{16,0},{1,17},{17,1},{2,18},{18,2},{3,19},{19,3},{4,20},{20... | collective-permute-start | bytes 1769480 | tf_op jit(solution)/shard_map/ppermute | solution.py:23
  114.9 101.6 %collective-permute-start.5 = (bf16[576,4096]{1,0:T(8,128)(2,1)}, bf16[576,4096]{1,0:T(8,128)(2,1)S(1)}, u32[]{:S(2)}, u32[]{:S(2)}) collective-permute-start(bf16[576,4096]{1,0:T(8,128)(2,1)} %bitcast.580), channel_id=1, source_target_pairs={{0,2},{1,3},{2,0},{3,1},{4,6},{5,7},{6,4},{7,5},{8,10},{9,11},{10,... | collective-permute-start | bytes 14155784 | tf_op jit(solution)/shard_map/ppermute | solution.py:19
  238.6 50.9 %collective-permute-start.18 = (bf16[32,4096]{1,0:T(8,128)(2,1)S(1)}, bf16[32,4096]{1,0:T(8,128)(2,1)S(1)}, u32[]{:S(2)}, u32[]{:S(2)}) collective-permute-start(bf16[32,4096]{1,0:T(8,128)(2,1)S(1)} %get-tuple-element.107), channel_id=1, source_target_pairs={{0,8},{1,9},{2,10},{3,11},{4,12},{5,13},{6,14},{7,15},{8,0},{9,1},... | collective-permute-start | bytes 786440 | tf_op jit(solution)/shard_map/ppermute | solution.py:19
  245.5 46.2 %collective-permute-start.27 = (bf16[32,4096]{1,0:T(8,128)(2,1)S(1)}, bf16[32,4096]{1,0:T(8,128)(2,1)S(1)}, u32[]{:S(2)}, u32[]{:S(2)}) collective-permute-start(bf16[32,4096]{1,0:T(8,128)(2,1)S(1)} %get-tuple-element.108), channel_id=1, source_target_pairs={{0,4},{1,5},{2,6},{3,7},{4,0},{5,1},{6,2},{7,3},{8,12},{9,13},{10,... | collective-permute-start | bytes 786440 | tf_op jit(solution)/shard_map/ppermute | solution.py:19
  255.8 38.8 %collective-permute-start.29 = (bf16[32,4096]{1,0:T(8,128)(2,1)S(1)}, bf16[32,4096]{1,0:T(8,128)(2,1)S(1)}, u32[]{:S(2)}, u32[]{:S(2)}) collective-permute-start(bf16[32,4096]{1,0:T(8,128)(2,1)S(1)} %get-tuple-element.109), channel_id=1, source_target_pairs={{0,12},{1,13},{2,14},{3,15},{4,8},{5,9},{6,10},{7,11},{8,4},{9,5},... | collective-permute-start | bytes 786440 | tf_op jit(solution)/shard_map/ppermute | solution.py:19
  258.2 59.4 %collective-permute-start.28 = (bf16[32,4096]{1,0:T(8,128)(2,1)S(1)}, bf16[32,4096]{1,0:T(8,128)(2,1)S(1)}, u32[]{:S(2)}, u32[]{:S(2)}) collective-permute-start(bf16[32,4096]{1,0:T(8,128)(2,1)S(1)} %get-tuple-element.110), channel_id=1, source_target_pairs={{0,8},{1,9},{2,10},{3,11},{4,12},{5,13},{6,14},{7,15},{8,0},{9,1},... | collective-permute-start | bytes 786440 | tf_op jit(solution)/shard_map/ppermute | solution.py:19
  262.4 55.2 %collective-permute-start.37 = (bf16[32,4096]{1,0:T(8,128)(2,1)S(1)}, bf16[32,4096]{1,0:T(8,128)(2,1)S(1)}, u32[]{:S(2)}, u32[]{:S(2)}) collective-permute-start(bf16[32,4096]{1,0:T(8,128)(2,1)S(1)} %get-tuple-element.111), channel_id=1, source_target_pairs={{0,4},{1,5},{2,6},{3,7},{4,0},{5,1},{6,2},{7,3},{8,12},{9,13},{10,... | collective-permute-start | bytes 786440 | tf_op jit(solution)/shard_map/ppermute | solution.py:19
  291.7 48.4 %collective-permute-start.38 = (bf16[32,4096]{1,0:T(8,128)(2,1)S(1)}, bf16[32,4096]{1,0:T(8,128)(2,1)S(1)}, u32[]{:S(2)}, u32[]{:S(2)}) collective-permute-start(bf16[32,4096]{1,0:T(8,128)(2,1)S(1)} %get-tuple-element.113), channel_id=1, source_target_pairs={{0,8},{1,9},{2,10},{3,11},{4,12},{5,13},{6,14},{7,15},{8,0},{9,1},... | collective-permute-start | bytes 786440 | tf_op jit(solution)/shard_map/ppermute | solution.py:19
  294.6 77.0 %collective-permute-start.44 = (bf16[32,4096]{1,0:T(8,128)(2,1)S(1)}, bf16[32,4096]{1,0:T(8,128)(2,1)S(1)}, u32[]{:S(2)}, u32[]{:S(2)}) collective-permute-start(bf16[32,4096]{1,0:T(8,128)(2,1)S(1)} %get-tuple-element.63), channel_id=1, source_target_pairs={{0,12},{1,13},{2,14},{3,15},{4,8},{5,9},{6,10},{7,11},{8,4},{9,5},... | collective-permute-start | bytes 786440 | tf_op jit(solution)/shard_map/ppermute | solution.py:19
  317.6 54.0 %collective-permute-start.43 = (bf16[32,4096]{1,0:T(8,128)(2,1)S(1)}, bf16[32,4096]{1,0:T(8,128)(2,1)S(1)}, u32[]{:S(2)}, u32[]{:S(2)}) collective-permute-start(bf16[32,4096]{1,0:T(8,128)(2,1)S(1)} %get-tuple-element.63), channel_id=1, source_target_pairs={{0,8},{1,9},{2,10},{3,11},{4,12},{5,13},{6,14},{7,15},{8,0},{9,1},... | collective-permute-start | bytes 786440 | tf_op jit(solution)/shard_map/ppermute | solution.py:19
  317.6 45.0 %collective-permute-start.52 = (bf16[32,4096]{1,0:T(8,128)(2,1)S(1)}, bf16[32,4096]{1,0:T(8,128)(2,1)S(1)}, u32[]{:S(2)}, u32[]{:S(2)}) collective-permute-start(bf16[32,4096]{1,0:T(8,128)(2,1)S(1)} %get-tuple-element.85), channel_id=1, source_target_pairs={{0,8},{1,9},{2,10},{3,11},{4,12},{5,13},{6,14},{7,15},{8,0},{9,1},... | collective-permute-start | bytes 786440 | tf_op jit(solution)/shard_map/ppermute | solution.py:19
  320.0 42.6 %collective-permute-start.51 = (bf16[32,4096]{1,0:T(8,128)(2,1)S(1)}, bf16[32,4096]{1,0:T(8,128)(2,1)S(1)}, u32[]{:S(2)}, u32[]{:S(2)}) collective-permute-start(bf16[32,4096]{1,0:T(8,128)(2,1)S(1)} %get-tuple-element.85), channel_id=1, source_target_pairs={{0,4},{1,5},{2,6},{3,7},{4,0},{5,1},{6,2},{7,3},{8,12},{9,13},{10,... | collective-permute-start | bytes 786440 | tf_op jit(solution)/shard_map/ppermute | solution.py:19
  362.6 47.5 %collective-permute-start.62 = (bf16[32,4096]{1,0:T(8,128)(2,1)S(1)}, bf16[32,4096]{1,0:T(8,128)(2,1)S(1)}, u32[]{:S(2)}, u32[]{:S(2)}) collective-permute-start(bf16[32,4096]{1,0:T(8,128)(2,1)S(1)} %get-tuple-element.65), channel_id=1, source_target_pairs={{0,12},{1,13},{2,14},{3,15},{4,8},{5,9},{6,10},{7,11},{8,4},{9,5},... | collective-permute-start | bytes 786440 | tf_op jit(solution)/shard_map/ppermute | solution.py:19
  364.8 45.4 %collective-permute-start.61 = (bf16[32,4096]{1,0:T(8,128)(2,1)S(1)}, bf16[32,4096]{1,0:T(8,128)(2,1)S(1)}, u32[]{:S(2)}, u32[]{:S(2)}) collective-permute-start(bf16[32,4096]{1,0:T(8,128)(2,1)S(1)} %get-tuple-element.65), channel_id=1, source_target_pairs={{0,8},{1,9},{2,10},{3,11},{4,12},{5,13},{6,14},{7,15},{8,0},{9,1},... | collective-permute-start | bytes 786440 | tf_op jit(solution)/shard_map/ppermute | solution.py:19
  371.6 35.9 %collective-permute-start.70 = (bf16[32,4096]{1,0:T(8,128)(2,1)S(1)}, bf16[32,4096]{1,0:T(8,128)(2,1)S(1)}, u32[]{:S(2)}, u32[]{:S(2)}) collective-permute-start(bf16[32,4096]{1,0:T(8,128)(2,1)S(1)} %get-tuple-element.87), channel_id=1, source_target_pairs={{0,8},{1,9},{2,10},{3,11},{4,12},{5,13},{6,14},{7,15},{8,0},{9,1},... | collective-permute-start | bytes 786440 | tf_op jit(solution)/shard_map/ppermute | solution.py:19
  371.6 35.9 %collective-permute-start.69 = (bf16[32,4096]{1,0:T(8,128)(2,1)S(1)}, bf16[32,4096]{1,0:T(8,128)(2,1)S(1)}, u32[]{:S(2)}, u32[]{:S(2)}) collective-permute-start(bf16[32,4096]{1,0:T(8,128)(2,1)S(1)} %get-tuple-element.87), channel_id=1, source_target_pairs={{0,4},{1,5},{2,6},{3,7},{4,0},{5,1},{6,2},{7,3},{8,12},{9,13},{10,... | collective-permute-start | bytes 786440 | tf_op jit(solution)/shard_map/ppermute | solution.py:19
  372.8 34.7 %collective-permute-start.71 = (bf16[32,4096]{1,0:T(8,128)(2,1)S(1)}, bf16[32,4096]{1,0:T(8,128)(2,1)S(1)}, u32[]{:S(2)}, u32[]{:S(2)}) collective-permute-start(bf16[32,4096]{1,0:T(8,128)(2,1)S(1)} %get-tuple-element.87), channel_id=1, source_target_pairs={{0,12},{1,13},{2,14},{3,15},{4,8},{5,9},{6,10},{7,11},{8,4},{9,5},... | collective-permute-start | bytes 786440 | tf_op jit(solution)/shard_map/ppermute | solution.py:19
  417.8 33.9 %collective-permute-start.54 = (bf16[4,32,4096]{2,1,0:T(8,128)(2,1)}, bf16[4,32,4096]{2,1,0:T(8,128)(2,1)}, u32[]{:S(2)}, u32[]{:S(2)}) collective-permute-start(bf16[4,32,4096]{2,1,0:T(8,128)(2,1)} %get-tuple-element.97), channel_id=1, source_target_pairs={{0,1},{1,0},{2,3},{3,2},{4,5},{5,4},{6,7},{7,6},{8,9},{9,8},{10,11... | collective-permute-start | bytes 3145736 | tf_op jit(solution)/shard_map/ppermute | solution.py:19
  419.1 48.9 %collective-permute-start.63 = (bf16[4,32,4096]{2,1,0:T(8,128)(2,1)}, bf16[4,32,4096]{2,1,0:T(8,128)(2,1)}, u32[]{:S(2)}, u32[]{:S(2)}) collective-permute-start(bf16[4,32,4096]{2,1,0:T(8,128)(2,1)} %get-tuple-element.99), channel_id=1, source_target_pairs={{0,1},{1,0},{2,3},{3,2},{4,5},{5,4},{6,7},{7,6},{8,9},{9,8},{10,11... | collective-permute-start | bytes 3145736 | tf_op jit(solution)/shard_map/ppermute | solution.py:19
  429.9 57.0 %collective-permute-start.72 = (bf16[4,32,4096]{2,1,0:T(8,128)(2,1)}, bf16[4,32,4096]{2,1,0:T(8,128)(2,1)}, u32[]{:S(2)}, u32[]{:S(2)}) collective-permute-start(bf16[4,32,4096]{2,1,0:T(8,128)(2,1)} %get-tuple-element.101), channel_id=1, source_target_pairs={{0,1},{1,0},{2,3},{3,2},{4,5},{5,4},{6,7},{7,6},{8,9},{9,8},{10,11... | collective-permute-start | bytes 3145736 | tf_op jit(solution)/shard_map/ppermute | solution.py:19
  447.9 59.8 %collective-permute-start.47 = (bf16[2,32,1152]{2,1,0:T(8,128)(2,1)}, bf16[2,32,1152]{2,1,0:T(8,128)(2,1)}, u32[]{:S(2)}, u32[]{:S(2)}) collective-permute-start(bf16[2,32,1152]{2,1,0:T(8,128)(2,1)} %bitcast.686), channel_id=1, source_target_pairs={{0,8},{1,9},{2,10},{3,11},{4,12},{5,13},{6,14},{7,15},{8,0},{9,1},... | collective-permute-start | bytes 442376 | tf_op jit(solution)/shard_map/ppermute | solution.py:19
  450.5 57.1 %collective-permute-start.48 = (bf16[2,32,1152]{2,1,0:T(8,128)(2,1)}, bf16[2,32,1152]{2,1,0:T(8,128)(2,1)}, u32[]{:S(2)}, u32[]{:S(2)}) collective-permute-start(bf16[2,32,1152]{2,1,0:T(8,128)(2,1)} %bitcast.682), channel_id=1, source_target_pairs={{0,12},{1,13},{2,14},{3,15},{4,8},{5,9},{6,10},{7,11},{8,4},{9,5},... | collective-permute-start | bytes 442376 | tf_op jit(solution)/shard_map/ppermute | solution.py:19
  451.6 58.5 %collective-permute-start.46 = (bf16[2,32,1152]{2,1,0:T(8,128)(2,1)}, bf16[2,32,1152]{2,1,0:T(8,128)(2,1)}, u32[]{:S(2)}, u32[]{:S(2)}) collective-permute-start(bf16[2,32,1152]{2,1,0:T(8,128)(2,1)} %bitcast.678), channel_id=1, source_target_pairs={{0,4},{1,5},{2,6},{3,7},{4,0},{5,1},{6,2},{7,3},{8,12},{9,13},{10,... | collective-permute-start | bytes 442376 | tf_op jit(solution)/shard_map/ppermute | solution.py:19
  467.9 44.6 %collective-permute-start.56 = (bf16[2,32,1152]{2,1,0:T(8,128)(2,1)}, bf16[2,32,1152]{2,1,0:T(8,128)(2,1)}, u32[]{:S(2)}, u32[]{:S(2)}) collective-permute-start(bf16[2,32,1152]{2,1,0:T(8,128)(2,1)} %bitcast.688), channel_id=1, source_target_pairs={{0,8},{1,9},{2,10},{3,11},{4,12},{5,13},{6,14},{7,15},{8,0},{9,1},... | collective-permute-start | bytes 442376 | tf_op jit(solution)/shard_map/ppermute | solution.py:19
  518.9 252.7 %collective-permute-start.92 = (bf16[576,4096]{1,0:T(8,128)(2,1)}, bf16[576,4096]{1,0:T(8,128)(2,1)}, u32[]{:S(2)}, u32[]{:S(2)}) collective-permute-start(bf16[576,4096]{1,0:T(8,128)(2,1)} %convolution_convert_fusion), channel_id=1, source_target_pairs={{0,2},{1,3},{2,0},{3,1},{4,6},{5,7},{6,4},{7,5},{8,10},{9,11},{10,... | collective-permute-start | bytes 14155784 | tf_op jit(solution)/shard_map/ppermute | solution.py:19
  549.3 53.7 %collective-permute-start.50 = (bf16[32,9216]{1,0:T(8,128)(2,1)}, bf16[32,9216]{1,0:T(8,128)(2,1)}, u32[]{:S(2)}, u32[]{:S(2)}) collective-permute-start(bf16[32,9216]{1,0:T(8,128)(2,1)} %get-tuple-element.118), channel_id=1, source_target_pairs={{0,16},{16,0},{1,17},{17,1},{2,18},{18,2},{3,19},{19,3},{4,20},{20... | collective-permute-start | bytes 1769480 | tf_op jit(solution)/shard_map/ppermute | solution.py:23
  553.7 31.9 %collective-permute-start.59 = (bf16[32,9216]{1,0:T(8,128)(2,1)}, bf16[32,9216]{1,0:T(8,128)(2,1)}, u32[]{:S(2)}, u32[]{:S(2)}) collective-permute-start(bf16[32,9216]{1,0:T(8,128)(2,1)} %get-tuple-element.117), channel_id=1, source_target_pairs={{0,16},{16,0},{1,17},{17,1},{2,18},{18,2},{3,19},{19,3},{4,20},{20... | collective-permute-start | bytes 1769480 | tf_op jit(solution)/shard_map/ppermute | solution.py:23
  584.1 52.0 %collective-permute-start.68 = (bf16[32,9216]{1,0:T(8,128)(2,1)}, bf16[32,9216]{1,0:T(8,128)(2,1)}, u32[]{:S(2)}, u32[]{:S(2)}) collective-permute-start(bf16[32,9216]{1,0:T(8,128)(2,1)} %get-tuple-element.119), channel_id=1, source_target_pairs={{0,16},{16,0},{1,17},{17,1},{2,18},{18,2},{3,19},{19,3},{4,20},{20... | collective-permute-start | bytes 1769480 | tf_op jit(solution)/shard_map/ppermute | solution.py:23
  584.2 57.9 %collective-permute-start.77 = (bf16[32,9216]{1,0:T(8,128)(2,1)}, bf16[32,9216]{1,0:T(8,128)(2,1)}, u32[]{:S(2)}, u32[]{:S(2)}) collective-permute-start(bf16[32,9216]{1,0:T(8,128)(2,1)} %get-tuple-element.120), channel_id=1, source_target_pairs={{0,16},{16,0},{1,17},{17,1},{2,18},{18,2},{3,19},{19,3},{4,20},{20... | collective-permute-start | bytes 1769480 | tf_op jit(solution)/shard_map/ppermute | solution.py:23
  648.1 45.3 %collective-permute-start.88 = (f32[1,13056]{1,0:T(1,128)S(1)}, f32[1,13056]{1,0:T(1,128)S(1)}, u32[]{:S(2)}, u32[]{:S(2)}) collective-permute-start(f32[1,13056]{1,0:T(1,128)S(1)} %broadcast_in_dim.10), channel_id=1, source_target_pairs={{0,1},{1,0},{2,3},{3,2},{4,5},{5,4},{6,7},{7,6},{8,9},{9,8},{10,11... | collective-permute-start | bytes 156680 | tf_op jit(solution)/shard_map/ppermute | solution.py:19
  (138 other events, 2151.1 us)

commit v2 on v1

v2 whole, which is shorter than its diff:
```python
import functools

import jax
import jax.numpy as jnp
from jax import lax
from jax.experimental import pallas as pl
from jax.experimental.pallas import tpu as pltpu
from jax.sharding import PartitionSpec as P

PLAN = "01020130120321301223013201320103211030212130232W132303123W"
BF16 = jnp.bfloat16
F32 = jnp.float32
CONV_DIMS = ("NHWC", "HWIO", "NHWC")
VMEM_LIMIT = 48 * 1024 * 1024


def swap_core(block):
    return lax.ppermute(block, "core", [(0, 1), (1, 0)])


def swap_mid(block):
    return lax.ppermute(block, "mid", [(0, 1), (1, 0)])


def swap_outer(block, mask):
    count = lax.axis_size("outer")
    return lax.ppermute(block, "outer", [(i, i ^ mask) for i in range(count)])


def swap_tower(block):
    return lax.ppermute(block, "tower", [(0, 1), (1, 0)])


def pick(stack, index):
    return lax.dynamic_index_in_dim(stack, index, 0, keepdims=False)


def pool_kernel(e_ref, pooled_ref, inv_ref):
    extent = e_ref.shape[0]
    width = e_ref.shape[3]
    out = (extent - 3) // 2 + 1

    def columns(row):
        cells = [e_ref[row, col].astype(F32) for col in range(extent)]
        return [cells[2 * j] + cells[2 * j + 1] + cells[2 * j + 2] for j in range(out)]

    top = columns(0)
    for i in range(out):
        middle = columns(2 * i + 1)
        bottom = columns(2 * i + 2)
        for j in range(out):
            total = top[j] + middle[j] + bottom[j]
            lanes = pl.ds((i * out + j) * width, width)
            pooled_ref[:, lanes] = jnp.log(total).astype(pooled_ref.dtype)
            inv_ref[:, lanes] = 2.0 / total
        top = bottom


def pool_forward(e):
    extent, _, slots, width = e.shape
    out = (extent - 3) // 2 + 1
    block = 16
    flat = out * out * width
    return pl.pallas_call(
        pool_kernel,
        grid=(slots // block,),
        in_specs=[pl.BlockSpec((extent, extent, block, width), lambda s: (0, 0, s, 0))],
        out_specs=[
            pl.BlockSpec((block, flat), lambda s: (s, 0)),
            pl.BlockSpec((block, flat), lambda s: (s, 0)),
        ],
        out_shape=[
            jax.ShapeDtypeStruct((slots, flat), BF16),
            jax.ShapeDtypeStruct((slots, flat), F32),
        ],
        compiler_params=pltpu.CompilerParams(vmem_limit_bytes=VMEM_LIMIT),
        cost_estimate=pl.CostEstimate(flops=0, bytes_accessed=0, transcendentals=0),
        name="pool_forward",
    )(e)


def pool_back_kernel(slope_ref, grad_ref, back_ref, inv_ref, self_ref, g_ref, bias_ref):
    extent = slope_ref.shape[0]
    width = slope_ref.shape[3]
    out = (extent - 3) // 2 + 1
    coef = self_ref[0:1, :]

    @pl.when(pl.program_id(0) == 0)
    def _():
        bias_ref[...] = jnp.zeros_like(bias_ref)

    def window_row(i):
        row = []
        for j in range(out):
            lanes = pl.ds((i * out + j) * width, width)
            grad = coef * grad_ref[:, lanes].astype(F32) + back_ref[:, lanes].astype(F32)
            row.append(grad * inv_ref[:, lanes])
        return row

    sums = jnp.zeros((slope_ref.shape[2], width), F32)
    above = None
    current = window_row(0)
    for row in range(extent):
        if row % 2 == 0:
            if row == 0:
                rows = current
            elif row == extent - 1:
                rows = current
            else:
                above, current = current, window_row(row // 2)
                rows = [a + b for a, b in zip(above, current)]
        else:
            rows = current
        for col in range(extent):
            if col % 2 == 1:
                spread = rows[col // 2]
            elif col == 0:
                spread = rows[0]
            elif col == extent - 1:
                spread = rows[out - 1]
            else:
                spread = rows[col // 2 - 1] + rows[col // 2]
            grad = (slope_ref[row, col].astype(F32) * spread).astype(g_ref.dtype)
            g_ref[row, col] = grad
            sums = sums + grad.astype(F32)
    bias_ref[...] += sums


def pool_backward(slope, grad_mixed, back_pool, inv, self_pool):
    extent, _, slots, width = slope.shape
    block = 16
    flat = grad_mixed.shape[1]
    rows = pl.BlockSpec((block, flat), lambda s: (s, 0))
    grid_block = pl.BlockSpec((extent, extent, block, width), lambda s: (0, 0, s, 0))
    return pl.pallas_call(
        pool_back_kernel,
        grid=(slots // block,),
        in_specs=[grid_block, rows, rows, rows, pl.BlockSpec((1, width), lambda s: (0, 0))],
        out_specs=[grid_block, pl.BlockSpec((block, width), lambda s: (0, 0))],
        out_shape=[
            jax.ShapeDtypeStruct(slope.shape, BF16),
            jax.ShapeDtypeStruct((block, width), F32),
        ],
        compiler_params=pltpu.CompilerParams(vmem_limit_bytes=VMEM_LIMIT),
        cost_estimate=pl.CostEstimate(flops=0, bytes_accessed=0, transcendentals=0),
        name="pool_backward",
    )(slope, grad_mixed, back_pool, inv, self_pool[None])


def mix_kernel(block, target_ref, core_ref, pooled_ref, partner_ref, self_ref, cross_ref, *out_refs):
    reach = 4 * block
    is_zero = core_ref[0] == 0
    for p, out_ref in enumerate(out_refs):
        lanes = pl.ds(pl.multiple_of(target_ref[p] * reach, 128), reach)
        mixed = self_ref[...] * pooled_ref[:, lanes].astype(F32) + cross_ref[...] * partner_ref[:, lanes].astype(F32)
        piece = [mixed[:, i * block : (i + 1) * block] for i in range(4)]
        first = jnp.concatenate([piece[0], piece[2]], axis=1)
        second = jnp.concatenate([piece[1], piece[3]], axis=1)
        out_ref[0] = jnp.where(is_zero, first, second).astype(out_ref.dtype)
        out_ref[1] = jnp.where(is_zero, second, first).astype(out_ref.dtype)


def mix(pooled, partner_pool, self_pool, cross_pool, target, core, block):
    slots, flat = pooled.shape
    count = flat // (4 * block)
    shape = jax.ShapeDtypeStruct((2, slots, 2 * block), BF16)
    if (4 * block) % 128:
        width = self_pool.shape[0]
        mixed = (
            jnp.tile(self_pool, flat // width) * pooled.astype(F32)
            + jnp.tile(cross_pool, flat // width) * partner_pool.astype(F32)
        ).astype(BF16)
        mixed = mixed.reshape(slots, count, 2, 2, block).transpose(1, 3, 0, 2, 4).reshape(count, 2, slots, 2 * block)
        mixed = jnp.where(core == 0, mixed, mixed[:, ::-1])
        return [pick(mixed, target[p]) for p in range(count)]
    repeat = 4 * block // self_pool.shape[0]
    smem = pl.BlockSpec(memory_space=pltpu.SMEM)
    vmem = pl.BlockSpec(memory_space=pltpu.VMEM)
    return pl.pallas_call(
        functools.partial(mix_kernel, block),
        in_specs=[smem, smem, vmem, vmem, vmem, vmem],
        out_specs=[vmem] * count,
        out_shape=[shape] * count,
        compiler_params=pltpu.CompilerParams(vmem_limit_bytes=VMEM_LIMIT),
        cost_estimate=pl.CostEstimate(flops=0, bytes_accessed=0, transcendentals=0),
        name="mix",
    )(target, core[None], pooled, partner_pool, jnp.tile(self_pool, repeat)[None], jnp.tile(cross_pool, repeat)[None])


def join_kernel(block, count, width, target_ref, core_ref, cross_ref, pooled_ref, partner_ref, far_ref, *refs):
    here_refs = refs[:count]
    grad_ref, sent_ref, sums_ref = refs[count:]
    reach = 4 * block
    is_zero = core_ref[0] == 0
    own_sum = jnp.zeros((1, reach), F32)
    cross_sum = jnp.zeros((1, reach), F32)
    for p in range(count):
        lanes = pl.ds(pl.multiple_of(target_ref[p] * reach, 128), reach)
        here, there = here_refs[p][0].astype(F32), far_ref[p].astype(F32)
        zero, one = jnp.where(is_zero, here, there), jnp.where(is_zero, there, here)
        grad = jnp.concatenate([zero[:, :block], one[:, :block], zero[:, block:], one[:, block:]], axis=1)
        grad_ref[:, lanes] = grad.astype(grad_ref.dtype)
        sent_ref[:, lanes] = (cross_ref[...] * grad).astype(sent_ref.dtype)
        own_sum = own_sum + jnp.sum(pooled_ref[:, lanes].astype(F32) * grad, axis=0, keepdims=True)
        cross_sum = cross_sum + jnp.sum(partner_ref[:, lanes].astype(F32) * grad, axis=0, keepdims=True)
    for row, total in enumerate((own_sum, cross_sum)):
        folded = total[:, :width]
        for cell in range(1, reach // width):
            folded = folded + total[:, cell * width : (cell + 1) * width]
        sums_ref[row : row + 1, :] = folded


def join(here, far, pooled, partner_pool, cross_pool, target, core, block):
    slots, flat = pooled.shape
    count = flat // (4 * block)
    width = cross_pool.shape[0]
    if (4 * block) % 128:
        pieces = jnp.stack([jnp.stack([here[p][0], far[p]]) for p in range(count)])
        pieces = jnp.where(core == 0, pieces, pieces[:, ::-1]).reshape(count, 2, slots, 2, block)
        inverse = jnp.argsort(target)
        grad = jnp.take(pieces, inverse, axis=0).transpose(2, 0, 3, 1, 4).reshape(slots, flat)
        wide = grad.astype(F32)
        sent = (jnp.tile(cross_pool, flat // width) * wide).astype(BF16)
        sums = [
            jnp.sum(jnp.sum(a.astype(F32) * wide, axis=0).reshape(-1, width), axis=0) for a in (pooled, partner_pool)
        ]
        return grad, sent, jnp.stack(sums)
    smem = pl.BlockSpec(memory_space=pltpu.SMEM)
    vmem = pl.BlockSpec(memory_space=pltpu.VMEM)
    return pl.pallas_call(
        functools.partial(join_kernel, block, count, width),
        in_specs=[smem, smem] + [vmem] * (4 + count),
        out_specs=[vmem] * 3,
        out_shape=[
            jax.ShapeDtypeStruct((slots, flat), BF16),
            jax.ShapeDtypeStruct((slots, flat), BF16),
            jax.ShapeDtypeStruct((2, width), F32),
        ],
        compiler_params=pltpu.CompilerParams(vmem_limit_bytes=VMEM_LIMIT),
        cost_estimate=pl.CostEstimate(flops=0, bytes_accessed=0, transcendentals=0),
        name="join",
    )(target, core[None], jnp.tile(cross_pool, 4 * block // width)[None], pooled, partner_pool, far, *here)


def fc_forward_kernel(count, w_ref, got_ref, *refs):
    row_refs = refs[:count]
    chip_ref, sent_ref, all_ref = refs[count:]
    slots = got_ref.shape[1]

    @pl.when(pl.program_id(0) == 0)
    def _():
        for p in range(count):
            all_ref[pl.ds(p * slots, slots), :] = row_refs[p][0]
            all_ref[pl.ds((count + p) * slots, slots), :] = got_ref[p]

    total = jnp.dot(all_ref[...], w_ref[...], preferred_element_type=F32)
    half = count * slots
    for p in range(count):
        chip_ref[p] = total[p * slots : (p + 1) * slots]
        sent_ref[p] = total[half + p * slots : half + (p + 1) * slots].astype(sent_ref.dtype)


def fc_forward(rows, got, weight):
    count, (slots, depth), units = len(rows), got.shape[1:], weight.shape[1]
    tile = 1024
    if count > 4:
        used = jnp.concatenate([r[0] for r in rows] + [got.reshape(-1, depth)])
        total = jnp.dot(used, weight, preferred_element_type=F32).reshape(2, count, slots, units)
        return total[0], total[1].astype(BF16), used
    mine = pl.BlockSpec((1, slots, depth), lambda t: (0, 0, 0))
    out = pl.BlockSpec((count, slots, tile), lambda t: (0, 0, t))
    size = 2 * count * slots
    return pl.pallas_call(
        functools.partial(fc_forward_kernel, count),
        grid=(units // tile,),
        in_specs=[
            pl.BlockSpec((depth, tile), lambda t: (0, t)),
            pl.BlockSpec((count, slots, depth), lambda t: (0, 0, 0)),
        ]
        + [mine] * count,
        out_specs=[out, out, pl.BlockSpec((size, depth), lambda t: (0, 0))],
        out_shape=[
            jax.ShapeDtypeStruct((count, slots, units), F32),
            jax.ShapeDtypeStruct((count, slots, units), BF16),
            jax.ShapeDtypeStruct((size, depth), BF16),
        ],
        compiler_params=pltpu.CompilerParams(vmem_limit_bytes=VMEM_LIMIT),
        cost_estimate=pl.CostEstimate(flops=0, bytes_accessed=0, transcendentals=0),
        name="fc_forward",
    )(weight, got, *rows)


def fc_back_kernel(count, w_ref, own_ref, came_ref, *refs):
    slots = own_ref.shape[1]
    turned = (((1,), (1,)), ((), ()))
    for side, grads in enumerate((own_ref, came_ref)):
        rows = grads[...].reshape(count * slots, grads.shape[2])
        total = lax.dot_general(rows, w_ref[...], turned, preferred_element_type=F32)
        for p in range(count):
            refs[p][side] = total[p * slots : (p + 1) * slots].astype(refs[p].dtype)


def fc_backward(own, came, weight):
    count, slots, units = own.shape
    depth = weight.shape[0]
    tile = 384 if depth % 384 == 0 else depth
    if count > 4:
        grads = jnp.stack([own, came], axis=1).reshape(-1, units)
        columns = lax.dot_general(grads, weight, (((1,), (1,)), ((), ())), preferred_element_type=F32)
        columns = columns.astype(BF16).reshape(count, 2, slots, depth)
        return [columns[p] for p in range(count)]
    grads = pl.BlockSpec((count, slots, units), lambda t: (0, 0, 0))
    return pl.pallas_call(
        functools.partial(fc_back_kernel, count),
        grid=(depth // tile,),
        in_specs=[pl.BlockSpec((tile, units), lambda t: (t, 0)), grads, grads],
        out_specs=[pl.BlockSpec((2, slots, tile), lambda t: (0, 0, t))] * count,
        out_shape=[jax.ShapeDtypeStruct((2, slots, depth), BF16)] * count,
        compiler_params=pltpu.CompilerParams(vmem_limit_bytes=VMEM_LIMIT),
        cost_estimate=pl.CostEstimate(flops=0, bytes_accessed=0, transcendentals=0),
        name="fc_backward",
    )(weight, own, came)


def gelu_parts(v):
    root = 0.7978845608028654
    cubic = 0.044715
    tanh = jnp.tanh(root * (v + cubic * (v * v * v)))
    half = 0.5 * (1.0 + tanh)
    slope = half + 0.5 * v * (1.0 - tanh * tanh) * (root * (1.0 + 3.0 * cubic * (v * v)))
    return v * half, slope


def conv_forward(inputs, kernel, bias):
    pre_conv = lax.conv_general_dilated(
        inputs, kernel, (1, 1), ((1, 1), (1, 1)), dimension_numbers=CONV_DIMS, preferred_element_type=F32
    )
    activity, slope = gelu_parts(pre_conv + bias)
    e = jnp.exp(activity)
    return e.astype(BF16), ((0.5 * e) * slope).astype(BF16)


def conv_grad_inputs(grad_pre, kernel):
    turned = jnp.flip(kernel, (0, 1)).swapaxes(2, 3)
    return lax.conv_general_dilated(
        grad_pre, turned, (1, 1), ((1, 1), (1, 1)), dimension_numbers=CONV_DIMS, preferred_element_type=F32
    ).astype(BF16)


def conv_grad_kernel(inputs, grad_pre):
    dims = lax.ConvDimensionNumbers(lhs_spec=(3, 0, 1, 2), rhs_spec=(3, 0, 1, 2), out_spec=(2, 3, 0, 1))
    return lax.conv_general_dilated(
        inputs, grad_pre, (1, 1), ((1, 1), (1, 1)), dimension_numbers=dims, preferred_element_type=F32
    )


def sum_small(vector):
    vector = vector + swap_core(vector)
    vector = vector + swap_mid(vector)
    step = 1
    while step < lax.axis_size("outer"):
        vector = vector + swap_outer(vector, step)
        step *= 2
    return vector


def sum_kernel(rows, outer, mid, core):
    outer_count = lax.axis_size("outer")
    for swap, side in ((swap_core, core), (swap_mid, mid)):
        halves = rows.reshape(2, -1, rows.shape[1])
        got = swap(pick(halves, 1 - side).astype(BF16))
        rows = pick(halves, side) + got.astype(F32)
    parts = rows.reshape(outer_count, -1, rows.shape[1])
    total = pick(parts, outer)
    for k in range(1, outer_count):
        total = total + swap_outer(pick(parts, outer ^ k).astype(BF16), k).astype(F32)
    total = total.astype(BF16)
    stack = jnp.stack([total] + [swap_outer(total, k) for k in range(1, outer_count)])
    rows = jnp.concatenate([pick(stack, outer ^ k) for k in range(outer_count)])
    for swap, side in ((swap_mid, mid), (swap_core, core)):
        got = swap(rows)
        rows = jnp.where(side == 0, jnp.concatenate([rows, got]), jnp.concatenate([got, rows]))
    return rows.astype(F32)


def body(
    features,
    conv_weight,
    conv_bias,
    fc_weight,
    fc_bias,
    stitch_pool,
    stitch_fc,
    cotangent,
    crop_counts,
    slot_image,
    slot_mask,
):
    is_first = lax.axis_index("tower") == 0
    core, mid, outer = lax.axis_index("core"), lax.axis_index("mid"), lax.axis_index("outer")
    outer_count = lax.axis_size("outer")
    block, units = fc_weight.shape[1:]
    weight = lax.all_gather(fc_weight[0], "mid", axis=0, tiled=True)

    row_pool = stitch_pool[0]
    self_pool = jnp.where(is_first, row_pool[0], row_pool[1])
    cross_pool = jnp.where(is_first, row_pool[1], row_pool[0])
    row_fc = stitch_fc[0]
    self_fc = jnp.where(is_first, row_fc[0], row_fc[1])
    cross_fc = jnp.where(is_first, row_fc[1], row_fc[0])

    live_slots = slot_mask.astype(F32)
    image_ids = jnp.arange(crop_counts.shape[0], dtype=jnp.int32)
    matches = (slot_image[:, None] == image_ids[None, :]).astype(F32)
    per_slot = jnp.sum(matches * crop_counts.astype(F32)[None, :], axis=1)
    scaling = live_slots / per_slot
    sent_fc = (cross_fc * (cotangent[0].astype(F32) * scaling[:, None])).astype(BF16)
    back_fc = swap_tower(sent_fc)

    inputs = features[0]
    kernel = conv_weight[0]
    width = kernel.shape[3]
    hops = outer_count.bit_length() - 1
    order = [sum(((p >> b) & 1) << (hops - 1 - b) for b in range(hops)) for p in range(outer_count)]
    target = outer ^ jnp.array(order, jnp.int32)
    total_slots = inputs.shape[0]
    sizes = [total_slots // 4] * 4 if outer_count <= 4 else [total_slots]
    starts = [sum(sizes[:n]) for n in range(len(sizes))]
    last = [scaling]

    def after(array):
        return lax.optimization_barrier((array, last[0]))[0]

    sums = dict(fc_bias=0.0, hidden_self=0.0, hidden_cross=0.0, pool=0.0, conv_bias=0.0, kernel=0.0)
    stage = {}
    outputs, grads_in = {}, {}
    lead = (((0,), (0,)), ((), ()))

    def chunk(n):
        slots = sizes[n]
        rows = slice(starts[n], starts[n] + slots)
        part = inputs[rows]
        e, slope = conv_forward(part, kernel, after(conv_bias[0]))
        pooled, inv = pool_forward(jnp.transpose(e, (1, 2, 0, 3)))
        last[0] = pooled
        partner_pool = swap_tower(pooled)
        yield
        rows_of = mix(after(pooled), partner_pool, self_pool, cross_pool, target, core, block)
        last[0] = rows_of[0]
        arrived = [rows_of[0]] + [swap_outer(r, k) for r, k in zip(rows_of[1:], order[1:])]
        yield
        arrived[0] = after(arrived[0])
        give = jnp.stack([r[1] for r in arrived])
        last[0] = give
        got = swap_core(give)
        yield
        chip, sent, flat = fc_forward(arrived, after(got), weight)
        last[0] = sent
        came = swap_core(sent)
        yield
        for hop in range(hops):
            chip = chip + after(came).astype(F32)
            half = chip.shape[0] // 2
            sent = chip[half:].astype(BF16)
            chip = chip[:half]
            last[0] = sent
            came = swap_outer(sent, 1 << hop)
            yield
        pre_fc = chip[0] + after(came)[0].astype(F32) + fc_bias[0]
        hidden, slope_fc = gelu_parts(pre_fc)
        hidden = hidden.astype(BF16)
        grad_out = cotangent[0][rows].astype(F32) * scaling[rows, None]
        grad_pre_fc = ((self_fc * grad_out + back_fc[rows].astype(F32)) * slope_fc).astype(BF16)
        sums["fc_bias"] += jnp.sum(grad_pre_fc.astype(F32), axis=0)
        last[0] = grad_pre_fc
        gathered = grad_pre_fc[None]
        for hop in reversed(range(hops)):
            came = swap_outer(gathered, 1 << hop)
            if hop == hops - 1:
                partner_hidden = swap_tower(hidden)
            yield
            gathered = jnp.concatenate([gathered, after(came)])
            last[0] = gathered
        came = swap_core(gathered)
        yield
        came = after(came)
        stage[n] = (flat, gathered, came)
        columns = fc_backward(gathered, came, weight)
        last[0] = columns[0]
        arrived = [columns[0]] + [swap_outer(c, k) for c, k in zip(columns[1:], order[1:])]
        yield
        arrived[0] = after(arrived[0])
        give = jnp.stack([r[1] for r in arrived])
        last[0] = give
        far = swap_core(give)
        yield
        grad_mixed, sent, stitch_sums = join(
            arrived, after(far), pooled, partner_pool, cross_pool, target, core, block
        )
        sums["pool"] += stitch_sums
        last[0] = sent
        back_pool = swap_tower(sent)
        yield
        grad_pre, bias_rows = pool_backward(
            jnp.transpose(slope, (1, 2, 0, 3)), grad_mixed, after(back_pool), inv, self_pool
        )
        sums["conv_bias"] += jnp.sum(bias_rows, axis=0)
        grad_pre = jnp.transpose(grad_pre, (2, 0, 1, 3))
        grad_kernel = conv_grad_kernel(part, grad_pre)
        sums["kernel"] += grad_kernel
        last[0] = grad_kernel
        yield
        grads_in[n] = conv_grad_inputs(after(grad_pre), kernel)
        last[0] = grads_in[n]
        stitched = self_fc * hidden.astype(F32) + cross_fc * partner_hidden.astype(F32)
        outputs[n] = (stitched * live_slots[rows, None]).astype(BF16)
        sums["hidden_self"] += jnp.sum(hidden.astype(F32) * grad_out, axis=0)
        sums["hidden_cross"] += jnp.sum(partner_hidden.astype(F32) * grad_out, axis=0)

    def fc_weight_gradient():
        columns = jnp.concatenate([stage[n][0] for n in range(len(sizes))])
        grads = after(jnp.concatenate([g.reshape(-1, units) for n in range(len(sizes)) for g in stage[n][1:]]))
        own, far = columns[:, :block], columns[:, block:]
        own, far = jnp.where(mid == 0, own, far), jnp.where(mid == 0, far, own)
        far_term = lax.dot_general(far, grads, lead, preferred_element_type=F32).astype(BF16)
        last[0] = far_term
        came = swap_mid(far_term)
        yield
        own, came = lax.optimization_barrier((own, after(came)))
        stage["gradient"] = lax.dot_general(own, grads, lead, preferred_element_type=F32) + came.astype(F32)
        last[0] = stage["gradient"]

    running = [chunk(n) for n in range(len(sizes))]
    weight_run = fc_weight_gradient()
    for n in PLAN if len(sizes) > 1 else "0" * (2 * hops + 6) + "W" + "0" * 5 + "W":
        next(weight_run if n == "W" else running[int(n)], None)
    outputs = [outputs[n] for n in range(len(sizes))]
    grads_in = [grads_in[n] for n in range(len(sizes))]
    grad_fc_weight = stage["gradient"]
    kernel_sum = sums["kernel"]
    conv_bias_sum, fc_bias_sum = sums["conv_bias"], sums["fc_bias"]
    hidden_self, hidden_cross = sums["hidden_self"], sums["hidden_cross"]
    pool_self, pool_cross = sums["pool"]

    small = sum_small(
        jnp.concatenate([conv_bias_sum, pool_self, pool_cross, fc_bias_sum, hidden_self, hidden_cross])[None]
    )[0]
    cuts = [width, 2 * width, 3 * width, 3 * width + units, 3 * width + 2 * units]
    conv_bias_sum, pool_self, pool_cross, fc_bias_sum, hidden_self, hidden_cross = jnp.split(small, cuts)
    grad_row_pool = jnp.where(
        is_first, jnp.stack([pool_self, pool_cross]), jnp.stack([pool_cross, pool_self])
    )
    grad_row_fc = jnp.where(
        is_first, jnp.stack([hidden_self, hidden_cross]), jnp.stack([hidden_cross, hidden_self])
    )
    summed_kernel = sum_kernel(kernel_sum.reshape(-1, width), outer, mid, core).reshape(kernel.shape)
    return (
        jnp.concatenate(outputs)[None],
        jnp.concatenate(grads_in)[None],
        summed_kernel[None],
        conv_bias_sum[None],
        grad_fc_weight[None],
        fc_bias_sum[None],
        grad_row_pool[None],
        grad_row_fc[None],
    )


def solution(mesh):
    mesh = jax.sharding.Mesh(mesh.devices.reshape(mesh.shape["tower"], -1, 2, 2), ("tower", "outer", "mid", "core"))
    crops = ("outer", "mid", "core")
    placed = (
        P("tower", crops, None, None, None),
        P("tower", None, None, None, None),
        P("tower", None),
        P("tower", crops, None),
        P("tower", None),
        P("tower", None, None),
        P("tower", None, None),
        P("tower", crops, None),
        P(crops),
        P(crops),
        P(crops),
    )
    return jax.shard_map(
        body,
        mesh=mesh,
        in_specs=placed,
        out_specs=(
            P("tower", crops, None),
            P("tower", crops, None, None, None),
            P("tower", None, None, None, None),
            P("tower", None),
            P("tower", crops, None),
            P("tower", None),
            P("tower", None, None),
            P("tower", None, None),
        ),
        check_vma=False,
    )
```

time: 794 us -> 647 us (0.81)
  waiting for transfers between devices: 189 us -> 118 us
  starting transfers between devices: 160 us -> 91.7 us
  Pallas kernels: 24.3 us -> 90.1 us
  matrix products: 250 us -> 212 us
  other arithmetic: 101 us -> 63.9 us
  between operations: 3.23 us -> 16.2 us
  local copies, waits for them, and re-layouts: 54.9 us -> 44.3 us
    pallas_call x0 -> x16, Pallas kernels: none -> 74.7 us  [the longest x4 34 us: fc_backward(): pl.pallas_call(functools.partial(fc_back_kernel, count), grid=(depth // t...]
    ppermute x80 -> x71, starting transfers between devices: 149 us -> 80.8 us  [the longest x48 53.9 us: swap_outer(): return lax.ppermute(block, 'outer', [(i, i ^ mask) for i in range(count)])]
    ppermute x80 -> x71, waiting for transfers between devices: 153 us -> 94.9 us  [the longest x48 85.2 us: swap_outer(): return lax.ppermute(block, 'outer', [(i, i ^ mask) for i in range(count)])]
    ppermute x13, waiting for transfers between devices: 36 us -> 0.03 us  [swap_tower(): return lax.ppermute(block, 'tower', [(0, 1), (1, 0)])]
    dot_general x18 -> x2, matrix products: 52.9 us -> 19.9 us  [the longest x1 10.5 us: fc_weight_gradient(): lax.dot_general(own, grads, lead, preferred_element_type=F32)]
    all_gather x0 -> x1, waiting for transfers between devices: none -> 22 us  [body(): weight = lax.all_gather(fc_weight[0], 'mid', axis=0, tiled=True)]
    select_n x51 -> x2, other arithmetic: 22.8 us -> 1.55 us  [the longest x1 1.54 us: fc_weight_gradient(): own, far = (jnp.where(mid == 0, own, far), jnp.where(mid == 0, far, own))]
    slice x22 -> x42, local copies, waits for them, and re-layouts: 26.5 us -> 11.9 us  [the longest x32 6.16 us: chunk(): give = jnp.stack([r[1] for r in arrived])]
  transfers between devices with their start and end apart: 93 -> 85, of which waited for: 24 -> 20; matrix products, arithmetic and copies ran while one was open for 48% -> 46% of each run, Pallas kernels for 3% -> 14%
where the time goes in v2:
time: 647 us; the launch traced here: 636 us
  matrix products  212 us (33%)
  waiting for transfers between devices  118 us (18%)
  starting transfers between devices  91.7 us (14%)
  Pallas kernels  90.1 us (14%)
  other arithmetic  63.9 us (10%)
  local copies, waits for them, and re-layouts  44.3 us (7%)
  between operations  16.2 us (3%)
    ppermute x48, waiting for transfers between devices, swap_outer(): return lax.ppermute(block, 'outer', [(i, i ^ mask) for i in range(count)])  85.2 us
    conv_general_dilated x4, matrix products, conv_forward(): lax.conv_general_dilated(inputs, kernel, (1, 1), ((1, 1), (1, 1)), dimens...  74.9 us
    conv_general_dilated x4, matrix products, conv_grad_inputs(): lax.conv_general_dilated(grad_pre, turned, (1, 1), ((1, 1), (1, 1)), dime...  59.9 us
    conv_general_dilated x4, matrix products, conv_grad_kernel(): lax.conv_general_dilated(inputs, grad_pre, (1, 1), ((1, 1), (1, 1)), dime...  57.6 us
    ppermute x48, starting transfers between devices, swap_outer(): return lax.ppermute(block, 'outer', [(i, i ^ mask) for i in range(count)])  53.9 us
    pallas_call x4, Pallas kernels, fc_backward(): pl.pallas_call(functools.partial(fc_back_kernel, count), grid=(depth // t...  34 us
    unnamed x264, local copies, waits for them, and re-layouts  27.2 us
    pallas_call x4, Pallas kernels, fc_forward(): pl.pallas_call(functools.partial(fc_forward_kernel, count), grid=(units /...  26.4 us
  transfers between devices with their start and end apart: 85, of which 20 were waited for; matrix products, arithmetic and copies ran while one was open for 46% of the time, Pallas kernels for 14%

profile of v2, /device:TPU:1, one launch (start us, length us, event | category | flops | bytes accessed | tf_op | source)
XLA Modules:
  0.0 636.2 jit_solution(14379720806934570207)
XLA Ops:
  8.7 18.8 %fusion.9 = (bf16[13,13,32,256]{3,2,1,0:T(8,128)(2,1)}, bf16[13,13,32,256]{3,2,1,0:T(8,128)(2,1)S(1)}) fusion(f32[256]{0:T(256)S(1)} %bitcast.293, bf16[1,3,3,384,256]{4,3,2,1,0:T(8,128)(2,1)S(1)} %copy-done, bf16[1,128,13,13,384]{4,1,3,2,0:T(8,128)(2,1)} %param.12), kind=kOutput, calls=%fused_computation.20 | convolution fusion | flops 8643461120 | bytes 11461632 | tf_op jit(solution)/shard_map/conv_general_dilated | solution.py:335
  30.5 18.7 %fusion.19 = (bf16[13,13,32,256]{3,2,1,0:T(8,128)(2,1)}, bf16[13,13,32,256]{3,2,1,0:T(8,128)(2,1)S(1)}) fusion(f32[256]{0:T(256)S(1)} %bitcast.294, bf16[1,3,3,384,256]{4,3,2,1,0:T(8,128)(2,1)S(1)} %copy-done, bf16[1,128,13,13,384]{4,1,3,2,0:T(8,128)(2,1)} %param.12), kind=kOutput, calls=%fused_computation.30 | convolution fusion | flops 8643461120 | bytes 11461632 | tf_op jit(solution)/shard_map/conv_general_dilated | solution.py:335
  57.5 18.7 %fusion.29 = (bf16[13,13,32,256]{3,2,1,0:T(8,128)(2,1)}, bf16[13,13,32,256]{3,2,1,0:T(8,128)(2,1)S(1)}) fusion(f32[256]{0:T(256)} %bitcast.292, bf16[1,3,3,384,256]{4,3,2,1,0:T(8,128)(2,1)S(1)} %copy-done, bf16[1,128,13,13,384]{4,1,3,2,0:T(8,128)(2,1)} %param.12), kind=kOutput, calls=%fused_computation.40 | convolution fusion | flops 8643461120 | bytes 11461632 | tf_op jit(solution)/shard_map/conv_general_dilated | solution.py:335
  82.8 18.7 %fusion.39 = (bf16[13,13,32,256]{3,2,1,0:T(8,128)(2,1)}, bf16[13,13,32,256]{3,2,1,0:T(8,128)(2,1)S(1)}) fusion(f32[256]{0:T(256)S(1)} %bitcast.295, bf16[1,3,3,384,256]{4,3,2,1,0:T(8,128)(2,1)S(1)} %copy-done, bf16[1,128,13,13,384]{4,1,3,2,0:T(8,128)(2,1)} %param.12), kind=kOutput, calls=%fused_computation.50 | convolution fusion | flops 8643461120 | bytes 11461632 | tf_op jit(solution)/shard_map/conv_general_dilated | solution.py:335
  107.7 22.0 %all-gather.3.cloned.1.call-done = bf16[1,1152,4096]{2,1,0:T(8,128)(2,1)} async-done(((bf16[1,576,4096]{2,1,0:T(8,128)(2,1)}), bf16[1,1152,4096]{2,1,0:T(8,128)(2,1)}) %all-gather.3.cloned.1.call-update) | async-done | bytes 9437200 | tf_op jit(solution)/shard_map/all_gather | solution.py:403
  133.4 6.3 fc_forward.4
  148.4 5.6 collective-permute-done.14.refs_1_
  165.5 6.3 fc_forward.5
  182.3 7.3 %fc_forward.6 = (f32[4,32,4096]{2,1,0:T(8,128)S(1)}, bf16[4,32,4096]{2,1,0:T(8,128)(2,1)}, bf16[256,1152]{1,0:T(8,128)(2,1)S(1)}) custom-call(bf16[1152,4096]{1,0:T(8,128)(2,1)} %bitcast.251, bf16[4,32,1152]{2,1,0:T(8,128)(2,1)S(1)} %collective-permute-done.22.got_ref, bf16[2,32,1152]{2,1,0:T(8,128)(2,1)S(1)} %get-tuple-element.168.refs_0_, ...), custom_call_target="tpu_custom_call" | custom-call | tf_op jit(solution)/shard_map/fc_forward/pallas_call | solution.py:273
  202.2 6.5 %fc_forward.7 = (f32[4,32,4096]{2,1,0:T(8,128)S(1)}, bf16[4,32,4096]{2,1,0:T(8,128)(2,1)S(1)}, bf16[256,1152]{1,0:T(8,128)(2,1)S(1)}) custom-call(bf16[1152,4096]{1,0:T(8,128)(2,1)} %bitcast.252, bf16[4,32,1152]{2,1,0:T(8,128)(2,1)S(1)} %collective-permute-done.21.got_ref, bf16[2,32,1152]{2,1,0:T(8,128)(2,1)S(1)} %copy-done.33, ...), custom_call_target="tpu_custom_call" | custom-call | tf_op jit(solution)/shard_map/fc_forward/pallas_call | solution.py:273
  222.3 11.9 %collective-permute-done.30 = bf16[2,32,4096]{2,1,0:T(8,128)(2,1)} collective-permute-done((bf16[2,32,4096]{2,1,0:T(8,128)(2,1)}, bf16[2,32,4096]{2,1,0:T(8,128)(2,1)}, u32[]{:S(2)}, u32[]{:S(2)}) %collective-permute-start.30) | collective-permute-done | bytes 524320 | tf_op jit(solution)/shard_map/ppermute | solution.py:27
  236.9 5.4 collective-permute-done.28
  245.2 16.1 %collective-permute-done.34 = bf16[2,32,4096]{2,1,0:T(8,128)(2,1)S(1)} collective-permute-done((bf16[2,32,4096]{2,1,0:T(8,128)(2,1)S(1)}, bf16[2,32,4096]{2,1,0:T(8,128)(2,1)S(1)}, u32[]{:S(2)}, u32[]{:S(2)}) %collective-permute-start.34) | collective-permute-done | bytes 524320 | tf_op jit(solution)/shard_map/ppermute | solution.py:27
  265.0 7.6 %collective-permute-done.37 = bf16[2,32,4096]{2,1,0:T(8,128)(2,1)S(1)} collective-permute-done((bf16[2,32,4096]{2,1,0:T(8,128)(2,1)S(1)}, bf16[2,32,4096]{2,1,0:T(8,128)(2,1)S(1)}, u32[]{:S(2)}, u32[]{:S(2)}) %collective-permute-start.37) | collective-permute-done | bytes 524320 | tf_op jit(solution)/shard_map/ppermute | solution.py:27
  279.1 8.0 %fc_backward.4 = (bf16[2,32,1152]{2,1,0:T(8,128)(2,1)S(1)}, bf16[2,32,1152]{2,1,0:T(8,128)(2,1)S(1)}, bf16[2,32,1152]{2,1,0:T(8,128)(2,1)S(1)}, bf16[2,32,1152]{2,1,0:T(8,128)(2,1)S(1)}) custom-call(bf16[1152,4096]{1,0:T(8,128)(2,1)} %bitcast.253, bf16[4,32,4096]{2,1,0:T(8,128)(2,1)S(1)} %pad_maximum_fusion.own_ref, ...), custom_call_target="tpu_custom_call" | custom-call | tf_op jit(solution)/shard_map/fc_backward/pallas_call | solution.py:313
  293.8 10.3 %collective-permute-done.42 = bf16[1,32,4096]{2,1,0:T(8,128)(2,1)S(1)} collective-permute-done((bf16[1,32,4096]{2,1,0:T(8,128)(2,1)S(1)}, bf16[1,32,4096]{2,1,0:T(8,128)(2,1)S(1)}, u32[]{:S(2)}, u32[]{:S(2)}) %collective-permute-start.42) | collective-permute-done | bytes 262176 | tf_op jit(solution)/shard_map/ppermute | solution.py:27
  324.0 8.4 %fc_backward.5 = (bf16[2,32,1152]{2,1,0:T(8,128)(2,1)S(1)}, bf16[2,32,1152]{2,1,0:T(8,128)(2,1)S(1)}, bf16[2,32,1152]{2,1,0:T(8,128)(2,1)S(1)}, bf16[2,32,1152]{2,1,0:T(8,128)(2,1)S(1)}) custom-call(bf16[1152,4096]{1,0:T(8,128)(2,1)} %bitcast.254, bf16[4,32,4096]{2,1,0:T(8,128)(2,1)S(1)} %pad_maximum_fusion.1.own_ref, ...), custom_call_target="tpu_custom_call" | custom-call | tf_op jit(solution)/shard_map/fc_backward/pallas_call | solution.py:313
  354.1 8.7 %fc_backward.6 = (bf16[2,32,1152]{2,1,0:T(8,128)(2,1)S(1)}, bf16[2,32,1152]{2,1,0:T(8,128)(2,1)}, bf16[2,32,1152]{2,1,0:T(8,128)(2,1)}, bf16[2,32,1152]{2,1,0:T(8,128)(2,1)}) custom-call(bf16[1152,4096]{1,0:T(8,128)(2,1)} %bitcast.255, bf16[4,32,4096]{2,1,0:T(8,128)(2,1)S(1)} %pad_maximum_fusion.2.own_ref, ...), custom_call_target="tpu_custom_call" | custom-call | tf_op jit(solution)/shard_map/fc_backward/pallas_call | solution.py:313
  370.2 14.2 %fusion.56 = f32[3,3,384,256]{3,2,1,0:T(8,128)} fusion(bf16[13,13,32,256]{3,2,1,0:T(8,128)(2,1)S(1)} %get-tuple-element.225, bf16[1,128,13,13,384]{4,1,3,2,0:T(8,128)(2,1)} %param.12), kind=kOutput, calls=%fused_computation.75 | convolution fusion | flops 8613003264 | bytes 10461184 | tf_op jit(solution)/shard_map/conv_general_dilated | solution.py:352
  389.6 5.4 collective-permute-done.58.refs_1_
  400.3 9.0 %fc_backward.7 = (bf16[2,32,1152]{2,1,0:T(8,128)(2,1)S(1)}, bf16[2,32,1152]{2,1,0:T(8,128)(2,1)}, bf16[2,32,1152]{2,1,0:T(8,128)(2,1)}, bf16[2,32,1152]{2,1,0:T(8,128)(2,1)}) custom-call(bf16[1152,4096]{1,0:T(8,128)(2,1)} %bitcast.256, bf16[4,32,4096]{2,1,0:T(8,128)(2,1)S(1)} %pad_maximum_fusion.3.own_ref, bf16[4,32,4096]{2,1,0:T(8,128)(2,1)} %collective-permute-done.57.came_ref), custom_call_target="tpu_custom_call" | custom-call | tf_op jit(solution)/shard_map/fc_backward/pallas_call | solution.py:313
  415.8 9.4 %convolution_convert_fusion = bf16[576,4096]{1,0:T(8,128)(2,1)} fusion(bf16[1024,4096]{1,0:T(8,128)(2,1)} %constant_dynamic-update-slice_fusion.4, pred[]{:T(512)S(6)} %eq.28, bf16[1024,1152]{1,0:T(8,128)(2,1)S(1)} %copy-done.82), kind=kOutput, calls=%fused_computation.10 | convolution fusion | flops 4834787328 | bytes 15728641 | tf_op jit(solution)/shard_map/dot_general | solution.py:525
  433.7 14.2 %fusion.52 = f32[3,3,384,256]{3,2,1,0:T(8,128)} fusion(bf16[13,13,32,256]{3,2,1,0:T(8,128)(2,1)S(1)} %get-tuple-element.242, bf16[1,128,13,13,384]{4,1,3,2,0:T(8,128)(2,1)} %param.12), kind=kOutput, calls=%fused_computation.71 | convolution fusion | flops 8613003264 | bytes 10461184 | tf_op jit(solution)/shard_map/conv_general_dilated | solution.py:352
  458.9 14.8 %fusion.48 = f32[3,3,384,256]{3,2,1,0:T(8,128)} fusion(bf16[13,13,32,256]{3,2,1,0:T(8,128)(2,1)S(1)} %get-tuple-element.250, bf16[1,128,13,13,384]{4,1,3,2,0:T(8,128)(2,1)} %param.12), kind=kOutput, calls=%fused_computation.67 | convolution fusion | flops 8613003264 | bytes 10461184 | tf_op jit(solution)/shard_map/conv_general_dilated | solution.py:352
  476.4 14.9 %convolution_convert_fusion.4 = bf16[32,13,13,384]{3,0,2,1:T(8,128)(2,1)} fusion(bf16[32,13,13,256]{3,0,2,1:T(8,128)(2,1)S(1)} %bitcast.245, bf16[1,3,3,384,256]{4,3,2,1,0:T(8,128)(2,1)S(1)} %copy-done), kind=kOutput, calls=%fused_computation.91 | convolution fusion | flops 8615079936 | bytes 8691712 | tf_op jit(solution)/shard_map/conv_general_dilated | solution.py:345
  511.7 14.5 %add_add_fusion = f32[3,3,384,256]{3,2,1,0:T(8,128)S(1)} fusion(f32[3,3,384,256]{3,2,1,0:T(8,128)} %fusion.48, f32[3,3,384,256]{3,2,1,0:T(8,128)} %fusion.56, f32[3,3,384,256]{3,2,1,0:T(8,128)} %fusion.52, bf16[13,13,32,256]{3,2,1,0:T(8,128)(2,1)} %copy-done.72, bf16[1,128,13,13,384]{4,1,3,2,0:T(8,128)(2,1)} %param.12), kind=kOutput, calls=%fused_computation.87 | convolution fusion | flops 8615657472 | bytes 21078016 | tf_op jit(solution)/shard_map/conv_general_dilated | solution.py:352
  526.7 15.1 %convolution_convert_fusion.3 = bf16[32,13,13,384]{3,0,2,1:T(8,128)(2,1)} fusion(bf16[32,13,13,256]{3,0,2,1:T(8,128)(2,1)S(1)} %bitcast.247, bf16[1,3,3,384,256]{4,3,2,1,0:T(8,128)(2,1)S(1)} %copy-done), kind=kOutput, calls=%fused_computation.90 | convolution fusion | flops 8615079936 | bytes 8691712 | tf_op jit(solution)/shard_map/conv_general_dilated | solution.py:345
  543.9 9.6 %collective-permute-done.70 = bf16[864,256]{1,0:T(8,128)(2,1)S(1)} collective-permute-done((bf16[864,256]{1,0:T(8,128)(2,1)S(1)}, bf16[864,256]{1,0:T(8,128)(2,1)S(1)}, u32[]{:S(2)}, u32[]{:S(2)}) %collective-permute-start.70) | collective-permute-done | bytes 442400 | tf_op jit(solution)/shard_map/ppermute | solution.py:22
  557.3 14.9 %convolution_convert_fusion.2 = bf16[32,13,13,384]{3,0,2,1:T(8,128)(2,1)} fusion(bf16[32,13,13,256]{3,0,2,1:T(8,128)(2,1)S(1)} %bitcast.246, bf16[1,3,3,384,256]{4,3,2,1,0:T(8,128)(2,1)S(1)} %copy-done), kind=kOutput, calls=%fused_computation.89 | convolution fusion | flops 8615079936 | bytes 8691712 | tf_op jit(solution)/shard_map/conv_general_dilated | solution.py:345
  576.1 15.1 %convolution_convert_fusion.1 = bf16[32,13,13,384]{3,0,2,1:T(8,128)(2,1)} fusion(bf16[32,13,13,256]{3,0,2,1:T(8,128)(2,1)S(1)} %bitcast.248, bf16[1,3,3,384,256]{4,3,2,1,0:T(8,128)(2,1)S(1)} %copy-done), kind=kOutput, calls=%fused_computation.88 | convolution fusion | flops 8615079936 | bytes 8691712 | tf_op jit(solution)/shard_map/conv_general_dilated | solution.py:345
  593.8 15.0 %maximum_bitcast_fusion = bf16[1,128,13,13,384]{4,1,3,2,0:T(8,128)(2,1)} fusion(bf16[32,13,13,384]{3,0,2,1:T(8,128)(2,1)} %convolution_convert_fusion.1, bf16[32,13,13,384]{3,0,2,1:T(8,128)(2,1)} %convolution_convert_fusion.2, bf16[32,13,13,384]{3,0,2,1:T(8,128)(2,1)} %convolution_convert_fusion.3, bf16[32,13,13,384]{3,0,2,1:T(8,128)(2,1)S(1)} %copy-done.83), kind=kLoop, calls=%fused_computation | loop fusion | flops 66453504 | bytes 33226752 | tf_op jit(solution)/shard_map/broadcast_in_dim | solution.py:559
  618.4 10.5 %add_bitcast_fusion = f32[1,576,4096]{2,1,0:T(8,128)} fusion(bf16[576,4096]{1,0:T(8,128)(2,1)} %collective-permute-done.83, bf16[1024,576]{1,0:T(8,128)(2,1)S(1)} %copy-done.75, bf16[1024,4096]{1,0:T(8,128)(2,1)} %constant_dynamic-update-slice_fusion.4), kind=kOutput, calls=%fused_computation.1 | convolution fusion | flops 4836556800 | bytes 23724032 | tf_op jit(solution)/shard_map/dot_general | solution.py:530
  (557 shorter events, 238.4 us)
Async XLA Ops:
  7.2 122.5 %all-gather.3.cloned.1.call-start = ((), (), s32[]{:S(2)}) async-start(), calls=%async_computation | async-start | bytes 14155776 | tf_op jit(solution)/shard_map/all_gather | solution.py:403
  28.4 23.9 %collective-permute-start = (bf16[32,9216]{1,0:T(8,128)(2,1)S(1)}, bf16[32,9216]{1,0:T(8,128)(2,1)}, u32[]{:S(2)}, u32[]{:S(2)}) collective-permute-start(bf16[32,9216]{1,0:T(8,128)(2,1)S(1)} %get-tuple-element.144.pooled_ref), channel_id=1, source_target_pairs={{0,16},{16,0},{1,17},{17,1},{2,18},{18,2},{3,19},{19,3},{4,20},{20... | collective-permute-start | bytes 1769480 | tf_op jit(solution)/shard_map/ppermute | solution.py:31
  51.1 30.1 %collective-permute-start.5 = (bf16[32,9216]{1,0:T(8,128)(2,1)S(1)}, bf16[32,9216]{1,0:T(8,128)(2,1)S(1)}, u32[]{:S(2)}, u32[]{:S(2)}) collective-permute-start(bf16[32,9216]{1,0:T(8,128)(2,1)S(1)} %get-tuple-element.152.pooled_ref), channel_id=1, source_target_pairs={{0,16},{16,0},{1,17},{17,1},{2,18},{18,2},{3,19},{19,3},{4,20},{20... | collective-permute-start | bytes 1769480 | tf_op jit(solution)/shard_map/ppermute | solution.py:31
  53.6 25.0 %collective-permute-start.1 = (bf16[2,32,1152]{2,1,0:T(8,128)(2,1)S(1)}, bf16[2,32,1152]{2,1,0:T(8,128)(2,1)S(1)}, u32[]{:S(2)}, u32[]{:S(2)}) collective-permute-start(bf16[2,32,1152]{2,1,0:T(8,128)(2,1)S(1)} %get-tuple-element.149), channel_id=1, source_target_pairs={{0,8},{4,12},{8,0},{12,4},{1,9},{5,13},{9,1},{13,5},{2,10},{6,14},... | collective-permute-start | bytes 442376 | tf_op jit(solution)/shard_map/ppermute | solution.py:27
  56.2 22.5 %collective-permute-start.2 = (bf16[2,32,1152]{2,1,0:T(8,128)(2,1)S(1)}, bf16[2,32,1152]{2,1,0:T(8,128)(2,1)S(1)}, u32[]{:S(2)}, u32[]{:S(2)}) collective-permute-start(bf16[2,32,1152]{2,1,0:T(8,128)(2,1)S(1)} %get-tuple-element.150), channel_id=1, source_target_pairs={{0,4},{4,0},{8,12},{12,8},{1,5},{5,1},{9,13},{13,9},{2,6},{6,2},{1... | collective-permute-start | bytes 442376 | tf_op jit(solution)/shard_map/ppermute | solution.py:27
  77.8 65.1 %collective-permute-start.10 = (bf16[32,9216]{1,0:T(8,128)(2,1)}, bf16[32,9216]{1,0:T(8,128)(2,1)}, u32[]{:S(2)}, u32[]{:S(2)}) collective-permute-start(bf16[32,9216]{1,0:T(8,128)(2,1)} %get-tuple-element.163.pooled_ref), channel_id=1, source_target_pairs={{0,16},{16,0},{1,17},{17,1},{2,18},{18,2},{3,19},{19,3},{4,20},{20... | collective-permute-start | bytes 1769480 | tf_op jit(solution)/shard_map/ppermute | solution.py:31
  78.8 28.2 %collective-permute-start.4 = (bf16[4,32,1152]{2,1,0:T(8,128)(2,1)S(1)}, bf16[4,32,1152]{2,1,0:T(8,128)(2,1)S(1)}, u32[]{:S(2)}, u32[]{:S(2)}) collective-permute-start(bf16[4,32,1152]{2,1,0:T(8,128)(2,1)S(1)} %pad_maximum_fusion.10), channel_id=1, source_target_pairs={{0,1},{1,0},{2,3},{3,2},{4,5},{5,4},{6,7},{7,6},{8,9},{9,8},{10,11... | collective-permute-start | bytes 884744 | tf_op jit(solution)/shard_map/ppermute | solution.py:18
  103.4 37.7 %collective-permute-start.7 = (bf16[2,32,1152]{2,1,0:T(8,128)(2,1)}, bf16[2,32,1152]{2,1,0:T(8,128)(2,1)S(1)}, u32[]{:S(2)}, u32[]{:S(2)}) collective-permute-start(bf16[2,32,1152]{2,1,0:T(8,128)(2,1)} %get-tuple-element.160), channel_id=1, source_target_pairs={{0,8},{4,12},{8,0},{12,4},{1,9},{5,13},{9,1},{13,5},{2,10},{6,14},... | collective-permute-start | bytes 442376 | tf_op jit(solution)/shard_map/ppermute | solution.py:27
  104.8 37.5 %collective-permute-start.8 = (bf16[2,32,1152]{2,1,0:T(8,128)(2,1)}, bf16[2,32,1152]{2,1,0:T(8,128)(2,1)S(1)}, u32[]{:S(2)}, u32[]{:S(2)}) collective-permute-start(bf16[2,32,1152]{2,1,0:T(8,128)(2,1)} %get-tuple-element.161), channel_id=1, source_target_pairs={{0,4},{4,0},{8,12},{12,8},{1,5},{5,1},{9,13},{13,9},{2,6},{6,2},{1... | collective-permute-start | bytes 442376 | tf_op jit(solution)/shard_map/ppermute | solution.py:27
  107.0 35.4 %collective-permute-start.9 = (bf16[2,32,1152]{2,1,0:T(8,128)(2,1)}, bf16[2,32,1152]{2,1,0:T(8,128)(2,1)S(1)}, u32[]{:S(2)}, u32[]{:S(2)}) collective-permute-start(bf16[2,32,1152]{2,1,0:T(8,128)(2,1)} %get-tuple-element.162), channel_id=1, source_target_pairs={{0,12},{4,8},{8,4},{12,0},{1,13},{5,9},{9,5},{13,1},{2,14},{6,10},... | collective-permute-start | bytes 442376 | tf_op jit(solution)/shard_map/ppermute | solution.py:27
  142.5 22.7 %collective-permute-start.13 = (bf16[4,32,1152]{2,1,0:T(8,128)(2,1)S(1)}, bf16[4,32,1152]{2,1,0:T(8,128)(2,1)S(1)}, u32[]{:S(2)}, u32[]{:S(2)}) collective-permute-start(bf16[4,32,1152]{2,1,0:T(8,128)(2,1)S(1)} %pad_maximum_fusion.11), channel_id=1, source_target_pairs={{0,1},{1,0},{2,3},{3,2},{4,5},{5,4},{6,7},{7,6},{8,9},{9,8},{10,11... | collective-permute-start | bytes 884744 | tf_op jit(solution)/shard_map/ppermute | solution.py:18
  154.0 26.0 %collective-permute-start.11 = (bf16[2,32,4096]{2,1,0:T(8,128)(2,1)S(1)}, bf16[2,32,4096]{2,1,0:T(8,128)(2,1)S(1)}, u32[]{:S(2)}, u32[]{:S(2)}) collective-permute-start(bf16[2,32,4096]{2,1,0:T(8,128)(2,1)S(1)} %slice.501), channel_id=1, source_target_pairs={{0,4},{4,0},{8,12},{12,8},{1,5},{5,1},{9,13},{13,9},{2,6},{6,2},{1... | collective-permute-start | bytes 1572872 | tf_op jit(solution)/shard_map/ppermute | solution.py:27
  165.2 45.7 %collective-permute-start.27 = (bf16[128,4096]{1,0:T(8,128)(2,1)}, bf16[128,4096]{1,0:T(8,128)(2,1)}, u32[]{:S(2)}, u32[]{:S(2)}) collective-permute-start(bf16[128,4096]{1,0:T(8,128)(2,1)} %fusion.69), channel_id=1, source_target_pairs={{0,16},{16,0},{1,17},{17,1},{2,18},{18,2},{3,19},{19,3},{4,20},{20... | collective-permute-start | bytes 3145736 | tf_op jit(solution)/shard_map/ppermute | solution.py:31
  202.1 32.1 %collective-permute-start.30 = (bf16[2,32,4096]{2,1,0:T(8,128)(2,1)}, bf16[2,32,4096]{2,1,0:T(8,128)(2,1)}, u32[]{:S(2)}, u32[]{:S(2)}) collective-permute-start(bf16[2,32,4096]{2,1,0:T(8,128)(2,1)} %slice.499), channel_id=1, source_target_pairs={{0,4},{4,0},{8,12},{12,8},{1,5},{5,1},{9,13},{13,9},{2,6},{6,2},{1... | collective-permute-start | bytes 1572872 | tf_op jit(solution)/shard_map/ppermute | solution.py:27
  218.0 24.3 %collective-permute-start.28 = (bf16[1,32,4096]{2,1,0:T(8,128)(2,1)S(1)}, bf16[1,32,4096]{2,1,0:T(8,128)(2,1)S(1)}, u32[]{:S(2)}, u32[]{:S(2)}) collective-permute-start(bf16[1,32,4096]{2,1,0:T(8,128)(2,1)S(1)} %slice.504), channel_id=1, source_target_pairs={{0,8},{4,12},{8,0},{12,4},{1,9},{5,13},{9,1},{13,5},{2,10},{6,14},... | collective-permute-start | bytes 786440 | tf_op jit(solution)/shard_map/ppermute | solution.py:27
  220.2 69.9 %collective-permute-start.25 = (bf16[32,4096]{1,0:T(8,128)(2,1)}, bf16[32,4096]{1,0:T(8,128)(2,1)}, u32[]{:S(2)}, u32[]{:S(2)}) collective-permute-start(bf16[32,4096]{1,0:T(8,128)(2,1)} %get-tuple-element.309), channel_id=1, source_target_pairs={{0,16},{16,0},{1,17},{17,1},{2,18},{18,2},{3,19},{19,3},{4,20},{20... | collective-permute-start | bytes 786440 | tf_op jit(solution)/shard_map/ppermute | solution.py:31
  222.2 39.1 %collective-permute-start.34 = (bf16[2,32,4096]{2,1,0:T(8,128)(2,1)S(1)}, bf16[2,32,4096]{2,1,0:T(8,128)(2,1)S(1)}, u32[]{:S(2)}, u32[]{:S(2)}) collective-permute-start(bf16[2,32,4096]{2,1,0:T(8,128)(2,1)S(1)} %slice.498), channel_id=1, source_target_pairs={{0,4},{4,0},{8,12},{12,8},{1,5},{5,1},{9,13},{13,9},{2,6},{6,2},{1... | collective-permute-start | bytes 1572872 | tf_op jit(solution)/shard_map/ppermute | solution.py:27
  235.4 26.8 %collective-permute-start.33 = (bf16[1,32,4096]{2,1,0:T(8,128)(2,1)S(1)}, bf16[1,32,4096]{2,1,0:T(8,128)(2,1)S(1)}, u32[]{:S(2)}, u32[]{:S(2)}) collective-permute-start(bf16[1,32,4096]{2,1,0:T(8,128)(2,1)S(1)} %slice.503), channel_id=1, source_target_pairs={{0,8},{4,12},{8,0},{12,4},{1,9},{5,13},{9,1},{13,5},{2,10},{6,14},... | collective-permute-start | bytes 786440 | tf_op jit(solution)/shard_map/ppermute | solution.py:27
  235.6 37.0 %collective-permute-start.37 = (bf16[2,32,4096]{2,1,0:T(8,128)(2,1)S(1)}, bf16[2,32,4096]{2,1,0:T(8,128)(2,1)S(1)}, u32[]{:S(2)}, u32[]{:S(2)}) collective-permute-start(bf16[2,32,4096]{2,1,0:T(8,128)(2,1)S(1)} %pad_maximum_fusion.4), channel_id=1, source_target_pairs={{0,4},{4,0},{8,12},{12,8},{1,5},{5,1},{9,13},{13,9},{2,6},{6,2},{1... | collective-permute-start | bytes 1572872 | tf_op jit(solution)/shard_map/ppermute | solution.py:27
  245.2 30.2 %collective-permute-start.39 = (bf16[1,32,4096]{2,1,0:T(8,128)(2,1)S(1)}, bf16[1,32,4096]{2,1,0:T(8,128)(2,1)S(1)}, u32[]{:S(2)}, u32[]{:S(2)}) collective-permute-start(bf16[1,32,4096]{2,1,0:T(8,128)(2,1)S(1)} %bitcast.263), channel_id=1, source_target_pairs={{0,8},{4,12},{8,0},{12,4},{1,9},{5,13},{9,1},{13,5},{2,10},{6,14},... | collective-permute-start | bytes 786440 | tf_op jit(solution)/shard_map/ppermute | solution.py:27
  277.7 27.3 %collective-permute-start.41 = (bf16[2,32,4096]{2,1,0:T(8,128)(2,1)}, bf16[2,32,4096]{2,1,0:T(8,128)(2,1)}, u32[]{:S(2)}, u32[]{:S(2)}) collective-permute-start(bf16[2,32,4096]{2,1,0:T(8,128)(2,1)} %pad_maximum_fusion.5), channel_id=1, source_target_pairs={{0,4},{4,0},{8,12},{12,8},{1,5},{5,1},{9,13},{13,9},{2,6},{6,2},{1... | collective-permute-start | bytes 1572872 | tf_op jit(solution)/shard_map/ppermute | solution.py:27
  317.2 25.2 %collective-permute-start.51 = (bf16[2,32,4096]{2,1,0:T(8,128)(2,1)}, bf16[2,32,4096]{2,1,0:T(8,128)(2,1)}, u32[]{:S(2)}, u32[]{:S(2)}) collective-permute-start(bf16[2,32,4096]{2,1,0:T(8,128)(2,1)} %pad_maximum_fusion.6), channel_id=1, source_target_pairs={{0,4},{4,0},{8,12},{12,8},{1,5},{5,1},{9,13},{13,9},{2,6},{6,2},{1... | collective-permute-start | bytes 1572872 | tf_op jit(solution)/shard_map/ppermute | solution.py:27
  340.0 25.9 %collective-permute-start.50 = (bf16[2,32,4096]{2,1,0:T(8,128)(2,1)S(1)}, bf16[2,32,4096]{2,1,0:T(8,128)(2,1)S(1)}, u32[]{:S(2)}, u32[]{:S(2)}) collective-permute-start(bf16[2,32,4096]{2,1,0:T(8,128)(2,1)S(1)} %pad_maximum_fusion.7), channel_id=1, source_target_pairs={{0,4},{4,0},{8,12},{12,8},{1,5},{5,1},{9,13},{13,9},{2,6},{6,2},{1... | collective-permute-start | bytes 1572872 | tf_op jit(solution)/shard_map/ppermute | solution.py:27
  365.6 59.8 %collective-permute-start.61 = (bf16[32,9216]{1,0:T(8,128)(2,1)}, bf16[32,9216]{1,0:T(8,128)(2,1)}, u32[]{:S(2)}, u32[]{:S(2)}) collective-permute-start(bf16[32,9216]{1,0:T(8,128)(2,1)} %get-tuple-element.221), channel_id=1, source_target_pairs={{0,16},{16,0},{1,17},{17,1},{2,18},{18,2},{3,19},{19,3},{4,20},{20... | collective-permute-start | bytes 1769480 | tf_op jit(solution)/shard_map/ppermute | solution.py:31
  367.0 33.3 %collective-permute-start.57 = (bf16[4,32,4096]{2,1,0:T(8,128)(2,1)S(1)}, bf16[4,32,4096]{2,1,0:T(8,128)(2,1)}, u32[]{:S(2)}, u32[]{:S(2)}) collective-permute-start(bf16[4,32,4096]{2,1,0:T(8,128)(2,1)S(1)} %pad_maximum_fusion.3.own_ref), channel_id=1, source_target_pairs={{0,1},{1,0},{2,3},{3,2},{4,5},{5,4},{6,7},{7,6},{8,9},{9,8},{10,11... | collective-permute-start | bytes 3145736 | tf_op jit(solution)/shard_map/ppermute | solution.py:18
  412.3 42.4 %collective-permute-start.67 = (bf16[32,9216]{1,0:T(8,128)(2,1)}, bf16[32,9216]{1,0:T(8,128)(2,1)S(1)}, u32[]{:S(2)}, u32[]{:S(2)}) collective-permute-start(bf16[32,9216]{1,0:T(8,128)(2,1)} %get-tuple-element.238), channel_id=1, source_target_pairs={{0,16},{16,0},{1,17},{17,1},{2,18},{18,2},{3,19},{19,3},{4,20},{20... | collective-permute-start | bytes 1769480 | tf_op jit(solution)/shard_map/ppermute | solution.py:31
  425.2 193.2 %collective-permute-start.83 = (bf16[576,4096]{1,0:T(8,128)(2,1)}, bf16[576,4096]{1,0:T(8,128)(2,1)}, u32[]{:S(2)}, u32[]{:S(2)}) collective-permute-start(bf16[576,4096]{1,0:T(8,128)(2,1)} %convolution_convert_fusion), channel_id=1, source_target_pairs={{0,2},{2,0},{1,3},{3,1},{4,6},{6,4},{5,7},{7,5},{8,10},{10,8},{9,1... | collective-permute-start | bytes 14155784 | tf_op jit(solution)/shard_map/ppermute | solution.py:22
  425.5 24.4 %collective-permute-start.63 = (bf16[2,32,1152]{2,1,0:T(8,128)(2,1)}, bf16[2,32,1152]{2,1,0:T(8,128)(2,1)}, u32[]{:S(2)}, u32[]{:S(2)}) collective-permute-start(bf16[2,32,1152]{2,1,0:T(8,128)(2,1)} %get-tuple-element.244), channel_id=1, source_target_pairs={{0,8},{4,12},{8,0},{12,4},{1,9},{5,13},{9,1},{13,5},{2,10},{6,14},... | collective-permute-start | bytes 442376 | tf_op jit(solution)/shard_map/ppermute | solution.py:27
  429.3 21.4 %collective-permute-start.64 = (bf16[2,32,1152]{2,1,0:T(8,128)(2,1)}, bf16[2,32,1152]{2,1,0:T(8,128)(2,1)}, u32[]{:S(2)}, u32[]{:S(2)}) collective-permute-start(bf16[2,32,1152]{2,1,0:T(8,128)(2,1)} %get-tuple-element.245), channel_id=1, source_target_pairs={{0,4},{4,0},{8,12},{12,8},{1,5},{5,1},{9,13},{13,9},{2,6},{6,2},{1... | collective-permute-start | bytes 442376 | tf_op jit(solution)/shard_map/ppermute | solution.py:27
  429.3 22.3 %collective-permute-start.65 = (bf16[2,32,1152]{2,1,0:T(8,128)(2,1)}, bf16[2,32,1152]{2,1,0:T(8,128)(2,1)}, u32[]{:S(2)}, u32[]{:S(2)}) collective-permute-start(bf16[2,32,1152]{2,1,0:T(8,128)(2,1)} %get-tuple-element.246), channel_id=1, source_target_pairs={{0,12},{4,8},{8,4},{12,0},{1,13},{5,9},{9,5},{13,1},{2,14},{6,10},... | collective-permute-start | bytes 442376 | tf_op jit(solution)/shard_map/ppermute | solution.py:27
  511.4 31.9 %collective-permute-start.79 = (f32[1,13056]{1,0:T(1,128)S(1)}, f32[1,13056]{1,0:T(1,128)S(1)}, u32[]{:S(2)}, u32[]{:S(2)}) collective-permute-start(f32[1,13056]{1,0:T(1,128)S(1)} %broadcast_in_dim.25), channel_id=1, source_target_pairs={{0,1},{1,0},{2,3},{3,2},{4,5},{5,4},{6,7},{7,6},{8,9},{9,8},{10,11... | collective-permute-start | bytes 156680 | tf_op jit(solution)/shard_map/ppermute | solution.py:18
  543.3 28.9 %collective-permute-start.80 = (f32[1,13056]{1,0:T(1,128)S(1)}, f32[1,13056]{1,0:T(1,128)S(1)}, u32[]{:S(2)}, u32[]{:S(2)}) collective-permute-start(f32[1,13056]{1,0:T(1,128)S(1)} %reshape_add_fusion), channel_id=1, source_target_pairs={{0,2},{2,0},{1,3},{3,1},{4,6},{6,4},{5,7},{7,5},{8,10},{10,8},{9,1... | collective-permute-start | bytes 156680 | tf_op jit(solution)/shard_map/ppermute | solution.py:22
  (173 other events, 2175.3 us)
Sparse Core Ops, SparseCore 0:
  9.6 120.0 all-gather.2

commit v3 on v2

--- a/solution.py
+++ b/solution.py
@@ -7,7 +7,7 @@
 from jax.experimental.pallas import tpu as pltpu
 from jax.sharding import PartitionSpec as P
 
-PLAN = "01020130120321301223013201320103211030212130232W132303123W"
+PLAN = "0102010213012301320130210321301230210231S021302123W2313W32S3"
 BF16 = jnp.bfloat16
 F32 = jnp.float32
 CONV_DIMS = ("NHWC", "HWIO", "NHWC")
@@ -153,9 +153,8 @@
     for p, out_ref in enumerate(out_refs):
         lanes = pl.ds(pl.multiple_of(target_ref[p] * reach, 128), reach)
         mixed = self_ref[...] * pooled_ref[:, lanes].astype(F32) + cross_ref[...] * partner_ref[:, lanes].astype(F32)
-        piece = [mixed[:, i * block : (i + 1) * block] for i in range(4)]
-        first = jnp.concatenate([piece[0], piece[2]], axis=1)
-        second = jnp.concatenate([piece[1], piece[3]], axis=1)
+        first = mixed[:, : 2 * block]
+        second = mixed[:, 2 * block :]
         out_ref[0] = jnp.where(is_zero, first, second).astype(out_ref.dtype)
         out_ref[1] = jnp.where(is_zero, second, first).astype(out_ref.dtype)
 
@@ -170,7 +169,7 @@
             jnp.tile(self_pool, flat // width) * pooled.astype(F32)
             + jnp.tile(cross_pool, flat // width) * partner_pool.astype(F32)
         ).astype(BF16)
-        mixed = mixed.reshape(slots, count, 2, 2, block).transpose(1, 3, 0, 2, 4).reshape(count, 2, slots, 2 * block)
+        mixed = mixed.reshape(slots, count, 2, 2, block).transpose(1, 2, 0, 3, 4).reshape(count, 2, slots, 2 * block)
         mixed = jnp.where(core == 0, mixed, mixed[:, ::-1])
         return [pick(mixed, target[p]) for p in range(count)]
     repeat = 4 * block // self_pool.shape[0]
@@ -198,7 +197,7 @@
         lanes = pl.ds(pl.multiple_of(target_ref[p] * reach, 128), reach)
         here, there = here_refs[p][0].astype(F32), far_ref[p].astype(F32)
         zero, one = jnp.where(is_zero, here, there), jnp.where(is_zero, there, here)
-        grad = jnp.concatenate([zero[:, :block], one[:, :block], zero[:, block:], one[:, block:]], axis=1)
+        grad = jnp.concatenate([zero, one], axis=1)
         grad_ref[:, lanes] = grad.astype(grad_ref.dtype)
         sent_ref[:, lanes] = (cross_ref[...] * grad).astype(sent_ref.dtype)
         own_sum = own_sum + jnp.sum(pooled_ref[:, lanes].astype(F32) * grad, axis=0, keepdims=True)
@@ -218,7 +217,7 @@
         pieces = jnp.stack([jnp.stack([here[p][0], far[p]]) for p in range(count)])
         pieces = jnp.where(core == 0, pieces, pieces[:, ::-1]).reshape(count, 2, slots, 2, block)
         inverse = jnp.argsort(target)
-        grad = jnp.take(pieces, inverse, axis=0).transpose(2, 0, 3, 1, 4).reshape(slots, flat)
+        grad = jnp.take(pieces, inverse, axis=0).transpose(2, 0, 1, 3, 4).reshape(slots, flat)
         wide = grad.astype(F32)
         sent = (jnp.tile(cross_pool, flat // width) * wide).astype(BF16)
         sums = [
@@ -291,13 +290,20 @@
 
 
 def fc_back_kernel(count, w_ref, own_ref, came_ref, *refs):
-    slots = own_ref.shape[1]
-    turned = (((1,), (1,)), ((), ()))
-    for side, grads in enumerate((own_ref, came_ref)):
-        rows = grads[...].reshape(count * slots, grads.shape[2])
-        total = lax.dot_general(rows, w_ref[...], turned, preferred_element_type=F32)
-        for p in range(count):
-            refs[p][side] = total[p * slots : (p + 1) * slots].astype(refs[p].dtype)
+    out_refs, grads_ref = refs[:count], refs[count]
+    slots, units = own_ref.shape[1:]
+    half = count * slots
+
+    @pl.when(pl.program_id(0) == 0)
+    def _():
+        grads_ref[:half] = own_ref[...].reshape(half, units)
+        grads_ref[half:] = came_ref[...].reshape(half, units)
+
+    total = lax.dot_general(grads_ref[...], w_ref[...], (((1,), (1,)), ((), ())), preferred_element_type=F32)
+    for p, out_ref in enumerate(out_refs):
+        for side in range(2):
+            first = side * half + p * slots
+            out_ref[side] = total[first : first + slots].astype(out_ref.dtype)
 
 
 def fc_backward(own, came, weight):
@@ -316,18 +322,90 @@
         in_specs=[pl.BlockSpec((tile, units), lambda t: (t, 0)), grads, grads],
         out_specs=[pl.BlockSpec((2, slots, tile), lambda t: (0, 0, t))] * count,
         out_shape=[jax.ShapeDtypeStruct((2, slots, depth), BF16)] * count,
+        scratch_shapes=[pltpu.VMEM((2 * count * slots, units), BF16)],
         compiler_params=pltpu.CompilerParams(vmem_limit_bytes=VMEM_LIMIT),
         cost_estimate=pl.CostEstimate(flops=0, bytes_accessed=0, transcendentals=0),
         name="fc_backward",
     )(weight, own, came)
+
+
+def halve_kernel(kept_ref, came_ref, out_ref, sent_ref):
+    total = kept_ref[...] + came_ref[...].astype(F32)
+    half = out_ref.shape[0]
+    out_ref[...] = total[:half]
+    sent_ref[...] = total[half:].astype(sent_ref.dtype)
+
+
+def halve(kept, came):
+    count, slots, units = kept.shape
+    half = count // 2
+    if count > 4:
+        total = kept + came.astype(F32)
+        return total[:half], total[half:].astype(BF16)
+    tile = units // 4
+    return pl.pallas_call(
+        halve_kernel,
+        grid=(4,),
+        in_specs=[pl.BlockSpec((count, slots, tile), lambda t: (0, 0, t))] * 2,
+        out_specs=[pl.BlockSpec((half, slots, tile), lambda t: (0, 0, t))] * 2,
+        out_shape=[
+            jax.ShapeDtypeStruct((half, slots, units), F32),
+            jax.ShapeDtypeStruct((half, slots, units), BF16),
+        ],
+        compiler_params=pltpu.CompilerParams(vmem_limit_bytes=VMEM_LIMIT),
+        cost_estimate=pl.CostEstimate(flops=0, bytes_accessed=0, transcendentals=0),
+        name="halve",
+    )(kept, came)
+
+
+def hidden_kernel(kept_ref, came_ref, bias_ref, self_ref, cot_ref, scale_ref, back_ref, hidden_ref, grad_ref, sum_ref):
+    pre = kept_ref[0] + came_ref[0].astype(F32) + bias_ref[...]
+    hidden, slope = gelu_parts(pre)
+    hidden_ref[...] = hidden.astype(hidden_ref.dtype)
+    grad_out = cot_ref[...].astype(F32) * scale_ref[...]
+    grad = ((self_ref[...] * grad_out + back_ref[...].astype(F32)) * slope).astype(grad_ref.dtype)
+    grad_ref[0] = grad
+    sum_ref[...] = jnp.sum(grad.astype(F32), axis=0, keepdims=True)
+
+
+def hidden_step(n, kept, came, bias, self_fc, cotangent, scaling, back_fc):
+    _, slots, units = kept.shape
+    tile = units // 4
+    one = pl.BlockSpec((1, tile), lambda t: (0, t))
+    block = pl.BlockSpec((1, slots, tile), lambda t: (0, 0, t))
+    rows = pl.BlockSpec((slots, tile), lambda t: (n, t))
+    return pl.pallas_call(
+        hidden_kernel,
+        grid=(4,),
+        in_specs=[block, block, one, one, rows, pl.BlockSpec((slots, 1), lambda t: (n, 0)), rows],
+        out_specs=[pl.BlockSpec((slots, tile), lambda t: (0, t)), block, one],
+        out_shape=[
+            jax.ShapeDtypeStruct((slots, units), BF16),
+            jax.ShapeDtypeStruct((1, slots, units), BF16),
+            jax.ShapeDtypeStruct((1, units), F32),
+        ],
+        compiler_params=pltpu.CompilerParams(vmem_limit_bytes=VMEM_LIMIT),
+        cost_estimate=pl.CostEstimate(flops=0, bytes_accessed=0, transcendentals=0),
+        name="hidden",
+    )(kept, came, bias[None], self_fc[None], cotangent, scaling[:, None], back_fc)
+
+
+def unwritten(shape, dtype):
+    return pl.pallas_call(
+        lambda ref: None,
+        out_specs=pl.BlockSpec(memory_space=pl.ANY),
+        out_shape=jax.ShapeDtypeStruct(shape, dtype),
+        cost_estimate=pl.CostEstimate(flops=0, bytes_accessed=0, transcendentals=0),
+        name="unwritten",
+    )()
 
 
 def gelu_parts(v):
     root = 0.7978845608028654
     cubic = 0.044715
-    tanh = jnp.tanh(root * (v + cubic * (v * v * v)))
-    half = 0.5 * (1.0 + tanh)
-    slope = half + 0.5 * v * (1.0 - tanh * tanh) * (root * (1.0 + 3.0 * cubic * (v * v)))
+    square = v * v
+    half = 0.5 + 0.5 * jnp.tanh(v * (root + (root * cubic) * square))
+    slope = half + (half * (1.0 - half)) * (v * (2.0 * root + (6.0 * root * cubic) * square))
     return v * half, slope
 
 
@@ -366,7 +444,7 @@
 
 def sum_kernel(rows, outer, mid, core):
     outer_count = lax.axis_size("outer")
-    for swap, side in ((swap_core, core), (swap_mid, mid)):
+    for swap, side in ((swap_mid, mid), (swap_core, core)):
         halves = rows.reshape(2, -1, rows.shape[1])
         got = swap(pick(halves, 1 - side).astype(BF16))
         rows = pick(halves, side) + got.astype(F32)
@@ -377,7 +455,7 @@
     total = total.astype(BF16)
     stack = jnp.stack([total] + [swap_outer(total, k) for k in range(1, outer_count)])
     rows = jnp.concatenate([pick(stack, outer ^ k) for k in range(outer_count)])
-    for swap, side in ((swap_mid, mid), (swap_core, core)):
+    for swap, side in ((swap_core, core), (swap_mid, mid)):
         got = swap(rows)
         rows = jnp.where(side == 0, jnp.concatenate([rows, got]), jnp.concatenate([got, rows]))
     return rows.astype(F32)
@@ -431,9 +509,11 @@
     def after(array):
         return lax.optimization_barrier((array, last[0]))[0]
 
-    sums = dict(fc_bias=0.0, hidden_self=0.0, hidden_cross=0.0, pool=0.0, conv_bias=0.0, kernel=0.0)
+    sums = dict(fc_bias=0.0, pool=0.0, conv_bias=0.0, kernel=0.0)
     stage = {}
-    outputs, grads_in = {}, {}
+    hiddens = {}
+    count, extent, _, depth = inputs.shape
+    stage["grad_in"] = jnp.transpose(unwritten((extent, extent, count, depth), BF16), (2, 0, 1, 3))
     lead = (((0,), (0,)), ((), ()))
 
     def chunk(n):
@@ -459,25 +539,17 @@
         came = swap_core(sent)
         yield
         for hop in range(hops):
-            chip = chip + after(came).astype(F32)
-            half = chip.shape[0] // 2
-            sent = chip[half:].astype(BF16)
-            chip = chip[:half]
+            chip, sent = halve(chip, after(came))
             last[0] = sent
             came = swap_outer(sent, 1 << hop)
             yield
-        pre_fc = chip[0] + after(came)[0].astype(F32) + fc_bias[0]
-        hidden, slope_fc = gelu_parts(pre_fc)
-        hidden = hidden.astype(BF16)
-        grad_out = cotangent[0][rows].astype(F32) * scaling[rows, None]
-        grad_pre_fc = ((self_fc * grad_out + back_fc[rows].astype(F32)) * slope_fc).astype(BF16)
-        sums["fc_bias"] += jnp.sum(grad_pre_fc.astype(F32), axis=0)
-        last[0] = grad_pre_fc
-        gathered = grad_pre_fc[None]
+        hiddens[n], gathered, bias_sum = hidden_step(
+            n, chip, after(came), fc_bias[0], self_fc, cotangent[0], scaling, back_fc
+        )
+        sums["fc_bias"] += bias_sum[0]
+        last[0] = gathered
         for hop in reversed(range(hops)):
             came = swap_outer(gathered, 1 << hop)
-            if hop == hops - 1:
-                partner_hidden = swap_tower(hidden)
             yield
             gathered = jnp.concatenate([gathered, after(came)])
             last[0] = gathered
@@ -510,12 +582,21 @@
         sums["kernel"] += grad_kernel
         last[0] = grad_kernel
         yield
-        grads_in[n] = conv_grad_inputs(after(grad_pre), kernel)
-        last[0] = grads_in[n]
-        stitched = self_fc * hidden.astype(F32) + cross_fc * partner_hidden.astype(F32)
-        outputs[n] = (stitched * live_slots[rows, None]).astype(BF16)
-        sums["hidden_self"] += jnp.sum(hidden.astype(F32) * grad_out, axis=0)
-        sums["hidden_cross"] += jnp.sum(partner_hidden.astype(F32) * grad_out, axis=0)
+        part = conv_grad_inputs(after(grad_pre), kernel)
+        stage["grad_in"] = lax.dynamic_update_slice(stage["grad_in"], part, (starts[n], 0, 0, 0))
+        last[0] = stage["grad_in"]
+
+    def stitch():
+        hidden = after(jnp.concatenate([hiddens[n] for n in range(len(sizes))]))
+        last[0] = hidden
+        partner_hidden = swap_tower(hidden)
+        yield
+        partner_hidden = after(partner_hidden).astype(F32)
+        hidden = hidden.astype(F32)
+        stage["output"] = ((self_fc * hidden + cross_fc * partner_hidden) * live_slots[:, None]).astype(BF16)
+        grad_out = cotangent[0].astype(F32) * scaling[:, None]
+        stage["hidden"] = jnp.sum(hidden * grad_out, axis=0), jnp.sum(partner_hidden * grad_out, axis=0)
+        last[0] = stage["output"]
 
     def fc_weight_gradient():
         columns = jnp.concatenate([stage[n][0] for n in range(len(sizes))])
@@ -530,16 +611,14 @@
         stage["gradient"] = lax.dot_general(own, grads, lead, preferred_element_type=F32) + came.astype(F32)
         last[0] = stage["gradient"]
 
-    running = [chunk(n) for n in range(len(sizes))]
-    weight_run = fc_weight_gradient()
-    for n in PLAN if len(sizes) > 1 else "0" * (2 * hops + 6) + "W" + "0" * 5 + "W":
-        next(weight_run if n == "W" else running[int(n)], None)
-    outputs = [outputs[n] for n in range(len(sizes))]
-    grads_in = [grads_in[n] for n in range(len(sizes))]
+    runs = {str(n): chunk(n) for n in range(len(sizes))}
+    runs.update(W=fc_weight_gradient(), S=stitch())
+    for n in PLAN if len(sizes) > 1 else "0" * (2 * hops + 6) + "WS" + "0" * 5 + "WS":
+        next(runs[n], None)
     grad_fc_weight = stage["gradient"]
     kernel_sum = sums["kernel"]
     conv_bias_sum, fc_bias_sum = sums["conv_bias"], sums["fc_bias"]
-    hidden_self, hidden_cross = sums["hidden_self"], sums["hidden_cross"]
+    hidden_self, hidden_cross = stage["hidden"]
     pool_self, pool_cross = sums["pool"]
 
     small = sum_small(
@@ -555,8 +634,8 @@
     )
     summed_kernel = sum_kernel(kernel_sum.reshape(-1, width), outer, mid, core).reshape(kernel.shape)
     return (
-        jnp.concatenate(outputs)[None],
-        jnp.concatenate(grads_in)[None],
+        stage["output"][None],
+        stage["grad_in"][None],
         summed_kernel[None],
         conv_bias_sum[None],
         grad_fc_weight[None],
@@ -567,8 +646,8 @@
 
 
 def solution(mesh):
-    mesh = jax.sharding.Mesh(mesh.devices.reshape(mesh.shape["tower"], -1, 2, 2), ("tower", "outer", "mid", "core"))
-    crops = ("outer", "mid", "core")
+    mesh = jax.sharding.Mesh(mesh.devices.reshape(mesh.shape["tower"], -1, 2, 2), ("tower", "outer", "core", "mid"))
+    crops = ("outer", "core", "mid")
     placed = (
         P("tower", crops, None, None, None),
         P("tower", None, None, None, None),

time: 647 us -> 622 us (0.961)
  other arithmetic: 63.9 us -> 17.8 us
  starting transfers between devices: 91.7 us -> 113 us
  waiting for transfers between devices: 118 us -> 101 us
  Pallas kernels: 90.1 us -> 99.9 us
  local copies, waits for them, and re-layouts: 44.3 us -> 50.9 us
    all_gather x1, waiting for transfers between devices: 22 us -> 0.01 us  [body(): weight = lax.all_gather(fc_weight[0], 'mid', axis=0, tiled=True)]
    ppermute x4, starting transfers between devices: 3.35 us -> 22.2 us  [swap_mid(): return lax.ppermute(block, 'mid', [(0, 1), (1, 0)])]
    pallas_call x0 -> x13, Pallas kernels: none -> 17.3 us  [the longest x4 9.16 us: hidden_step(): pl.pallas_call(hidden_kernel, grid=(4,), in_specs=[block, block, one, one...]
    broadcast_in_dim x2 -> x0, other arithmetic: 16 us -> none  [the longest x1 15 us: body(): jnp.concatenate(grads_in)[None]]
    ppermute x19, waiting for transfers between devices: 0.05 us -> 14.9 us  [swap_core(): return lax.ppermute(block, 'core', [(0, 1), (1, 0)])]
    ppermute x48, starting transfers between devices: 53.9 us -> 68 us  [swap_outer(): return lax.ppermute(block, 'outer', [(i, i ^ mask) for i in range(count)])]
    reduce_sum x5 -> x1, other arithmetic: 15.1 us -> 3.53 us  [stitch(): jnp.sum(partner_hidden * grad_out, axis=0)]
    ppermute x19, starting transfers between devices: 23.5 us -> 14.5 us  [swap_core(): return lax.ppermute(block, 'core', [(0, 1), (1, 0)])]
  transfers between devices with their start and end apart: 85 -> 82, of which waited for: 20 -> 23; matrix products, arithmetic and copies ran while one was open for 46% -> 42% of each run, Pallas kernels for 14% -> 16%
where the time goes in v3:
time: 622 us; the launch traced here: 611 us
  matrix products  211 us (34%)
  starting transfers between devices  113 us (18%)
  waiting for transfers between devices  101 us (16%)
  Pallas kernels  99.9 us (16%)
  local copies, waits for them, and re-layouts  50.9 us (8%)
  other arithmetic  17.8 us (3%)
  between operations  16.1 us (3%)
    ppermute x48, waiting for transfers between devices, swap_outer(): return lax.ppermute(block, 'outer', [(i, i ^ mask) for i in range(count)])  80.2 us
    conv_general_dilated x4, matrix products, conv_forward(): lax.conv_general_dilated(inputs, kernel, (1, 1), ((1, 1), (1, 1)), dimens...  72.6 us
    ppermute x48, starting transfers between devices, swap_outer(): return lax.ppermute(block, 'outer', [(i, i ^ mask) for i in range(count)])  68 us
    conv_general_dilated x4, matrix products, conv_grad_inputs(): lax.conv_general_dilated(grad_pre, turned, (1, 1), ((1, 1), (1, 1)), dime...  62.4 us
    conv_general_dilated x4, matrix products, conv_grad_kernel(): lax.conv_general_dilated(inputs, grad_pre, (1, 1), ((1, 1), (1, 1)), dime...  56.9 us
    unnamed x193, local copies, waits for them, and re-layouts  34.4 us
    pallas_call x4, Pallas kernels, fc_backward(): pl.pallas_call(functools.partial(fc_back_kernel, count), grid=(depth // t...  27.7 us
    pallas_call x4, Pallas kernels, fc_forward(): pl.pallas_call(functools.partial(fc_forward_kernel, count), grid=(units /...  26.3 us
  transfers between devices with their start and end apart: 82, of which 23 were waited for; matrix products, arithmetic and copies ran while one was open for 42% of the time, Pallas kernels for 16%

profile of v3, /device:TPU:1, one launch (start us, length us, event | category | flops | bytes accessed | tf_op | source)
XLA Modules:
  0.0 610.5 jit_solution(17370808504413426403)
XLA Ops:
  8.7 18.3 %fusion.3 = (bf16[13,13,32,256]{3,2,1,0:T(8,128)(2,1)}, bf16[13,13,32,256]{3,2,1,0:T(8,128)(2,1)S(1)}) fusion(f32[256]{0:T(256)S(1)} %bitcast.226, bf16[1,3,3,384,256]{4,3,2,1,0:T(8,128)(2,1)S(1)} %copy-done, bf16[1,128,13,13,384]{4,1,3,2,0:T(8,128)(2,1)} %param.12), kind=kOutput, calls=%fused_computation.9 | convolution fusion | flops 8639307776 | bytes 11461632 | tf_op jit(solution)/shard_map/conv_general_dilated | solution.py:413
  30.0 18.1 %fusion.7 = (bf16[13,13,32,256]{3,2,1,0:T(8,128)(2,1)}, bf16[13,13,32,256]{3,2,1,0:T(8,128)(2,1)S(1)}) fusion(f32[256]{0:T(256)S(1)} %bitcast.227, bf16[1,3,3,384,256]{4,3,2,1,0:T(8,128)(2,1)S(1)} %copy-done, bf16[1,128,13,13,384]{4,1,3,2,0:T(8,128)(2,1)} %param.12), kind=kOutput, calls=%fused_computation.13 | convolution fusion | flops 8639307776 | bytes 11461632 | tf_op jit(solution)/shard_map/conv_general_dilated | solution.py:413
  56.0 18.1 %fusion.11 = (bf16[13,13,32,256]{3,2,1,0:T(8,128)(2,1)}, bf16[13,13,32,256]{3,2,1,0:T(8,128)(2,1)S(1)}) fusion(f32[256]{0:T(256)S(1)} %bitcast.228, bf16[1,3,3,384,256]{4,3,2,1,0:T(8,128)(2,1)S(1)} %copy-done, bf16[1,128,13,13,384]{4,1,3,2,0:T(8,128)(2,1)} %param.12), kind=kOutput, calls=%fused_computation.17 | convolution fusion | flops 8639307776 | bytes 11461632 | tf_op jit(solution)/shard_map/conv_general_dilated | solution.py:413
  88.8 6.1 collective-permute-done.8.refs_1_
  101.6 6.3 %fc_forward.4 = (f32[4,32,4096]{2,1,0:T(8,128)S(1)}, bf16[4,32,4096]{2,1,0:T(8,128)(2,1)S(1)}, bf16[256,1152]{1,0:T(8,128)(2,1)S(1)}) custom-call(bf16[1152,4096]{1,0:T(8,128)(2,1)} %bitcast.194, bf16[4,32,1152]{2,1,0:T(8,128)(2,1)S(1)} %copy-done.54, bf16[2,32,1152]{2,1,0:T(8,128)(2,1)S(1)} %copy-done.46, bf16[2,32,1152]{2,1,0:T(8,128)(2,1)S(1)} %copy-done.52, ...), custom_call_target="tpu_custom_call" | custom-call | tf_op jit(solution)/shard_map/fc_forward/pallas_call | solution.py:272
  111.4 18.1 %fusion.15 = (bf16[13,13,32,256]{3,2,1,0:T(8,128)(2,1)}, bf16[13,13,32,256]{3,2,1,0:T(8,128)(2,1)S(1)}) fusion(f32[256]{0:T(256)S(1)} %bitcast.229, bf16[1,3,3,384,256]{4,3,2,1,0:T(8,128)(2,1)S(1)} %copy-done, bf16[1,128,13,13,384]{4,1,3,2,0:T(8,128)(2,1)} %param.12), kind=kOutput, calls=%fused_computation.21 | convolution fusion | flops 8639307776 | bytes 11461632 | tf_op jit(solution)/shard_map/conv_general_dilated | solution.py:413
  142.9 7.2 %fc_forward.5 = (f32[4,32,4096]{2,1,0:T(8,128)S(1)}, bf16[4,32,4096]{2,1,0:T(8,128)(2,1)}, bf16[256,1152]{1,0:T(8,128)(2,1)S(1)}) custom-call(bf16[1152,4096]{1,0:T(8,128)(2,1)} %bitcast.195, bf16[4,32,1152]{2,1,0:T(8,128)(2,1)S(1)} %collective-permute-done.12.got_ref, bf16[2,32,1152]{2,1,0:T(8,128)(2,1)S(1)} %copy-done.38, ...), custom_call_target="tpu_custom_call" | custom-call | tf_op jit(solution)/shard_map/fc_forward/pallas_call | solution.py:272
  181.1 6.5 %fc_forward.6 = (f32[4,32,4096]{2,1,0:T(8,128)S(1)}, bf16[4,32,4096]{2,1,0:T(8,128)(2,1)S(1)}, bf16[256,1152]{1,0:T(8,128)(2,1)S(1)}) custom-call(bf16[1152,4096]{1,0:T(8,128)(2,1)} %bitcast.196, bf16[4,32,1152]{2,1,0:T(8,128)(2,1)S(1)} %collective-permute-done.18.got_ref, bf16[2,32,1152]{2,1,0:T(8,128)(2,1)S(1)} %copy-done.36, ...), custom_call_target="tpu_custom_call" | custom-call | tf_op jit(solution)/shard_map/fc_forward/pallas_call | solution.py:272
  197.9 6.3 %fc_forward.7 = (f32[4,32,4096]{2,1,0:T(8,128)S(1)}, bf16[4,32,4096]{2,1,0:T(8,128)(2,1)S(1)}, bf16[256,1152]{1,0:T(8,128)(2,1)S(1)}) custom-call(bf16[1152,4096]{1,0:T(8,128)(2,1)} %bitcast.197, bf16[4,32,1152]{2,1,0:T(8,128)(2,1)S(1)} %collective-permute-done.28.got_ref, bf16[2,32,1152]{2,1,0:T(8,128)(2,1)S(1)} %get-tuple-element.212.refs_0_, ...), custom_call_target="tpu_custom_call" | custom-call | tf_op jit(solution)/shard_map/fc_forward/pallas_call | solution.py:272
  216.1 10.5 %collective-permute-done.31 = bf16[2,32,4096]{2,1,0:T(8,128)(2,1)S(1)} collective-permute-done((bf16[2,32,4096]{2,1,0:T(8,128)(2,1)}, bf16[2,32,4096]{2,1,0:T(8,128)(2,1)S(1)}, u32[]{:S(2)}, u32[]{:S(2)}) %collective-permute-start.31) | collective-permute-done | bytes 524320 | tf_op jit(solution)/shard_map/ppermute | solution.py:27
  233.9 6.8 %collective-permute-done.29.came_ref = bf16[2,32,4096]{2,1,0:T(8,128)(2,1)S(1)} collective-permute-done((bf16[2,32,4096]{2,1,0:T(8,128)(2,1)S(1)}, bf16[2,32,4096]{2,1,0:T(8,128)(2,1)S(1)}, u32[]{:S(2)}, u32[]{:S(2)}) %collective-permute-start.29) | collective-permute-done | bytes 524320 | tf_op jit(solution)/shard_map/ppermute | solution.py:27
  253.9 6.5 %fc_backward.4 = (bf16[2,32,1152]{2,1,0:T(8,128)(2,1)S(1)}, bf16[2,32,1152]{2,1,0:T(8,128)(2,1)S(1)}, bf16[2,32,1152]{2,1,0:T(8,128)(2,1)S(1)}, bf16[2,32,1152]{2,1,0:T(8,128)(2,1)S(1)}) custom-call(bf16[1152,4096]{1,0:T(8,128)(2,1)} %bitcast.198, bf16[4,32,4096]{2,1,0:T(8,128)(2,1)S(1)} %constant_dynamic-update-slice_fusion.2.own_ref, ...), custom_call_target="tpu_custom_call" | custom-call | tf_op jit(solution)/shard_map/fc_backward/pallas_call | solution.py:319
  260.4 7.5 %collective-permute-done.34 = bf16[2,32,4096]{2,1,0:T(8,128)(2,1)S(1)} collective-permute-done((bf16[2,32,4096]{2,1,0:T(8,128)(2,1)S(1)}, bf16[2,32,4096]{2,1,0:T(8,128)(2,1)S(1)}, u32[]{:S(2)}, u32[]{:S(2)}) %collective-permute-start.34) | collective-permute-done | bytes 524320 | tf_op jit(solution)/shard_map/ppermute | solution.py:27
  282.0 16.9 %collective-permute-done.40.refs_1_ = bf16[2,32,1152]{2,1,0:T(8,128)(2,1)S(1)} collective-permute-done((bf16[2,32,1152]{2,1,0:T(8,128)(2,1)S(1)}, bf16[2,32,1152]{2,1,0:T(8,128)(2,1)S(1)}, u32[]{:S(2)}, u32[]{:S(2)}) %collective-permute-start.40) | collective-permute-done | bytes 147488 | tf_op jit(solution)/shard_map/ppermute | solution.py:27
  307.4 6.6 %fc_backward.5 = (bf16[2,32,1152]{2,1,0:T(8,128)(2,1)S(1)}, bf16[2,32,1152]{2,1,0:T(8,128)(2,1)S(1)}, bf16[2,32,1152]{2,1,0:T(8,128)(2,1)S(1)}, bf16[2,32,1152]{2,1,0:T(8,128)(2,1)S(1)}) custom-call(bf16[1152,4096]{1,0:T(8,128)(2,1)} %bitcast.199, bf16[4,32,4096]{2,1,0:T(8,128)(2,1)S(1)} %constant_dynamic-update-slice_fusion.7.own_ref, ...), custom_call_target="tpu_custom_call" | custom-call | tf_op jit(solution)/shard_map/fc_backward/pallas_call | solution.py:319
  315.7 7.4 %collective-permute-start.47 = (bf16[2,32,1152]{2,1,0:T(8,128)(2,1)S(1)}, bf16[2,32,1152]{2,1,0:T(8,128)(2,1)S(1)}, u32[]{:S(2)}, u32[]{:S(2)}) collective-permute-start(bf16[2,32,1152]{2,1,0:T(8,128)(2,1)S(1)} %get-tuple-element.269), channel_id=1, source_target_pairs={{0,4},{4,0},{8,12},{12,8},{1,5},{5,1},{9,13},{13,9},{2,6},{6,2},{1... | collective-permute-start | bytes 442376 | tf_op jit(solution)/shard_map/ppermute | solution.py:27
  337.9 14.1 %fusion.32 = f32[3,3,384,256]{3,2,1,0:T(8,128)} fusion(bf16[13,13,32,256]{3,2,1,0:T(8,128)(2,1)S(1)} %get-tuple-element.275, bf16[1,128,13,13,384]{4,1,3,2,0:T(8,128)(2,1)} %param.12), kind=kOutput, calls=%fused_computation.51 | convolution fusion | flops 8613003264 | bytes 10461184 | tf_op jit(solution)/shard_map/conv_general_dilated | solution.py:430
  352.1 7.3 %fc_backward.6 = (bf16[2,32,1152]{2,1,0:T(8,128)(2,1)S(1)}, bf16[2,32,1152]{2,1,0:T(8,128)(2,1)S(1)}, bf16[2,32,1152]{2,1,0:T(8,128)(2,1)S(1)}, bf16[2,32,1152]{2,1,0:T(8,128)(2,1)S(1)}) custom-call(bf16[1152,4096]{1,0:T(8,128)(2,1)} %bitcast.200, bf16[4,32,4096]{2,1,0:T(8,128)(2,1)} %constant_dynamic-update-slice_fusion.12.own_ref, ...), custom_call_target="tpu_custom_call" | custom-call | tf_op jit(solution)/shard_map/fc_backward/pallas_call | solution.py:319
  368.3 14.8 %convert_dynamic-update-slice_fusion.2 = bf16[128,13,13,384]{3,0,2,1:T(8,128)(2,1)} fusion(bf16[128,13,13,384]{3,0,2,1:T(8,128)(2,1)} %bitcast.205, bf16[32,13,13,256]{3,0,2,1:T(8,128)(2,1)S(1)} %bitcast.193, bf16[1,3,3,384,256]{4,3,2,1,0:T(8,128)(2,1)S(1)} %copy-done), kind=kOutput, calls=%fused_computation.57 | convolution fusion | flops 8615079936 | bytes 8691712 | tf_op jit(solution)/shard_map/conv_general_dilated | solution.py:423
  392.8 14.2 %fusion.28 = f32[3,3,384,256]{3,2,1,0:T(8,128)} fusion(bf16[13,13,32,256]{3,2,1,0:T(8,128)(2,1)S(1)} %get-tuple-element.289, bf16[1,128,13,13,384]{4,1,3,2,0:T(8,128)(2,1)} %param.12), kind=kOutput, calls=%fused_computation.47 | convolution fusion | flops 8613003264 | bytes 10461184 | tf_op jit(solution)/shard_map/conv_general_dilated | solution.py:430
  409.7 7.3 %fc_backward.7 = (bf16[2,32,1152]{2,1,0:T(8,128)(2,1)S(1)}, bf16[2,32,1152]{2,1,0:T(8,128)(2,1)S(1)}, bf16[2,32,1152]{2,1,0:T(8,128)(2,1)S(1)}, bf16[2,32,1152]{2,1,0:T(8,128)(2,1)S(1)}) custom-call(bf16[1152,4096]{1,0:T(8,128)(2,1)} %bitcast.201, bf16[4,32,4096]{2,1,0:T(8,128)(2,1)} %constant_dynamic-update-slice_fusion.17.own_ref, ...), custom_call_target="tpu_custom_call" | custom-call | tf_op jit(solution)/shard_map/fc_backward/pallas_call | solution.py:319
  422.9 9.5 %convolution_convert_fusion = bf16[576,4096]{1,0:T(8,128)(2,1)} fusion(bf16[1024,4096]{1,0:T(8,128)(2,1)} %constant_dynamic-update-slice_fusion.24, pred[]{:T(512)S(6)} %eq.28, bf16[1024,1152]{1,0:T(8,128)(2,1)S(1)} %copy-done.64), kind=kOutput, calls=%fused_computation.5 | convolution fusion | flops 4834787328 | bytes 15728641 | tf_op jit(solution)/shard_map/dot_general | solution.py:606
  432.4 18.0 %collective-permute-start.66 = (bf16[576,4096]{1,0:T(8,128)(2,1)}, bf16[576,4096]{1,0:T(8,128)(2,1)}, u32[]{:S(2)}, u32[]{:S(2)}) collective-permute-start(bf16[576,4096]{1,0:T(8,128)(2,1)} %convolution_convert_fusion), channel_id=1, source_target_pairs={{0,1},{1,0},{2,3},{3,2},{4,5},{5,4},{6,7},{7,6},{8,9},{9,8},{10,11... | collective-permute-start | bytes 14155784 | tf_op jit(solution)/shard_map/ppermute | solution.py:22
  453.3 14.1 %fusion.24 = f32[3,3,384,256]{3,2,1,0:T(8,128)} fusion(bf16[13,13,32,256]{3,2,1,0:T(8,128)(2,1)S(1)} %get-tuple-element.302, bf16[1,128,13,13,384]{4,1,3,2,0:T(8,128)(2,1)} %param.12), kind=kOutput, calls=%fused_computation.43 | convolution fusion | flops 8613003264 | bytes 10461184 | tf_op jit(solution)/shard_map/conv_general_dilated | solution.py:430
  473.3 16.2 %convert_dynamic-update-slice_fusion.1 = bf16[128,13,13,384]{3,0,2,1:T(8,128)(2,1)} fusion(bf16[128,13,13,384]{3,0,2,1:T(8,128)(2,1)} %convert_dynamic-update-slice_fusion.2, bf16[32,13,13,256]{3,0,2,1:T(8,128)(2,1)} %bitcast.191, bf16[1,3,3,384,256]{4,3,2,1,0:T(8,128)(2,1)S(1)} %copy-done), kind=kOutput, calls=%fused_computation.56 | convolution fusion | flops 8615079936 | bytes 8691712 | tf_op jit(solution)/shard_map/conv_general_dilated | solution.py:423
  491.8 10.0 %convert_add_fusion = f32[576,4096]{1,0:T(8,128)} fusion(bf16[576,4096]{1,0:T(8,128)(2,1)} %collective-permute-done.66, bf16[1024,576]{1,0:T(8,128)(2,1)} %broadcast_select_fusion, bf16[1024,4096]{1,0:T(8,128)(2,1)S(1)} %bitcast.204), kind=kOutput, calls=%fused_computation | convolution fusion | flops 4836556800 | bytes 23724032 | tf_op jit(solution)/shard_map/dot_general | solution.py:611
  509.0 14.4 %add_add_fusion = f32[3,3,384,256]{3,2,1,0:T(8,128)S(1)} fusion(f32[3,3,384,256]{3,2,1,0:T(8,128)} %fusion.24, f32[3,3,384,256]{3,2,1,0:T(8,128)} %fusion.32, f32[3,3,384,256]{3,2,1,0:T(8,128)} %fusion.28, bf16[13,13,32,256]{3,2,1,0:T(8,128)(2,1)S(1)} %get-tuple-element.316, bf16[1,128,13,13,384]{4,1,3,2,0:T(8,128)(2,1)} %param.12), kind=kOutput, calls=%fused_computation.66 | convolution fusion | flops 8615657472 | bytes 21078016 | tf_op jit(solution)/shard_map/conv_general_dilated | solution.py:430
  525.7 15.1 %convert_dynamic-update-slice_fusion = bf16[128,13,13,384]{3,0,2,1:T(8,128)(2,1)} fusion(bf16[128,13,13,384]{3,0,2,1:T(8,128)(2,1)} %convert_dynamic-update-slice_fusion.1, bf16[32,13,13,256]{3,0,2,1:T(8,128)(2,1)S(1)} %bitcast.192, bf16[1,3,3,384,256]{4,3,2,1,0:T(8,128)(2,1)S(1)} %copy-done), kind=kOutput, calls=%fused_computation.55 | convolution fusion | flops 8615079936 | bytes 8691712 | tf_op jit(solution)/shard_map/conv_general_dilated | solution.py:423
  546.6 8.1 %collective-permute-done.68 = bf16[864,256]{1,0:T(8,128)(2,1)S(1)} collective-permute-done((bf16[864,256]{1,0:T(8,128)(2,1)S(1)}, bf16[864,256]{1,0:T(8,128)(2,1)S(1)}, u32[]{:S(2)}, u32[]{:S(2)}) %collective-permute-start.68) | collective-permute-done | bytes 442400 | tf_op jit(solution)/shard_map/ppermute | solution.py:18
  560.6 6.2 %collective-permute-done.70 = bf16[216,256]{1,0:T(8,128)(2,1)S(1)} collective-permute-done((bf16[216,256]{1,0:T(8,128)(2,1)S(1)}, bf16[216,256]{1,0:T(8,128)(2,1)S(1)}, u32[]{:S(2)}, u32[]{:S(2)}) %collective-permute-start.70) | collective-permute-done | bytes 110624 | tf_op jit(solution)/shard_map/ppermute | solution.py:27
  573.1 6.4 %collective-permute-done.79 = f32[1,13056]{1,0:T(1,128)S(1)} collective-permute-done((f32[1,13056]{1,0:T(1,128)S(1)}, f32[1,13056]{1,0:T(1,128)S(1)}, u32[]{:S(2)}, u32[]{:S(2)}) %collective-permute-start.79) | collective-permute-done | bytes 52256 | tf_op jit(solution)/shard_map/ppermute | solution.py:27
  580.0 16.3 %bitcast_dynamic-update-slice_fusion = bf16[1,128,13,13,384]{4,1,3,2,0:T(8,128)(2,1)} fusion(bf16[1,128,13,13,384]{4,1,3,2,0:T(8,128)(2,1)} %bitcast.206, bf16[32,13,13,256]{3,0,2,1:T(8,128)(2,1)} %bitcast.190, bf16[1,3,3,384,256]{4,3,2,1,0:T(8,128)(2,1)S(1)} %copy-done), kind=kOutput, calls=%fused_computation.38 | convolution fusion | flops 8615079936 | bytes 8691712 | tf_op jit(solution)/shard_map/conv_general_dilated | solution.py:423
  (470 shorter events, 235.0 us)
Async XLA Ops:
  7.2 89.7 %all-gather.3.cloned.1.call-start = ((), (), s32[]{:S(2)}) async-start(), calls=%async_computation | async-start | bytes 14155776 | tf_op jit(solution)/shard_map/all_gather | solution.py:481
  27.9 23.3 %collective-permute-start = (bf16[32,9216]{1,0:T(8,128)(2,1)S(1)}, bf16[32,9216]{1,0:T(8,128)(2,1)S(1)}, u32[]{:S(2)}, u32[]{:S(2)}) collective-permute-start(bf16[32,9216]{1,0:T(8,128)(2,1)S(1)} %get-tuple-element.174.pooled_ref), channel_id=1, source_target_pairs={{0,16},{16,0},{1,17},{17,1},{2,18},{18,2},{3,19},{19,3},{4,20},{20... | collective-permute-start | bytes 1769480 | tf_op jit(solution)/shard_map/ppermute | solution.py:31
  50.8 27.7 %collective-permute-start.5 = (bf16[32,9216]{1,0:T(8,128)(2,1)}, bf16[32,9216]{1,0:T(8,128)(2,1)}, u32[]{:S(2)}, u32[]{:S(2)}) collective-permute-start(bf16[32,9216]{1,0:T(8,128)(2,1)} %get-tuple-element.182.pooled_ref), channel_id=1, source_target_pairs={{0,16},{16,0},{1,17},{17,1},{2,18},{18,2},{3,19},{19,3},{4,20},{20... | collective-permute-start | bytes 1769480 | tf_op jit(solution)/shard_map/ppermute | solution.py:31
  52.1 24.8 %collective-permute-start.3 = (bf16[2,32,1152]{2,1,0:T(8,128)(2,1)S(1)}, bf16[2,32,1152]{2,1,0:T(8,128)(2,1)S(1)}, u32[]{:S(2)}, u32[]{:S(2)}) collective-permute-start(bf16[2,32,1152]{2,1,0:T(8,128)(2,1)S(1)} %get-tuple-element.181), channel_id=1, source_target_pairs={{0,12},{4,8},{8,4},{12,0},{1,13},{5,9},{9,5},{13,1},{2,14},{6,10},... | collective-permute-start | bytes 442376 | tf_op jit(solution)/shard_map/ppermute | solution.py:27
  76.0 31.9 %collective-permute-start.7 = (bf16[32,9216]{1,0:T(8,128)(2,1)S(1)}, bf16[32,9216]{1,0:T(8,128)(2,1)S(1)}, u32[]{:S(2)}, u32[]{:S(2)}) collective-permute-start(bf16[32,9216]{1,0:T(8,128)(2,1)S(1)} %get-tuple-element.187.pooled_ref), channel_id=1, source_target_pairs={{0,16},{16,0},{1,17},{17,1},{2,18},{18,2},{3,19},{19,3},{4,20},{20... | collective-permute-start | bytes 1769480 | tf_op jit(solution)/shard_map/ppermute | solution.py:31
  109.9 33.0 %collective-permute-start.12 = (bf16[4,32,1152]{2,1,0:T(8,128)(2,1)S(1)}, bf16[4,32,1152]{2,1,0:T(8,128)(2,1)S(1)}, u32[]{:S(2)}, u32[]{:S(2)}) collective-permute-start(bf16[4,32,1152]{2,1,0:T(8,128)(2,1)S(1)} %pad_maximum_fusion.4), channel_id=1, source_target_pairs={{0,2},{2,0},{1,3},{3,1},{4,6},{6,4},{5,7},{7,5},{8,10},{10,8},{9,1... | collective-permute-start | bytes 884744 | tf_op jit(solution)/shard_map/ppermute | solution.py:18
  110.6 28.6 %collective-permute-start.6 = (bf16[4,32,4096]{2,1,0:T(8,128)(2,1)S(1)}, bf16[4,32,4096]{2,1,0:T(8,128)(2,1)S(1)}, u32[]{:S(2)}, u32[]{:S(2)}) collective-permute-start(bf16[4,32,4096]{2,1,0:T(8,128)(2,1)S(1)} %get-tuple-element.186), channel_id=1, source_target_pairs={{0,2},{2,0},{1,3},{3,1},{4,6},{6,4},{5,7},{7,5},{8,10},{10,8},{9,1... | collective-permute-start | bytes 3145736 | tf_op jit(solution)/shard_map/ppermute | solution.py:18
  132.5 22.5 %collective-permute-start.14 = (bf16[2,32,1152]{2,1,0:T(8,128)(2,1)S(1)}, bf16[2,32,1152]{2,1,0:T(8,128)(2,1)}, u32[]{:S(2)}, u32[]{:S(2)}) collective-permute-start(bf16[2,32,1152]{2,1,0:T(8,128)(2,1)S(1)} %get-tuple-element.202), channel_id=1, source_target_pairs={{0,4},{4,0},{8,12},{12,8},{1,5},{5,1},{9,13},{13,9},{2,6},{6,2},{1... | collective-permute-start | bytes 442376 | tf_op jit(solution)/shard_map/ppermute | solution.py:27
  132.5 24.7 %collective-permute-start.13 = (bf16[2,32,1152]{2,1,0:T(8,128)(2,1)}, bf16[2,32,1152]{2,1,0:T(8,128)(2,1)}, u32[]{:S(2)}, u32[]{:S(2)}) collective-permute-start(bf16[2,32,1152]{2,1,0:T(8,128)(2,1)} %get-tuple-element.201), channel_id=1, source_target_pairs={{0,8},{4,12},{8,0},{12,4},{1,9},{5,13},{9,1},{13,5},{2,10},{6,14},... | collective-permute-start | bytes 442376 | tf_op jit(solution)/shard_map/ppermute | solution.py:27
  152.3 22.5 %collective-permute-start.19 = (bf16[4,32,4096]{2,1,0:T(8,128)(2,1)}, bf16[4,32,4096]{2,1,0:T(8,128)(2,1)}, u32[]{:S(2)}, u32[]{:S(2)}) collective-permute-start(bf16[4,32,4096]{2,1,0:T(8,128)(2,1)} %get-tuple-element.199), channel_id=1, source_target_pairs={{0,2},{2,0},{1,3},{3,1},{4,6},{6,4},{5,7},{7,5},{8,10},{10,8},{9,1... | collective-permute-start | bytes 3145736 | tf_op jit(solution)/shard_map/ppermute | solution.py:18
  154.1 33.9 %collective-permute-start.23 = (bf16[128,4096]{1,0:T(8,128)(2,1)}, bf16[128,4096]{1,0:T(8,128)(2,1)}, u32[]{:S(2)}, u32[]{:S(2)}) collective-permute-start(bf16[128,4096]{1,0:T(8,128)(2,1)} %multiply_convert_fusion), channel_id=1, source_target_pairs={{0,16},{16,0},{1,17},{17,1},{2,18},{18,2},{3,19},{19,3},{4,20},{20... | collective-permute-start | bytes 3145736 | tf_op jit(solution)/shard_map/ppermute | solution.py:31
  205.1 26.3 %collective-permute-start.30 = (bf16[4,32,4096]{2,1,0:T(8,128)(2,1)}, bf16[4,32,4096]{2,1,0:T(8,128)(2,1)S(1)}, u32[]{:S(2)}, u32[]{:S(2)}) collective-permute-start(bf16[4,32,4096]{2,1,0:T(8,128)(2,1)} %copy-done.62), channel_id=1, source_target_pairs={{0,2},{2,0},{1,3},{3,1},{4,6},{6,4},{5,7},{7,5},{8,10},{10,8},{9,1... | collective-permute-start | bytes 3145736 | tf_op jit(solution)/shard_map/ppermute | solution.py:18
  210.2 30.5 %collective-permute-start.29 = (bf16[2,32,4096]{2,1,0:T(8,128)(2,1)S(1)}, bf16[2,32,4096]{2,1,0:T(8,128)(2,1)S(1)}, u32[]{:S(2)}, u32[]{:S(2)}) collective-permute-start(bf16[2,32,4096]{2,1,0:T(8,128)(2,1)S(1)} %get-tuple-element.230), channel_id=1, source_target_pairs={{0,4},{4,0},{8,12},{12,8},{1,5},{5,1},{9,13},{13,9},{2,6},{6,2},{1... | collective-permute-start | bytes 1572872 | tf_op jit(solution)/shard_map/ppermute | solution.py:27
  213.8 27.2 %collective-permute-start.33 = (bf16[1,32,4096]{2,1,0:T(8,128)(2,1)S(1)}, bf16[1,32,4096]{2,1,0:T(8,128)(2,1)S(1)}, u32[]{:S(2)}, u32[]{:S(2)}) collective-permute-start(bf16[1,32,4096]{2,1,0:T(8,128)(2,1)S(1)} %get-tuple-element.235), channel_id=1, source_target_pairs={{0,8},{4,12},{8,0},{12,4},{1,9},{5,13},{9,1},{13,5},{2,10},{6,14},... | collective-permute-start | bytes 786440 | tf_op jit(solution)/shard_map/ppermute | solution.py:27
  226.7 27.2 %collective-permute-start.35 = (bf16[4,32,4096]{2,1,0:T(8,128)(2,1)S(1)}, bf16[4,32,4096]{2,1,0:T(8,128)(2,1)S(1)}, u32[]{:S(2)}, u32[]{:S(2)}) collective-permute-start(bf16[4,32,4096]{2,1,0:T(8,128)(2,1)S(1)} %constant_dynamic-update-slice_fusion.2.own_ref), channel_id=1, source_target_pairs={{0,2},{2,0},{1,3},{3,1},{4,6},{6,4},{5,7},{7,5},{8,10},{10,8},{9,1... | collective-permute-start | bytes 3145736 | tf_op jit(solution)/shard_map/ppermute | solution.py:18
  241.1 26.8 %collective-permute-start.34 = (bf16[2,32,4096]{2,1,0:T(8,128)(2,1)S(1)}, bf16[2,32,4096]{2,1,0:T(8,128)(2,1)S(1)}, u32[]{:S(2)}, u32[]{:S(2)}) collective-permute-start(bf16[2,32,4096]{2,1,0:T(8,128)(2,1)S(1)} %get-tuple-element.365), channel_id=1, source_target_pairs={{0,4},{4,0},{8,12},{12,8},{1,5},{5,1},{9,13},{13,9},{2,6},{6,2},{1... | collective-permute-start | bytes 1572872 | tf_op jit(solution)/shard_map/ppermute | solution.py:27
  245.5 22.4 %collective-permute-start.32 = (bf16[1,32,4096]{2,1,0:T(8,128)(2,1)S(1)}, bf16[1,32,4096]{2,1,0:T(8,128)(2,1)S(1)}, u32[]{:S(2)}, u32[]{:S(2)}) collective-permute-start(bf16[1,32,4096]{2,1,0:T(8,128)(2,1)S(1)} %get-tuple-element.241), channel_id=1, source_target_pairs={{0,8},{4,12},{8,0},{12,4},{1,9},{5,13},{9,1},{13,5},{2,10},{6,14},... | collective-permute-start | bytes 786440 | tf_op jit(solution)/shard_map/ppermute | solution.py:27
  249.1 49.8 %collective-permute-start.37 = (bf16[1,32,4096]{2,1,0:T(8,128)(2,1)S(1)}, bf16[1,32,4096]{2,1,0:T(8,128)(2,1)S(1)}, u32[]{:S(2)}, u32[]{:S(2)}) collective-permute-start(bf16[1,32,4096]{2,1,0:T(8,128)(2,1)S(1)} %get-tuple-element.245), channel_id=1, source_target_pairs={{0,8},{4,12},{8,0},{12,4},{1,9},{5,13},{9,1},{13,5},{2,10},{6,14},... | collective-permute-start | bytes 786440 | tf_op jit(solution)/shard_map/ppermute | solution.py:27
  270.3 32.5 %collective-permute-start.39 = (bf16[1,32,4096]{2,1,0:T(8,128)(2,1)S(1)}, bf16[1,32,4096]{2,1,0:T(8,128)(2,1)S(1)}, u32[]{:S(2)}, u32[]{:S(2)}) collective-permute-start(bf16[1,32,4096]{2,1,0:T(8,128)(2,1)S(1)} %get-tuple-element.252), channel_id=1, source_target_pairs={{0,8},{4,12},{8,0},{12,4},{1,9},{5,13},{9,1},{13,5},{2,10},{6,14},... | collective-permute-start | bytes 786440 | tf_op jit(solution)/shard_map/ppermute | solution.py:27
  274.6 24.3 %collective-permute-start.40 = (bf16[2,32,1152]{2,1,0:T(8,128)(2,1)S(1)}, bf16[2,32,1152]{2,1,0:T(8,128)(2,1)S(1)}, u32[]{:S(2)}, u32[]{:S(2)}) collective-permute-start(bf16[2,32,1152]{2,1,0:T(8,128)(2,1)S(1)} %get-tuple-element.257), channel_id=1, source_target_pairs={{0,8},{4,12},{8,0},{12,4},{1,9},{5,13},{9,1},{13,5},{2,10},{6,14},... | collective-permute-start | bytes 442376 | tf_op jit(solution)/shard_map/ppermute | solution.py:27
  279.8 27.6 %collective-permute-start.38 = (bf16[4,32,4096]{2,1,0:T(8,128)(2,1)S(1)}, bf16[4,32,4096]{2,1,0:T(8,128)(2,1)S(1)}, u32[]{:S(2)}, u32[]{:S(2)}) collective-permute-start(bf16[4,32,4096]{2,1,0:T(8,128)(2,1)S(1)} %constant_dynamic-update-slice_fusion.7.own_ref), channel_id=1, source_target_pairs={{0,2},{2,0},{1,3},{3,1},{4,6},{6,4},{5,7},{7,5},{8,10},{10,8},{9,1... | collective-permute-start | bytes 3145736 | tf_op jit(solution)/shard_map/ppermute | solution.py:18
  301.2 25.8 %collective-permute-start.43 = (bf16[1,32,4096]{2,1,0:T(8,128)(2,1)S(1)}, bf16[1,32,4096]{2,1,0:T(8,128)(2,1)S(1)}, u32[]{:S(2)}, u32[]{:S(2)}) collective-permute-start(bf16[1,32,4096]{2,1,0:T(8,128)(2,1)S(1)} %get-tuple-element.255), channel_id=1, source_target_pairs={{0,8},{4,12},{8,0},{12,4},{1,9},{5,13},{9,1},{13,5},{2,10},{6,14},... | collective-permute-start | bytes 786440 | tf_op jit(solution)/shard_map/ppermute | solution.py:27
  327.8 35.1 %collective-permute-start.51 = (bf16[2,32,4096]{2,1,0:T(8,128)(2,1)}, bf16[2,32,4096]{2,1,0:T(8,128)(2,1)}, u32[]{:S(2)}, u32[]{:S(2)}) collective-permute-start(bf16[2,32,4096]{2,1,0:T(8,128)(2,1)} %get-tuple-element.357), channel_id=1, source_target_pairs={{0,4},{4,0},{8,12},{12,8},{1,5},{5,1},{9,13},{13,9},{2,6},{6,2},{1... | collective-permute-start | bytes 1572872 | tf_op jit(solution)/shard_map/ppermute | solution.py:27
  333.6 25.8 %collective-permute-start.52 = (bf16[4,32,1152]{2,1,0:T(8,128)(2,1)}, bf16[4,32,1152]{2,1,0:T(8,128)(2,1)}, u32[]{:S(2)}, u32[]{:S(2)}) collective-permute-start(bf16[4,32,1152]{2,1,0:T(8,128)(2,1)} %pad_maximum_fusion.8), channel_id=1, source_target_pairs={{0,2},{2,0},{1,3},{3,1},{4,6},{6,4},{5,7},{7,5},{8,10},{10,8},{9,1... | collective-permute-start | bytes 884744 | tf_op jit(solution)/shard_map/ppermute | solution.py:18
  335.0 205.8 %collective-permute-start.49 = (bf16[128,4096]{1,0:T(8,128)(2,1)}, bf16[128,4096]{1,0:T(8,128)(2,1)}, u32[]{:S(2)}, u32[]{:S(2)}) collective-permute-start(bf16[128,4096]{1,0:T(8,128)(2,1)} %pad_maximum_fusion), channel_id=1, source_target_pairs={{0,16},{16,0},{1,17},{17,1},{2,18},{18,2},{3,19},{19,3},{4,20},{20... | collective-permute-start | bytes 3145736 | tf_op jit(solution)/shard_map/ppermute | solution.py:31
  361.3 28.2 %collective-permute-start.54 = (bf16[32,9216]{1,0:T(8,128)(2,1)S(1)}, bf16[32,9216]{1,0:T(8,128)(2,1)S(1)}, u32[]{:S(2)}, u32[]{:S(2)}) collective-permute-start(bf16[32,9216]{1,0:T(8,128)(2,1)S(1)} %get-tuple-element.279), channel_id=1, source_target_pairs={{0,16},{16,0},{1,17},{17,1},{2,18},{18,2},{3,19},{19,3},{4,20},{20... | collective-permute-start | bytes 1769480 | tf_op jit(solution)/shard_map/ppermute | solution.py:31
  364.7 23.1 %collective-permute-start.57 = (bf16[2,32,1152]{2,1,0:T(8,128)(2,1)S(1)}, bf16[2,32,1152]{2,1,0:T(8,128)(2,1)S(1)}, u32[]{:S(2)}, u32[]{:S(2)}) collective-permute-start(bf16[2,32,1152]{2,1,0:T(8,128)(2,1)S(1)} %get-tuple-element.286), channel_id=1, source_target_pairs={{0,12},{4,8},{8,4},{12,0},{1,13},{5,9},{9,5},{13,1},{2,14},{6,10},... | collective-permute-start | bytes 442376 | tf_op jit(solution)/shard_map/ppermute | solution.py:27
  409.6 22.8 %collective-permute-start.60 = (bf16[32,9216]{1,0:T(8,128)(2,1)}, bf16[32,9216]{1,0:T(8,128)(2,1)}, u32[]{:S(2)}, u32[]{:S(2)}) collective-permute-start(bf16[32,9216]{1,0:T(8,128)(2,1)} %get-tuple-element.291), channel_id=1, source_target_pairs={{0,16},{16,0},{1,17},{17,1},{2,18},{18,2},{3,19},{19,3},{4,20},{20... | collective-permute-start | bytes 1769480 | tf_op jit(solution)/shard_map/ppermute | solution.py:31
  417.0 51.1 %collective-permute-start.63 = (bf16[2,32,1152]{2,1,0:T(8,128)(2,1)S(1)}, bf16[2,32,1152]{2,1,0:T(8,128)(2,1)}, u32[]{:S(2)}, u32[]{:S(2)}) collective-permute-start(bf16[2,32,1152]{2,1,0:T(8,128)(2,1)S(1)} %get-tuple-element.306), channel_id=1, source_target_pairs={{0,12},{4,8},{8,4},{12,0},{1,13},{5,9},{9,5},{13,1},{2,14},{6,10},... | collective-permute-start | bytes 442376 | tf_op jit(solution)/shard_map/ppermute | solution.py:27
  418.8 50.2 %collective-permute-start.62 = (bf16[2,32,1152]{2,1,0:T(8,128)(2,1)S(1)}, bf16[2,32,1152]{2,1,0:T(8,128)(2,1)}, u32[]{:S(2)}, u32[]{:S(2)}) collective-permute-start(bf16[2,32,1152]{2,1,0:T(8,128)(2,1)S(1)} %get-tuple-element.305), channel_id=1, source_target_pairs={{0,4},{4,0},{8,12},{12,8},{1,5},{5,1},{9,13},{13,9},{2,6},{6,2},{1... | collective-permute-start | bytes 442376 | tf_op jit(solution)/shard_map/ppermute | solution.py:27
  418.8 51.1 %collective-permute-start.61 = (bf16[2,32,1152]{2,1,0:T(8,128)(2,1)S(1)}, bf16[2,32,1152]{2,1,0:T(8,128)(2,1)}, u32[]{:S(2)}, u32[]{:S(2)}) collective-permute-start(bf16[2,32,1152]{2,1,0:T(8,128)(2,1)S(1)} %get-tuple-element.304), channel_id=1, source_target_pairs={{0,8},{4,12},{8,0},{12,4},{1,9},{5,13},{9,1},{13,5},{2,10},{6,14},... | collective-permute-start | bytes 442376 | tf_op jit(solution)/shard_map/ppermute | solution.py:27
  432.4 59.4 %collective-permute-start.66 = (bf16[576,4096]{1,0:T(8,128)(2,1)}, bf16[576,4096]{1,0:T(8,128)(2,1)}, u32[]{:S(2)}, u32[]{:S(2)}) collective-permute-start(bf16[576,4096]{1,0:T(8,128)(2,1)} %convolution_convert_fusion), channel_id=1, source_target_pairs={{0,1},{1,0},{2,3},{3,2},{4,5},{5,4},{6,7},{7,6},{8,9},{9,8},{10,11... | collective-permute-start | bytes 14155784 | tf_op jit(solution)/shard_map/ppermute | solution.py:22
  (132 other events, 1579.7 us)
Sparse Core Ops, SparseCore 0:
  9.6 24.2 all-gather.2

commit v4 on v3

--- a/solution.py
+++ b/solution.py
@@ -7,7 +7,7 @@
 from jax.experimental.pallas import tpu as pltpu
 from jax.sharding import PartitionSpec as P
 
-PLAN = "0102010213012301320130210321301230210231S021302123W2313W32S3"
+PLAN = "0102010213012301320130210321301230210231S021302123W23W3S3AA1A2A3AAA"
 BF16 = jnp.bfloat16
 F32 = jnp.float32
 CONV_DIMS = ("NHWC", "HWIO", "NHWC")
@@ -442,23 +442,37 @@
     return vector
 
 
-def sum_kernel(rows, outer, mid, core):
+def sum_kernel(stage, last, after, rows, outer, mid, core):
     outer_count = lax.axis_size("outer")
     for swap, side in ((swap_mid, mid), (swap_core, core)):
         halves = rows.reshape(2, -1, rows.shape[1])
-        got = swap(pick(halves, 1 - side).astype(BF16))
-        rows = pick(halves, side) + got.astype(F32)
+        sent, kept = pick(halves, 1 - side).astype(BF16), pick(halves, side)
+        last[0] = sent
+        got = swap(sent)
+        yield
+        rows = kept + after(got).astype(F32)
     parts = rows.reshape(outer_count, -1, rows.shape[1])
     total = pick(parts, outer)
-    for k in range(1, outer_count):
-        total = total + swap_outer(pick(parts, outer ^ k).astype(BF16), k).astype(F32)
+    sent = [pick(parts, outer ^ k).astype(BF16) for k in range(1, outer_count)]
+    last[0] = sent[-1]
+    got = [swap_outer(s, k + 1) for k, s in enumerate(sent)]
+    yield
+    got[0] = after(got[0])
+    for g in got:
+        total = total + g.astype(F32)
     total = total.astype(BF16)
-    stack = jnp.stack([total] + [swap_outer(total, k) for k in range(1, outer_count)])
+    last[0] = total
+    stack = [total] + [swap_outer(total, k) for k in range(1, outer_count)]
+    yield
+    stack = jnp.stack([after(total), *stack[1:]])
     rows = jnp.concatenate([pick(stack, outer ^ k) for k in range(outer_count)])
     for swap, side in ((swap_core, core), (swap_mid, mid)):
+        last[0] = rows
         got = swap(rows)
+        yield
+        got = after(got)
         rows = jnp.where(side == 0, jnp.concatenate([rows, got]), jnp.concatenate([got, rows]))
-    return rows.astype(F32)
+    stage["kernel"] = rows.astype(F32)
 
 
 def body(
@@ -611,12 +625,14 @@
         stage["gradient"] = lax.dot_general(own, grads, lead, preferred_element_type=F32) + came.astype(F32)
         last[0] = stage["gradient"]
 
+    def kernel_sum():
+        yield from sum_kernel(stage, last, after, sums["kernel"].reshape(-1, width), outer, mid, core)
+
     runs = {str(n): chunk(n) for n in range(len(sizes))}
-    runs.update(W=fc_weight_gradient(), S=stitch())
-    for n in PLAN if len(sizes) > 1 else "0" * (2 * hops + 6) + "WS" + "0" * 5 + "WS":
+    runs.update(W=fc_weight_gradient(), S=stitch(), A=kernel_sum())
+    for n in PLAN if len(sizes) > 1 else "0" * (2 * hops + 6) + "WS" + "0" * 4 + "AA0" + "WS" + "A" * 5:
         next(runs[n], None)
     grad_fc_weight = stage["gradient"]
-    kernel_sum = sums["kernel"]
     conv_bias_sum, fc_bias_sum = sums["conv_bias"], sums["fc_bias"]
     hidden_self, hidden_cross = stage["hidden"]
     pool_self, pool_cross = sums["pool"]
@@ -632,7 +648,7 @@
     grad_row_fc = jnp.where(
         is_first, jnp.stack([hidden_self, hidden_cross]), jnp.stack([hidden_cross, hidden_self])
     )
-    summed_kernel = sum_kernel(kernel_sum.reshape(-1, width), outer, mid, core).reshape(kernel.shape)
+    summed_kernel = stage["kernel"].reshape(kernel.shape)
     return (
         stage["output"][None],
         stage["grad_in"][None],

time: 622 us -> 597 us (0.960)
  waiting for transfers between devices: 101 us -> 78.6 us
  local copies, waits for them, and re-layouts: 50.9 us -> 43.9 us
    ppermute x48, waiting for transfers between devices: 80.2 us -> 43 us  [swap_outer(): return lax.ppermute(block, 'outer', [(i, i ^ mask) for i in range(count)])]
    ppermute x48, starting transfers between devices: 68 us -> 81.3 us  [swap_outer(): return lax.ppermute(block, 'outer', [(i, i ^ mask) for i in range(count)])]
    ppermute x19, waiting for transfers between devices: 14.9 us -> 22.7 us  [swap_core(): return lax.ppermute(block, 'core', [(0, 1), (1, 0)])]
    unnamed x193 -> x185, local copies, waits for them, and re-layouts: 34.4 us -> 32.9 us
  transfers between devices with their start and end apart: 82 -> 82, of which waited for: 23 -> 23; matrix products, arithmetic and copies ran while one was open for 42% -> 40% of each run, Pallas kernels for 16% -> 16%
where the time goes in v4:
time: 597 us; the launch traced here: 585 us
  matrix products  208 us (35%)
  starting transfers between devices  119 us (20%)
  Pallas kernels  99.3 us (17%)
  waiting for transfers between devices  78.6 us (13%)
  local copies, waits for them, and re-layouts  43.9 us (7%)
  other arithmetic  20.5 us (3%)
  between operations  16.1 us (3%)
    ppermute x48, starting transfers between devices, swap_outer(): return lax.ppermute(block, 'outer', [(i, i ^ mask) for i in range(count)])  81.3 us
    conv_general_dilated x4, matrix products, conv_forward(): lax.conv_general_dilated(inputs, kernel, (1, 1), ((1, 1), (1, 1)), dimens...  72.6 us
    conv_general_dilated x4, matrix products, conv_grad_inputs(): lax.conv_general_dilated(grad_pre, turned, (1, 1), ((1, 1), (1, 1)), dime...  59.8 us
    conv_general_dilated x4, matrix products, conv_grad_kernel(): lax.conv_general_dilated(inputs, grad_pre, (1, 1), ((1, 1), (1, 1)), dime...  56.3 us
    ppermute x48, waiting for transfers between devices, swap_outer(): return lax.ppermute(block, 'outer', [(i, i ^ mask) for i in range(count)])  43 us
    unnamed x185, local copies, waits for them, and re-layouts  32.9 us
    pallas_call x4, Pallas kernels, fc_forward(): pl.pallas_call(functools.partial(fc_forward_kernel, count), grid=(units /...  27.1 us
    pallas_call x4, Pallas kernels, fc_backward(): pl.pallas_call(functools.partial(fc_back_kernel, count), grid=(depth // t...  26.3 us
  transfers between devices with their start and end apart: 82, of which 23 were waited for; matrix products, arithmetic and copies ran while one was open for 40% of the time, Pallas kernels for 16%

profile of v4, /device:TPU:1, one launch (start us, length us, event | category | flops | bytes accessed | tf_op | source)
XLA Modules:
  0.0 585.0 jit_solution(3776871882453701225)
XLA Ops:
  8.7 18.4 %fusion.3 = (bf16[13,13,32,256]{3,2,1,0:T(8,128)(2,1)}, bf16[13,13,32,256]{3,2,1,0:T(8,128)(2,1)S(1)}) fusion(f32[256]{0:T(256)S(1)} %bitcast.228, bf16[1,3,3,384,256]{4,3,2,1,0:T(8,128)(2,1)S(1)} %copy-done, bf16[1,128,13,13,384]{4,1,3,2,0:T(8,128)(2,1)} %param.12), kind=kOutput, calls=%fused_computation.9 | convolution fusion | flops 8639307776 | bytes 11461632 | tf_op jit(solution)/shard_map/conv_general_dilated | solution.py:413
  30.1 18.1 %fusion.7 = (bf16[13,13,32,256]{3,2,1,0:T(8,128)(2,1)}, bf16[13,13,32,256]{3,2,1,0:T(8,128)(2,1)S(1)}) fusion(f32[256]{0:T(256)S(1)} %bitcast.229, bf16[1,3,3,384,256]{4,3,2,1,0:T(8,128)(2,1)S(1)} %copy-done, bf16[1,128,13,13,384]{4,1,3,2,0:T(8,128)(2,1)} %param.12), kind=kOutput, calls=%fused_computation.13 | convolution fusion | flops 8639307776 | bytes 11461632 | tf_op jit(solution)/shard_map/conv_general_dilated | solution.py:413
  56.0 18.1 %fusion.11 = (bf16[13,13,32,256]{3,2,1,0:T(8,128)(2,1)}, bf16[13,13,32,256]{3,2,1,0:T(8,128)(2,1)S(1)}) fusion(f32[256]{0:T(256)S(1)} %bitcast.230, bf16[1,3,3,384,256]{4,3,2,1,0:T(8,128)(2,1)S(1)} %copy-done, bf16[1,128,13,13,384]{4,1,3,2,0:T(8,128)(2,1)} %param.12), kind=kOutput, calls=%fused_computation.17 | convolution fusion | flops 8639307776 | bytes 11461632 | tf_op jit(solution)/shard_map/conv_general_dilated | solution.py:413
  97.6 6.4 %fc_forward.4 = (f32[4,32,4096]{2,1,0:T(8,128)S(1)}, bf16[4,32,4096]{2,1,0:T(8,128)(2,1)S(1)}, bf16[256,1152]{1,0:T(8,128)(2,1)S(1)}) custom-call(bf16[1152,4096]{1,0:T(8,128)(2,1)} %bitcast.196, bf16[4,32,1152]{2,1,0:T(8,128)(2,1)S(1)} %copy-done.46, bf16[2,32,1152]{2,1,0:T(8,128)(2,1)S(1)} %copy-done.38, bf16[2,32,1152]{2,1,0:T(8,128)(2,1)S(1)} %copy-done.40, ...), custom_call_target="tpu_custom_call" | custom-call | tf_op jit(solution)/shard_map/fc_forward/pallas_call | solution.py:272
  108.2 18.1 %fusion.15 = (bf16[13,13,32,256]{3,2,1,0:T(8,128)(2,1)}, bf16[13,13,32,256]{3,2,1,0:T(8,128)(2,1)S(1)}) fusion(f32[256]{0:T(256)S(1)} %bitcast.231, bf16[1,3,3,384,256]{4,3,2,1,0:T(8,128)(2,1)S(1)} %copy-done, bf16[1,128,13,13,384]{4,1,3,2,0:T(8,128)(2,1)} %param.12), kind=kOutput, calls=%fused_computation.21 | convolution fusion | flops 8639307776 | bytes 11461632 | tf_op jit(solution)/shard_map/conv_general_dilated | solution.py:413
  138.7 7.2 %fc_forward.5 = (f32[4,32,4096]{2,1,0:T(8,128)S(1)}, bf16[4,32,4096]{2,1,0:T(8,128)(2,1)}, bf16[256,1152]{1,0:T(8,128)(2,1)S(1)}) custom-call(bf16[1152,4096]{1,0:T(8,128)(2,1)} %bitcast.197, bf16[4,32,1152]{2,1,0:T(8,128)(2,1)S(1)} %collective-permute-done.12.got_ref, bf16[2,32,1152]{2,1,0:T(8,128)(2,1)S(1)} %copy-done.30, ...), custom_call_target="tpu_custom_call" | custom-call | tf_op jit(solution)/shard_map/fc_forward/pallas_call | solution.py:272
  177.5 6.5 %fc_forward.6 = (f32[4,32,4096]{2,1,0:T(8,128)S(1)}, bf16[4,32,4096]{2,1,0:T(8,128)(2,1)S(1)}, bf16[256,1152]{1,0:T(8,128)(2,1)S(1)}) custom-call(bf16[1152,4096]{1,0:T(8,128)(2,1)} %bitcast.198, bf16[4,32,1152]{2,1,0:T(8,128)(2,1)S(1)} %collective-permute-done.18.got_ref, bf16[2,32,1152]{2,1,0:T(8,128)(2,1)S(1)} %copy-done.28, ...), custom_call_target="tpu_custom_call" | custom-call | tf_op jit(solution)/shard_map/fc_forward/pallas_call | solution.py:272
  191.5 7.0 %fc_forward.7 = (f32[4,32,4096]{2,1,0:T(8,128)S(1)}, bf16[4,32,4096]{2,1,0:T(8,128)(2,1)}, bf16[256,1152]{1,0:T(8,128)(2,1)S(1)}) custom-call(bf16[1152,4096]{1,0:T(8,128)(2,1)} %bitcast.199, bf16[4,32,1152]{2,1,0:T(8,128)(2,1)S(1)} %collective-permute-done.28.got_ref, bf16[2,32,1152]{2,1,0:T(8,128)(2,1)S(1)} %get-tuple-element.218.refs_0_, ...), custom_call_target="tpu_custom_call" | custom-call | tf_op jit(solution)/shard_map/fc_forward/pallas_call | solution.py:272
  214.8 12.9 %collective-permute-done.30.came_ref = bf16[4,32,4096]{2,1,0:T(8,128)(2,1)S(1)} collective-permute-done((bf16[4,32,4096]{2,1,0:T(8,128)(2,1)}, bf16[4,32,4096]{2,1,0:T(8,128)(2,1)S(1)}, u32[]{:S(2)}, u32[]{:S(2)}) %collective-permute-start.30) | collective-permute-done | bytes 1048608 | tf_op jit(solution)/shard_map/ppermute | solution.py:18
  234.7 6.0 %collective-permute-start.32 = (bf16[1,32,4096]{2,1,0:T(8,128)(2,1)S(1)}, bf16[1,32,4096]{2,1,0:T(8,128)(2,1)S(1)}, u32[]{:S(2)}, u32[]{:S(2)}) collective-permute-start(bf16[1,32,4096]{2,1,0:T(8,128)(2,1)S(1)} %get-tuple-element.247), channel_id=1, source_target_pairs={{0,8},{4,12},{8,0},{12,4},{1,9},{5,13},{9,1},{13,5},{2,10},{6,14},... | collective-permute-start | bytes 786440 | tf_op jit(solution)/shard_map/ppermute | solution.py:27
  241.6 5.6 collective-permute-start.37
  250.2 6.5 %fc_backward.4 = (bf16[2,32,1152]{2,1,0:T(8,128)(2,1)S(1)}, bf16[2,32,1152]{2,1,0:T(8,128)(2,1)S(1)}, bf16[2,32,1152]{2,1,0:T(8,128)(2,1)S(1)}, bf16[2,32,1152]{2,1,0:T(8,128)(2,1)S(1)}) custom-call(bf16[1152,4096]{1,0:T(8,128)(2,1)} %bitcast.200, bf16[4,32,4096]{2,1,0:T(8,128)(2,1)S(1)} %constant_dynamic-update-slice_fusion.2.own_ref, ...), custom_call_target="tpu_custom_call" | custom-call | tf_op jit(solution)/shard_map/fc_backward/pallas_call | solution.py:319
  257.2 6.5 %collective-permute-start.40 = (bf16[2,32,1152]{2,1,0:T(8,128)(2,1)S(1)}, bf16[2,32,1152]{2,1,0:T(8,128)(2,1)S(1)}, u32[]{:S(2)}, u32[]{:S(2)}) collective-permute-start(bf16[2,32,1152]{2,1,0:T(8,128)(2,1)S(1)} %get-tuple-element.263), channel_id=1, source_target_pairs={{0,8},{4,12},{8,0},{12,4},{1,9},{5,13},{9,1},{13,5},{2,10},{6,14},... | collective-permute-start | bytes 442376 | tf_op jit(solution)/shard_map/ppermute | solution.py:27
  271.6 9.3 %collective-permute-done.40.refs_1_ = bf16[2,32,1152]{2,1,0:T(8,128)(2,1)S(1)} collective-permute-done((bf16[2,32,1152]{2,1,0:T(8,128)(2,1)S(1)}, bf16[2,32,1152]{2,1,0:T(8,128)(2,1)S(1)}, u32[]{:S(2)}, u32[]{:S(2)}) %collective-permute-start.40) | collective-permute-done | bytes 147488 | tf_op jit(solution)/shard_map/ppermute | solution.py:27
  283.3 7.4 %collective-permute-start.43 = (bf16[1,32,4096]{2,1,0:T(8,128)(2,1)S(1)}, bf16[1,32,4096]{2,1,0:T(8,128)(2,1)S(1)}, u32[]{:S(2)}, u32[]{:S(2)}) collective-permute-start(bf16[1,32,4096]{2,1,0:T(8,128)(2,1)S(1)} %get-tuple-element.261), channel_id=1, source_target_pairs={{0,8},{4,12},{8,0},{12,4},{1,9},{5,13},{9,1},{13,5},{2,10},{6,14},... | collective-permute-start | bytes 786440 | tf_op jit(solution)/shard_map/ppermute | solution.py:27
  295.6 6.6 %fc_backward.5 = (bf16[2,32,1152]{2,1,0:T(8,128)(2,1)S(1)}, bf16[2,32,1152]{2,1,0:T(8,128)(2,1)S(1)}, bf16[2,32,1152]{2,1,0:T(8,128)(2,1)S(1)}, bf16[2,32,1152]{2,1,0:T(8,128)(2,1)S(1)}) custom-call(bf16[1152,4096]{1,0:T(8,128)(2,1)} %bitcast.201, bf16[4,32,4096]{2,1,0:T(8,128)(2,1)S(1)} %constant_dynamic-update-slice_fusion.7.own_ref, ...), custom_call_target="tpu_custom_call" | custom-call | tf_op jit(solution)/shard_map/fc_backward/pallas_call | solution.py:319
  303.5 9.1 %collective-permute-done.44 = bf16[2,32,4096]{2,1,0:T(8,128)(2,1)S(1)} collective-permute-done((bf16[2,32,4096]{2,1,0:T(8,128)(2,1)S(1)}, bf16[2,32,4096]{2,1,0:T(8,128)(2,1)S(1)}, u32[]{:S(2)}, u32[]{:S(2)}) %collective-permute-start.44) | collective-permute-done | bytes 524320 | tf_op jit(solution)/shard_map/ppermute | solution.py:27
  325.7 13.3 %fusion.32 = f32[3,3,384,256]{3,2,1,0:T(8,128)} fusion(bf16[13,13,32,256]{3,2,1,0:T(8,128)(2,1)S(1)} %get-tuple-element.281, bf16[1,128,13,13,384]{4,1,3,2,0:T(8,128)(2,1)} %param.12), kind=kOutput, calls=%fused_computation.50 | convolution fusion | flops 8613003264 | bytes 10461184 | tf_op jit(solution)/shard_map/conv_general_dilated | solution.py:430
  339.1 6.5 %fc_backward.6 = (bf16[2,32,1152]{2,1,0:T(8,128)(2,1)S(1)}, bf16[2,32,1152]{2,1,0:T(8,128)(2,1)S(1)}, bf16[2,32,1152]{2,1,0:T(8,128)(2,1)S(1)}, bf16[2,32,1152]{2,1,0:T(8,128)(2,1)S(1)}) custom-call(bf16[1152,4096]{1,0:T(8,128)(2,1)} %bitcast.202, bf16[4,32,4096]{2,1,0:T(8,128)(2,1)S(1)} %constant_dynamic-update-slice_fusion.12.own_ref, ...), custom_call_target="tpu_custom_call" | custom-call | tf_op jit(solution)/shard_map/fc_backward/pallas_call | solution.py:319
  348.2 4.9 collective-permute-start.55
  355.4 14.8 %convert_dynamic-update-slice_fusion.3 = bf16[128,13,13,384]{3,0,2,1:T(8,128)(2,1)} fusion(bf16[128,13,13,384]{3,0,2,1:T(8,128)(2,1)} %bitcast.207, bf16[32,13,13,256]{3,0,2,1:T(8,128)(2,1)S(1)} %bitcast.195, bf16[1,3,3,384,256]{4,3,2,1,0:T(8,128)(2,1)S(1)} %copy-done), kind=kOutput, calls=%fused_computation.57 | convolution fusion | flops 8615079936 | bytes 8691712 | tf_op jit(solution)/shard_map/conv_general_dilated | solution.py:423
  376.3 14.2 %fusion.28 = f32[3,3,384,256]{3,2,1,0:T(8,128)} fusion(bf16[13,13,32,256]{3,2,1,0:T(8,128)(2,1)S(1)} %get-tuple-element.295, bf16[1,128,13,13,384]{4,1,3,2,0:T(8,128)(2,1)} %param.12), kind=kOutput, calls=%fused_computation.46 | convolution fusion | flops 8613003264 | bytes 10461184 | tf_op jit(solution)/shard_map/conv_general_dilated | solution.py:430
  394.8 6.7 %fc_backward.7 = (bf16[2,32,1152]{2,1,0:T(8,128)(2,1)S(1)}, bf16[2,32,1152]{2,1,0:T(8,128)(2,1)S(1)}, bf16[2,32,1152]{2,1,0:T(8,128)(2,1)S(1)}, bf16[2,32,1152]{2,1,0:T(8,128)(2,1)S(1)}) custom-call(bf16[1152,4096]{1,0:T(8,128)(2,1)} %bitcast.203, bf16[4,32,4096]{2,1,0:T(8,128)(2,1)S(1)} %constant_dynamic-update-slice_fusion.17.own_ref, ...), custom_call_target="tpu_custom_call" | custom-call | tf_op jit(solution)/shard_map/fc_backward/pallas_call | solution.py:319
  402.6 9.5 %convolution_convert_fusion = bf16[576,4096]{1,0:T(8,128)(2,1)} fusion(bf16[1024,4096]{1,0:T(8,128)(2,1)} %constant_dynamic-update-slice_fusion.24, pred[]{:T(512)S(6)} %eq.28, bf16[1024,1152]{1,0:T(8,128)(2,1)S(1)} %copy-done.56), kind=kOutput, calls=%fused_computation.5 | convolution fusion | flops 4834787328 | bytes 15728641 | tf_op jit(solution)/shard_map/dot_general | solution.py:620
  416.2 10.3 %collective-permute-start.65 = (bf16[576,4096]{1,0:T(8,128)(2,1)}, bf16[576,4096]{1,0:T(8,128)(2,1)}, u32[]{:S(2)}, u32[]{:S(2)}) collective-permute-start(bf16[576,4096]{1,0:T(8,128)(2,1)} %convolution_convert_fusion), channel_id=1, source_target_pairs={{0,1},{1,0},{2,3},{3,2},{4,5},{5,4},{6,7},{7,6},{8,9},{9,8},{10,11... | collective-permute-start | bytes 14155784 | tf_op jit(solution)/shard_map/ppermute | solution.py:22
  429.3 14.4 %fusion.24 = f32[3,3,384,256]{3,2,1,0:T(8,128)} fusion(bf16[13,13,32,256]{3,2,1,0:T(8,128)(2,1)S(1)} %get-tuple-element.308, bf16[1,128,13,13,384]{4,1,3,2,0:T(8,128)(2,1)} %param.12), kind=kOutput, calls=%fused_computation.42 | convolution fusion | flops 8613003264 | bytes 10461184 | tf_op jit(solution)/shard_map/conv_general_dilated | solution.py:430
  444.9 9.4 %convert_add_fusion = f32[576,4096]{1,0:T(8,128)} fusion(bf16[576,4096]{1,0:T(8,128)(2,1)} %collective-permute-done.65, bf16[1024,576]{1,0:T(8,128)(2,1)S(1)} %copy-done.54, bf16[1024,4096]{1,0:T(8,128)(2,1)S(1)} %bitcast.206), kind=kOutput, calls=%fused_computation | convolution fusion | flops 4836556800 | bytes 23724032 | tf_op jit(solution)/shard_map/dot_general | solution.py:625
  462.7 9.9 %collective-permute-done.66.back_ref = bf16[32,9216]{1,0:T(8,128)(2,1)S(1)} collective-permute-done((bf16[32,9216]{1,0:T(8,128)(2,1)}, bf16[32,9216]{1,0:T(8,128)(2,1)S(1)}, u32[]{:S(2)}, u32[]{:S(2)}) %collective-permute-start.66) | collective-permute-done | bytes 589856 | tf_op jit(solution)/shard_map/ppermute | solution.py:31
  477.4 14.3 %add_add_fusion = f32[3,3,384,256]{3,2,1,0:T(8,128)S(1)} fusion(f32[3,3,384,256]{3,2,1,0:T(8,128)} %fusion.24, f32[3,3,384,256]{3,2,1,0:T(8,128)S(1)} %copy-done.73, f32[3,3,384,256]{3,2,1,0:T(8,128)} %fusion.28, bf16[13,13,32,256]{3,2,1,0:T(8,128)(2,1)S(1)} %get-tuple-element.322, bf16[1,128,13,13,384]{4,1,3,2,0:T(8,128)(2,1)} %param.12), kind=kOutput, calls=%fused_computation.66 | convolution fusion | flops 8615657472 | bytes 21078016 | tf_op jit(solution)/shard_map/conv_general_dilated | solution.py:430
  500.3 14.8 %convert_dynamic-update-slice_fusion.2 = bf16[128,13,13,384]{3,0,2,1:T(8,128)(2,1)} fusion(bf16[128,13,13,384]{3,0,2,1:T(8,128)(2,1)} %convert_dynamic-update-slice_fusion.3, bf16[32,13,13,256]{3,0,2,1:T(8,128)(2,1)S(1)} %bitcast.192, bf16[1,3,3,384,256]{4,3,2,1,0:T(8,128)(2,1)S(1)} %copy-done), kind=kOutput, calls=%fused_computation.56 | convolution fusion | flops 8615079936 | bytes 8691712 | tf_op jit(solution)/shard_map/conv_general_dilated | solution.py:423
  518.9 15.1 %convert_dynamic-update-slice_fusion.1 = bf16[128,13,13,384]{3,0,2,1:T(8,128)(2,1)} fusion(bf16[128,13,13,384]{3,0,2,1:T(8,128)(2,1)} %convert_dynamic-update-slice_fusion.2, bf16[32,13,13,256]{3,0,2,1:T(8,128)(2,1)S(1)} %bitcast.193, bf16[1,3,3,384,256]{4,3,2,1,0:T(8,128)(2,1)S(1)} %copy-done), kind=kOutput, calls=%fused_computation.55 | convolution fusion | flops 8615079936 | bytes 8691712 | tf_op jit(solution)/shard_map/conv_general_dilated | solution.py:423
  537.7 15.1 %convert_dynamic-update-slice_fusion = bf16[128,13,13,384]{3,0,2,1:T(8,128)(2,1)} fusion(bf16[128,13,13,384]{3,0,2,1:T(8,128)(2,1)} %convert_dynamic-update-slice_fusion.1, bf16[32,13,13,256]{3,0,2,1:T(8,128)(2,1)S(1)} %bitcast.194, bf16[1,3,3,384,256]{4,3,2,1,0:T(8,128)(2,1)S(1)} %copy-done), kind=kOutput, calls=%fused_computation.54 | convolution fusion | flops 8615079936 | bytes 8691712 | tf_op jit(solution)/shard_map/conv_general_dilated | solution.py:423
  (462 shorter events, 226.1 us)
Async XLA Ops:
  7.2 85.7 %all-gather.3.cloned.1.call-start = ((), (), s32[]{:S(2)}) async-start(), calls=%async_computation | async-start | bytes 14155776 | tf_op jit(solution)/shard_map/all_gather | solution.py:495
  28.0 23.3 %collective-permute-start = (bf16[32,9216]{1,0:T(8,128)(2,1)S(1)}, bf16[32,9216]{1,0:T(8,128)(2,1)S(1)}, u32[]{:S(2)}, u32[]{:S(2)}) collective-permute-start(bf16[32,9216]{1,0:T(8,128)(2,1)S(1)} %get-tuple-element.180.pooled_ref), channel_id=1, source_target_pairs={{0,16},{16,0},{1,17},{17,1},{2,18},{18,2},{3,19},{19,3},{4,20},{20... | collective-permute-start | bytes 1769480 | tf_op jit(solution)/shard_map/ppermute | solution.py:31
  50.8 27.6 %collective-permute-start.5 = (bf16[32,9216]{1,0:T(8,128)(2,1)}, bf16[32,9216]{1,0:T(8,128)(2,1)}, u32[]{:S(2)}, u32[]{:S(2)}) collective-permute-start(bf16[32,9216]{1,0:T(8,128)(2,1)} %get-tuple-element.188.pooled_ref), channel_id=1, source_target_pairs={{0,16},{16,0},{1,17},{17,1},{2,18},{18,2},{3,19},{19,3},{4,20},{20... | collective-permute-start | bytes 1769480 | tf_op jit(solution)/shard_map/ppermute | solution.py:31
  52.1 24.8 %collective-permute-start.1 = (bf16[2,32,1152]{2,1,0:T(8,128)(2,1)S(1)}, bf16[2,32,1152]{2,1,0:T(8,128)(2,1)S(1)}, u32[]{:S(2)}, u32[]{:S(2)}) collective-permute-start(bf16[2,32,1152]{2,1,0:T(8,128)(2,1)S(1)} %get-tuple-element.185), channel_id=1, source_target_pairs={{0,8},{4,12},{8,0},{12,4},{1,9},{5,13},{9,1},{13,5},{2,10},{6,14},... | collective-permute-start | bytes 442376 | tf_op jit(solution)/shard_map/ppermute | solution.py:27
  54.6 22.3 %collective-permute-start.2 = (bf16[2,32,1152]{2,1,0:T(8,128)(2,1)S(1)}, bf16[2,32,1152]{2,1,0:T(8,128)(2,1)S(1)}, u32[]{:S(2)}, u32[]{:S(2)}) collective-permute-start(bf16[2,32,1152]{2,1,0:T(8,128)(2,1)S(1)} %get-tuple-element.186), channel_id=1, source_target_pairs={{0,4},{4,0},{8,12},{12,8},{1,5},{5,1},{9,13},{13,9},{2,6},{6,2},{1... | collective-permute-start | bytes 442376 | tf_op jit(solution)/shard_map/ppermute | solution.py:27
  76.0 29.6 %collective-permute-start.7 = (bf16[32,9216]{1,0:T(8,128)(2,1)S(1)}, bf16[32,9216]{1,0:T(8,128)(2,1)S(1)}, u32[]{:S(2)}, u32[]{:S(2)}) collective-permute-start(bf16[32,9216]{1,0:T(8,128)(2,1)S(1)} %get-tuple-element.193.pooled_ref), channel_id=1, source_target_pairs={{0,16},{16,0},{1,17},{17,1},{2,18},{18,2},{3,19},{19,3},{4,20},{20... | collective-permute-start | bytes 1769480 | tf_op jit(solution)/shard_map/ppermute | solution.py:31
  104.8 30.3 %collective-permute-start.6 = (bf16[4,32,4096]{2,1,0:T(8,128)(2,1)S(1)}, bf16[4,32,4096]{2,1,0:T(8,128)(2,1)S(1)}, u32[]{:S(2)}, u32[]{:S(2)}) collective-permute-start(bf16[4,32,4096]{2,1,0:T(8,128)(2,1)S(1)} %get-tuple-element.192), channel_id=1, source_target_pairs={{0,2},{2,0},{1,3},{3,1},{4,6},{6,4},{5,7},{7,5},{8,10},{10,8},{9,1... | collective-permute-start | bytes 3145736 | tf_op jit(solution)/shard_map/ppermute | solution.py:18
  107.6 31.1 %collective-permute-start.12 = (bf16[4,32,1152]{2,1,0:T(8,128)(2,1)S(1)}, bf16[4,32,1152]{2,1,0:T(8,128)(2,1)S(1)}, u32[]{:S(2)}, u32[]{:S(2)}) collective-permute-start(bf16[4,32,1152]{2,1,0:T(8,128)(2,1)S(1)} %pad_maximum_fusion.4), channel_id=1, source_target_pairs={{0,2},{2,0},{1,3},{3,1},{4,6},{6,4},{5,7},{7,5},{8,10},{10,8},{9,1... | collective-permute-start | bytes 884744 | tf_op jit(solution)/shard_map/ppermute | solution.py:18
  148.0 23.0 %collective-permute-start.19 = (bf16[4,32,4096]{2,1,0:T(8,128)(2,1)}, bf16[4,32,4096]{2,1,0:T(8,128)(2,1)}, u32[]{:S(2)}, u32[]{:S(2)}) collective-permute-start(bf16[4,32,4096]{2,1,0:T(8,128)(2,1)} %get-tuple-element.205), channel_id=1, source_target_pairs={{0,2},{2,0},{1,3},{3,1},{4,6},{6,4},{5,7},{7,5},{8,10},{10,8},{9,1... | collective-permute-start | bytes 3145736 | tf_op jit(solution)/shard_map/ppermute | solution.py:18
  150.0 34.5 %collective-permute-start.23 = (bf16[128,4096]{1,0:T(8,128)(2,1)}, bf16[128,4096]{1,0:T(8,128)(2,1)}, u32[]{:S(2)}, u32[]{:S(2)}) collective-permute-start(bf16[128,4096]{1,0:T(8,128)(2,1)} %multiply_convert_fusion), channel_id=1, source_target_pairs={{0,16},{16,0},{1,17},{17,1},{2,18},{18,2},{3,19},{19,3},{4,20},{20... | collective-permute-start | bytes 3145736 | tf_op jit(solution)/shard_map/ppermute | solution.py:31
  198.5 29.2 %collective-permute-start.30 = (bf16[4,32,4096]{2,1,0:T(8,128)(2,1)}, bf16[4,32,4096]{2,1,0:T(8,128)(2,1)S(1)}, u32[]{:S(2)}, u32[]{:S(2)}) collective-permute-start(bf16[4,32,4096]{2,1,0:T(8,128)(2,1)} %get-tuple-element.233), channel_id=1, source_target_pairs={{0,2},{2,0},{1,3},{3,1},{4,6},{6,4},{5,7},{7,5},{8,10},{10,8},{9,1... | collective-permute-start | bytes 3145736 | tf_op jit(solution)/shard_map/ppermute | solution.py:18
  205.9 22.6 %collective-permute-start.29 = (bf16[2,32,4096]{2,1,0:T(8,128)(2,1)S(1)}, bf16[2,32,4096]{2,1,0:T(8,128)(2,1)S(1)}, u32[]{:S(2)}, u32[]{:S(2)}) collective-permute-start(bf16[2,32,4096]{2,1,0:T(8,128)(2,1)S(1)} %get-tuple-element.236), channel_id=1, source_target_pairs={{0,4},{4,0},{8,12},{12,8},{1,5},{5,1},{9,13},{13,9},{2,6},{6,2},{1... | collective-permute-start | bytes 1572872 | tf_op jit(solution)/shard_map/ppermute | solution.py:27
  214.2 36.0 %collective-permute-start.35 = (bf16[4,32,4096]{2,1,0:T(8,128)(2,1)S(1)}, bf16[4,32,4096]{2,1,0:T(8,128)(2,1)S(1)}, u32[]{:S(2)}, u32[]{:S(2)}) collective-permute-start(bf16[4,32,4096]{2,1,0:T(8,128)(2,1)S(1)} %constant_dynamic-update-slice_fusion.2.own_ref), channel_id=1, source_target_pairs={{0,2},{2,0},{1,3},{3,1},{4,6},{6,4},{5,7},{7,5},{8,10},{10,8},{9,1... | collective-permute-start | bytes 3145736 | tf_op jit(solution)/shard_map/ppermute | solution.py:18
  228.8 28.3 %collective-permute-start.34 = (bf16[2,32,4096]{2,1,0:T(8,128)(2,1)S(1)}, bf16[2,32,4096]{2,1,0:T(8,128)(2,1)S(1)}, u32[]{:S(2)}, u32[]{:S(2)}) collective-permute-start(bf16[2,32,4096]{2,1,0:T(8,128)(2,1)S(1)} %get-tuple-element.377), channel_id=1, source_target_pairs={{0,4},{4,0},{8,12},{12,8},{1,5},{5,1},{9,13},{13,9},{2,6},{6,2},{1... | collective-permute-start | bytes 1572872 | tf_op jit(solution)/shard_map/ppermute | solution.py:27
  234.7 22.5 %collective-permute-start.32 = (bf16[1,32,4096]{2,1,0:T(8,128)(2,1)S(1)}, bf16[1,32,4096]{2,1,0:T(8,128)(2,1)S(1)}, u32[]{:S(2)}, u32[]{:S(2)}) collective-permute-start(bf16[1,32,4096]{2,1,0:T(8,128)(2,1)S(1)} %get-tuple-element.247), channel_id=1, source_target_pairs={{0,8},{4,12},{8,0},{12,4},{1,9},{5,13},{9,1},{13,5},{2,10},{6,14},... | collective-permute-start | bytes 786440 | tf_op jit(solution)/shard_map/ppermute | solution.py:27
  241.6 39.4 %collective-permute-start.37 = (bf16[1,32,4096]{2,1,0:T(8,128)(2,1)S(1)}, bf16[1,32,4096]{2,1,0:T(8,128)(2,1)S(1)}, u32[]{:S(2)}, u32[]{:S(2)}) collective-permute-start(bf16[1,32,4096]{2,1,0:T(8,128)(2,1)S(1)} %get-tuple-element.251), channel_id=1, source_target_pairs={{0,8},{4,12},{8,0},{12,4},{1,9},{5,13},{9,1},{13,5},{2,10},{6,14},... | collective-permute-start | bytes 786440 | tf_op jit(solution)/shard_map/ppermute | solution.py:27
  257.2 23.7 %collective-permute-start.40 = (bf16[2,32,1152]{2,1,0:T(8,128)(2,1)S(1)}, bf16[2,32,1152]{2,1,0:T(8,128)(2,1)S(1)}, u32[]{:S(2)}, u32[]{:S(2)}) collective-permute-start(bf16[2,32,1152]{2,1,0:T(8,128)(2,1)S(1)} %get-tuple-element.263), channel_id=1, source_target_pairs={{0,8},{4,12},{8,0},{12,4},{1,9},{5,13},{9,1},{13,5},{2,10},{6,14},... | collective-permute-start | bytes 442376 | tf_op jit(solution)/shard_map/ppermute | solution.py:27
  268.2 25.5 %collective-permute-start.39 = (bf16[1,32,4096]{2,1,0:T(8,128)(2,1)S(1)}, bf16[1,32,4096]{2,1,0:T(8,128)(2,1)S(1)}, u32[]{:S(2)}, u32[]{:S(2)}) collective-permute-start(bf16[1,32,4096]{2,1,0:T(8,128)(2,1)S(1)} %get-tuple-element.258), channel_id=1, source_target_pairs={{0,8},{4,12},{8,0},{12,4},{1,9},{5,13},{9,1},{13,5},{2,10},{6,14},... | collective-permute-start | bytes 786440 | tf_op jit(solution)/shard_map/ppermute | solution.py:27
  283.3 30.0 %collective-permute-start.43 = (bf16[1,32,4096]{2,1,0:T(8,128)(2,1)S(1)}, bf16[1,32,4096]{2,1,0:T(8,128)(2,1)S(1)}, u32[]{:S(2)}, u32[]{:S(2)}) collective-permute-start(bf16[1,32,4096]{2,1,0:T(8,128)(2,1)S(1)} %get-tuple-element.261), channel_id=1, source_target_pairs={{0,8},{4,12},{8,0},{12,4},{1,9},{5,13},{9,1},{13,5},{2,10},{6,14},... | collective-permute-start | bytes 786440 | tf_op jit(solution)/shard_map/ppermute | solution.py:27
  312.7 26.4 %collective-permute-start.52 = (bf16[4,32,4096]{2,1,0:T(8,128)(2,1)S(1)}, bf16[4,32,4096]{2,1,0:T(8,128)(2,1)S(1)}, u32[]{:S(2)}, u32[]{:S(2)}) collective-permute-start(bf16[4,32,4096]{2,1,0:T(8,128)(2,1)S(1)} %constant_dynamic-update-slice_fusion.12.own_ref), channel_id=1, source_target_pairs={{0,2},{2,0},{1,3},{3,1},{4,6},{6,4},{5,7},{7,5},{8,10},{10,8},{9,1... | collective-permute-start | bytes 3145736 | tf_op jit(solution)/shard_map/ppermute | solution.py:18
  319.7 28.4 %collective-permute-start.50 = (bf16[2,32,4096]{2,1,0:T(8,128)(2,1)}, bf16[2,32,4096]{2,1,0:T(8,128)(2,1)S(1)}, u32[]{:S(2)}, u32[]{:S(2)}) collective-permute-start(bf16[2,32,4096]{2,1,0:T(8,128)(2,1)} %get-tuple-element.369), channel_id=1, source_target_pairs={{0,4},{4,0},{8,12},{12,8},{1,5},{5,1},{9,13},{13,9},{2,6},{6,2},{1... | collective-permute-start | bytes 1572872 | tf_op jit(solution)/shard_map/ppermute | solution.py:27
  321.5 24.1 %collective-permute-start.51 = (bf16[4,32,1152]{2,1,0:T(8,128)(2,1)S(1)}, bf16[4,32,1152]{2,1,0:T(8,128)(2,1)S(1)}, u32[]{:S(2)}, u32[]{:S(2)}) collective-permute-start(bf16[4,32,1152]{2,1,0:T(8,128)(2,1)S(1)} %pad_maximum_fusion.8), channel_id=1, source_target_pairs={{0,2},{2,0},{1,3},{3,1},{4,6},{6,4},{5,7},{7,5},{8,10},{10,8},{9,1... | collective-permute-start | bytes 884744 | tf_op jit(solution)/shard_map/ppermute | solution.py:18
  322.1 136.9 %collective-permute-start.49 = (bf16[128,4096]{1,0:T(8,128)(2,1)}, bf16[128,4096]{1,0:T(8,128)(2,1)}, u32[]{:S(2)}, u32[]{:S(2)}) collective-permute-start(bf16[128,4096]{1,0:T(8,128)(2,1)} %pad_maximum_fusion), channel_id=1, source_target_pairs={{0,16},{16,0},{1,17},{17,1},{2,18},{18,2},{3,19},{19,3},{4,20},{20... | collective-permute-start | bytes 3145736 | tf_op jit(solution)/shard_map/ppermute | solution.py:31
  347.4 25.6 %collective-permute-start.59 = (bf16[32,9216]{1,0:T(8,128)(2,1)S(1)}, bf16[32,9216]{1,0:T(8,128)(2,1)S(1)}, u32[]{:S(2)}, u32[]{:S(2)}) collective-permute-start(bf16[32,9216]{1,0:T(8,128)(2,1)S(1)} %get-tuple-element.285), channel_id=1, source_target_pairs={{0,16},{16,0},{1,17},{17,1},{2,18},{18,2},{3,19},{19,3},{4,20},{20... | collective-permute-start | bytes 1769480 | tf_op jit(solution)/shard_map/ppermute | solution.py:31
  348.2 23.1 %collective-permute-start.55 = (bf16[2,32,1152]{2,1,0:T(8,128)(2,1)S(1)}, bf16[2,32,1152]{2,1,0:T(8,128)(2,1)S(1)}, u32[]{:S(2)}, u32[]{:S(2)}) collective-permute-start(bf16[2,32,1152]{2,1,0:T(8,128)(2,1)S(1)} %get-tuple-element.289), channel_id=1, source_target_pairs={{0,8},{4,12},{8,0},{12,4},{1,9},{5,13},{9,1},{13,5},{2,10},{6,14},... | collective-permute-start | bytes 442376 | tf_op jit(solution)/shard_map/ppermute | solution.py:27
  371.3 23.5 %collective-permute-start.54 = (bf16[4,32,4096]{2,1,0:T(8,128)(2,1)S(1)}, bf16[4,32,4096]{2,1,0:T(8,128)(2,1)S(1)}, u32[]{:S(2)}, u32[]{:S(2)}) collective-permute-start(bf16[4,32,4096]{2,1,0:T(8,128)(2,1)S(1)} %constant_dynamic-update-slice_fusion.17.own_ref), channel_id=1, source_target_pairs={{0,2},{2,0},{1,3},{3,1},{4,6},{6,4},{5,7},{7,5},{8,10},{10,8},{9,1... | collective-permute-start | bytes 3145736 | tf_op jit(solution)/shard_map/ppermute | solution.py:18
  371.8 21.8 %collective-permute-start.58 = (bf16[4,32,1152]{2,1,0:T(8,128)(2,1)S(1)}, bf16[4,32,1152]{2,1,0:T(8,128)(2,1)S(1)}, u32[]{:S(2)}, u32[]{:S(2)}) collective-permute-start(bf16[4,32,1152]{2,1,0:T(8,128)(2,1)S(1)} %pad_maximum_fusion.9), channel_id=1, source_target_pairs={{0,2},{2,0},{1,3},{3,1},{4,6},{6,4},{5,7},{7,5},{8,10},{10,8},{9,1... | collective-permute-start | bytes 884744 | tf_op jit(solution)/shard_map/ppermute | solution.py:18
  412.0 31.7 %collective-permute-start.61 = (bf16[2,32,1152]{2,1,0:T(8,128)(2,1)S(1)}, bf16[2,32,1152]{2,1,0:T(8,128)(2,1)S(1)}, u32[]{:S(2)}, u32[]{:S(2)}) collective-permute-start(bf16[2,32,1152]{2,1,0:T(8,128)(2,1)S(1)} %get-tuple-element.310), channel_id=1, source_target_pairs={{0,8},{4,12},{8,0},{12,4},{1,9},{5,13},{9,1},{13,5},{2,10},{6,14},... | collective-permute-start | bytes 442376 | tf_op jit(solution)/shard_map/ppermute | solution.py:27
  415.0 28.8 %collective-permute-start.62 = (bf16[2,32,1152]{2,1,0:T(8,128)(2,1)S(1)}, bf16[2,32,1152]{2,1,0:T(8,128)(2,1)S(1)}, u32[]{:S(2)}, u32[]{:S(2)}) collective-permute-start(bf16[2,32,1152]{2,1,0:T(8,128)(2,1)S(1)} %get-tuple-element.311), channel_id=1, source_target_pairs={{0,4},{4,0},{8,12},{12,8},{1,5},{5,1},{9,13},{13,9},{2,6},{6,2},{1... | collective-permute-start | bytes 442376 | tf_op jit(solution)/shard_map/ppermute | solution.py:27
  415.0 28.8 %collective-permute-start.63 = (bf16[2,32,1152]{2,1,0:T(8,128)(2,1)S(1)}, bf16[2,32,1152]{2,1,0:T(8,128)(2,1)S(1)}, u32[]{:S(2)}, u32[]{:S(2)}) collective-permute-start(bf16[2,32,1152]{2,1,0:T(8,128)(2,1)S(1)} %get-tuple-element.312), channel_id=1, source_target_pairs={{0,12},{4,8},{8,4},{12,0},{1,13},{5,9},{9,5},{13,1},{2,14},{6,10},... | collective-permute-start | bytes 442376 | tf_op jit(solution)/shard_map/ppermute | solution.py:27
  416.2 28.7 %collective-permute-start.65 = (bf16[576,4096]{1,0:T(8,128)(2,1)}, bf16[576,4096]{1,0:T(8,128)(2,1)}, u32[]{:S(2)}, u32[]{:S(2)}) collective-permute-start(bf16[576,4096]{1,0:T(8,128)(2,1)} %convolution_convert_fusion), channel_id=1, source_target_pairs={{0,1},{1,0},{2,3},{3,2},{4,5},{5,4},{6,7},{7,6},{8,9},{9,8},{10,11... | collective-permute-start | bytes 14155784 | tf_op jit(solution)/shard_map/ppermute | solution.py:22
  496.0 58.1 %collective-permute-start.77 = (f32[1,13056]{1,0:T(1,128)S(1)}, f32[1,13056]{1,0:T(1,128)S(1)}, u32[]{:S(2)}, u32[]{:S(2)}) collective-permute-start(f32[1,13056]{1,0:T(1,128)S(1)} %broadcast_in_dim.16), channel_id=1, source_target_pairs={{0,2},{2,0},{1,3},{3,1},{4,6},{6,4},{5,7},{7,5},{8,10},{10,8},{9,1... | collective-permute-start | bytes 156680 | tf_op jit(solution)/shard_map/ppermute | solution.py:18
  (128 other events, 1552.6 us)
Sparse Core Ops, SparseCore 0:
  9.6 24.2 all-gather.2

commit v5 on v4

--- a/solution.py
+++ b/solution.py
@@ -7,7 +7,7 @@
 from jax.experimental.pallas import tpu as pltpu
 from jax.sharding import PartitionSpec as P
 
-PLAN = "0102010213012301320130210321301230210231S021302123W23W3S3AA1A2A3AAA"
+PLAN = ("0102010213012301320130210231301230210231", "S021302123W23W3S3AA1A2A3AAA")
 BF16 = jnp.bfloat16
 F32 = jnp.float32
 CONV_DIMS = ("NHWC", "HWIO", "NHWC")
@@ -630,7 +630,7 @@
 
     runs = {str(n): chunk(n) for n in range(len(sizes))}
     runs.update(W=fc_weight_gradient(), S=stitch(), A=kernel_sum())
-    for n in PLAN if len(sizes) > 1 else "0" * (2 * hops + 6) + "WS" + "0" * 4 + "AA0" + "WS" + "A" * 5:
+    for n in "".join(PLAN) if len(sizes) > 1 else "0" * (2 * hops + 6) + "WS" + "0" * 4 + "AA0" + "WS" + "A" * 5:
         next(runs[n], None)
     grad_fc_weight = stage["gradient"]
     conv_bias_sum, fc_bias_sum = sums["conv_bias"], sums["fc_bias"]

time: 597 us -> 593 us (level)
  waiting for transfers between devices: 78.6 us -> 70.9 us
    ppermute x48, starting transfers between devices: 81.3 us -> 62.8 us  [swap_outer(): return lax.ppermute(block, 'outer', [(i, i ^ mask) for i in range(count)])]
    ppermute x19, starting transfers between devices: 14.4 us -> 30.1 us  [swap_core(): return lax.ppermute(block, 'core', [(0, 1), (1, 0)])]
    ppermute x19, waiting for transfers between devices: 22.7 us -> 8.92 us  [swap_core(): return lax.ppermute(block, 'core', [(0, 1), (1, 0)])]
    ppermute x48, waiting for transfers between devices: 43 us -> 49.6 us  [swap_outer(): return lax.ppermute(block, 'outer', [(i, i ^ mask) for i in range(count)])]
    unnamed x185 -> x188, local copies, waits for them, and re-layouts: 32.9 us -> 36.1 us
  transfers between devices with their start and end apart: 82 -> 82, of which waited for: 23 -> 21; matrix products, arithmetic and copies ran while one was open for 40% -> 40% of each run, Pallas kernels for 16% -> 16%
where the time goes in v5:
time: 593 us; the launch traced here: 582 us
  matrix products  208 us (35%)
  starting transfers between devices  123 us (21%)
  Pallas kernels  98.5 us (17%)
  waiting for transfers between devices  70.9 us (12%)
  local copies, waits for them, and re-layouts  46.3 us (8%)
  other arithmetic  18.6 us (3%)
  between operations  16 us (3%)
    conv_general_dilated x4, matrix products, conv_forward(): lax.conv_general_dilated(inputs, kernel, (1, 1), ((1, 1), (1, 1)), dimens...  72.6 us
    ppermute x48, starting transfers between devices, swap_outer(): return lax.ppermute(block, 'outer', [(i, i ^ mask) for i in range(count)])  62.8 us
    conv_general_dilated x4, matrix products, conv_grad_inputs(): lax.conv_general_dilated(grad_pre, turned, (1, 1), ((1, 1), (1, 1)), dime...  59.9 us
    conv_general_dilated x4, matrix products, conv_grad_kernel(): lax.conv_general_dilated(inputs, grad_pre, (1, 1), ((1, 1), (1, 1)), dime...  56.3 us
    ppermute x48, waiting for transfers between devices, swap_outer(): return lax.ppermute(block, 'outer', [(i, i ^ mask) for i in range(count)])  49.6 us
    unnamed x188, local copies, waits for them, and re-layouts  36.1 us
    ppermute x19, starting transfers between devices, swap_core(): return lax.ppermute(block, 'core', [(0, 1), (1, 0)])  30.1 us
    pallas_call x4, Pallas kernels, fc_backward(): pl.pallas_call(functools.partial(fc_back_kernel, count), grid=(depth // t...  26.3 us
  transfers between devices with their start and end apart: 82, of which 21 were waited for; matrix products, arithmetic and copies ran while one was open for 40% of the time, Pallas kernels for 16%

profile of v5, /device:TPU:1, one launch (start us, length us, event | category | flops | bytes accessed | tf_op | source)
XLA Modules:
  0.0 581.5 jit_solution(17057687680048457951)
XLA Ops:
  8.7 18.4 %fusion.3 = (bf16[13,13,32,256]{3,2,1,0:T(8,128)(2,1)}, bf16[13,13,32,256]{3,2,1,0:T(8,128)(2,1)S(1)}) fusion(f32[256]{0:T(256)S(1)} %bitcast.228, bf16[1,3,3,384,256]{4,3,2,1,0:T(8,128)(2,1)S(1)} %copy-done, bf16[1,128,13,13,384]{4,1,3,2,0:T(8,128)(2,1)} %param.12), kind=kOutput, calls=%fused_computation.9 | convolution fusion | flops 8639307776 | bytes 11461632 | tf_op jit(solution)/shard_map/conv_general_dilated | solution.py:413
  30.1 18.1 %fusion.7 = (bf16[13,13,32,256]{3,2,1,0:T(8,128)(2,1)}, bf16[13,13,32,256]{3,2,1,0:T(8,128)(2,1)S(1)}) fusion(f32[256]{0:T(256)S(1)} %bitcast.229, bf16[1,3,3,384,256]{4,3,2,1,0:T(8,128)(2,1)S(1)} %copy-done, bf16[1,128,13,13,384]{4,1,3,2,0:T(8,128)(2,1)} %param.12), kind=kOutput, calls=%fused_computation.13 | convolution fusion | flops 8639307776 | bytes 11461632 | tf_op jit(solution)/shard_map/conv_general_dilated | solution.py:413
  55.9 18.1 %fusion.11 = (bf16[13,13,32,256]{3,2,1,0:T(8,128)(2,1)}, bf16[13,13,32,256]{3,2,1,0:T(8,128)(2,1)S(1)}) fusion(f32[256]{0:T(256)S(1)} %bitcast.230, bf16[1,3,3,384,256]{4,3,2,1,0:T(8,128)(2,1)S(1)} %copy-done, bf16[1,128,13,13,384]{4,1,3,2,0:T(8,128)(2,1)} %param.12), kind=kOutput, calls=%fused_computation.17 | convolution fusion | flops 8639307776 | bytes 11461632 | tf_op jit(solution)/shard_map/conv_general_dilated | solution.py:413
  97.5 6.3 %fc_forward.4 = (f32[4,32,4096]{2,1,0:T(8,128)S(1)}, bf16[4,32,4096]{2,1,0:T(8,128)(2,1)S(1)}, bf16[256,1152]{1,0:T(8,128)(2,1)S(1)}) custom-call(bf16[1152,4096]{1,0:T(8,128)(2,1)} %bitcast.196, bf16[4,32,1152]{2,1,0:T(8,128)(2,1)S(1)} %copy-done.48, bf16[2,32,1152]{2,1,0:T(8,128)(2,1)S(1)} %copy-done.40, bf16[2,32,1152]{2,1,0:T(8,128)(2,1)S(1)} %copy-done.42, ...), custom_call_target="tpu_custom_call" | custom-call | tf_op jit(solution)/shard_map/fc_forward/pallas_call | solution.py:272
  108.2 18.1 %fusion.15 = (bf16[13,13,32,256]{3,2,1,0:T(8,128)(2,1)}, bf16[13,13,32,256]{3,2,1,0:T(8,128)(2,1)S(1)}) fusion(f32[256]{0:T(256)S(1)} %bitcast.231, bf16[1,3,3,384,256]{4,3,2,1,0:T(8,128)(2,1)S(1)} %copy-done, bf16[1,128,13,13,384]{4,1,3,2,0:T(8,128)(2,1)} %param.12), kind=kOutput, calls=%fused_computation.21 | convolution fusion | flops 8639307776 | bytes 11461632 | tf_op jit(solution)/shard_map/conv_general_dilated | solution.py:413
  128.9 4.3 collective-permute-start.13
  138.7 7.1 %fc_forward.5 = (f32[4,32,4096]{2,1,0:T(8,128)S(1)}, bf16[4,32,4096]{2,1,0:T(8,128)(2,1)}, bf16[256,1152]{1,0:T(8,128)(2,1)S(1)}) custom-call(bf16[1152,4096]{1,0:T(8,128)(2,1)} %bitcast.197, bf16[4,32,1152]{2,1,0:T(8,128)(2,1)S(1)} %collective-permute-done.12.got_ref, bf16[2,32,1152]{2,1,0:T(8,128)(2,1)S(1)} %copy-done.32, ...), custom_call_target="tpu_custom_call" | custom-call | tf_op jit(solution)/shard_map/fc_forward/pallas_call | solution.py:272
  176.8 6.5 %fc_forward.6 = (f32[4,32,4096]{2,1,0:T(8,128)S(1)}, bf16[4,32,4096]{2,1,0:T(8,128)(2,1)S(1)}, bf16[256,1152]{1,0:T(8,128)(2,1)S(1)}) custom-call(bf16[1152,4096]{1,0:T(8,128)(2,1)} %bitcast.198, bf16[4,32,1152]{2,1,0:T(8,128)(2,1)S(1)} %collective-permute-done.18.got_ref, bf16[2,32,1152]{2,1,0:T(8,128)(2,1)S(1)} %copy-done.30, ...), custom_call_target="tpu_custom_call" | custom-call | tf_op jit(solution)/shard_map/fc_forward/pallas_call | solution.py:272
  191.4 6.3 %fc_forward.7 = (f32[4,32,4096]{2,1,0:T(8,128)S(1)}, bf16[4,32,4096]{2,1,0:T(8,128)(2,1)S(1)}, bf16[256,1152]{1,0:T(8,128)(2,1)S(1)}) custom-call(bf16[1152,4096]{1,0:T(8,128)(2,1)} %bitcast.199, bf16[4,32,1152]{2,1,0:T(8,128)(2,1)S(1)} %collective-permute-done.28.got_ref, bf16[2,32,1152]{2,1,0:T(8,128)(2,1)S(1)} %get-tuple-element.218.refs_0_, ...), custom_call_target="tpu_custom_call" | custom-call | tf_op jit(solution)/shard_map/fc_forward/pallas_call | solution.py:272
  208.6 4.1 collective-permute-start.32
  214.5 11.1 %collective-permute-done.29.came_ref = bf16[2,32,4096]{2,1,0:T(8,128)(2,1)S(1)} collective-permute-done((bf16[2,32,4096]{2,1,0:T(8,128)(2,1)S(1)}, bf16[2,32,4096]{2,1,0:T(8,128)(2,1)S(1)}, u32[]{:S(2)}, u32[]{:S(2)}) %collective-permute-start.29) | collective-permute-done | bytes 524320 | tf_op jit(solution)/shard_map/ppermute | solution.py:27
  235.3 7.9 %collective-permute-done.36.came_ref = bf16[2,32,4096]{2,1,0:T(8,128)(2,1)S(1)} collective-permute-done((bf16[2,32,4096]{2,1,0:T(8,128)(2,1)S(1)}, bf16[2,32,4096]{2,1,0:T(8,128)(2,1)S(1)}, u32[]{:S(2)}, u32[]{:S(2)}) %collective-permute-start.36) | collective-permute-done | bytes 524320 | tf_op jit(solution)/shard_map/ppermute | solution.py:27
  245.5 4.1 collective-permute-done.35.came_ref
  249.5 6.5 %fc_backward.4 = (bf16[2,32,1152]{2,1,0:T(8,128)(2,1)S(1)}, bf16[2,32,1152]{2,1,0:T(8,128)(2,1)S(1)}, bf16[2,32,1152]{2,1,0:T(8,128)(2,1)S(1)}, bf16[2,32,1152]{2,1,0:T(8,128)(2,1)S(1)}) custom-call(bf16[1152,4096]{1,0:T(8,128)(2,1)} %bitcast.200, bf16[4,32,4096]{2,1,0:T(8,128)(2,1)S(1)} %constant_dynamic-update-slice_fusion.2.own_ref, ...), custom_call_target="tpu_custom_call" | custom-call | tf_op jit(solution)/shard_map/fc_backward/pallas_call | solution.py:319
  273.8 15.7 %collective-permute-start.45 = (bf16[4,32,1152]{2,1,0:T(8,128)(2,1)S(1)}, bf16[4,32,1152]{2,1,0:T(8,128)(2,1)S(1)}, u32[]{:S(2)}, u32[]{:S(2)}) collective-permute-start(bf16[4,32,1152]{2,1,0:T(8,128)(2,1)S(1)} %pad_maximum_fusion.7), channel_id=1, source_target_pairs={{0,2},{2,0},{1,3},{3,1},{4,6},{6,4},{5,7},{7,5},{8,10},{10,8},{9,1... | collective-permute-start | bytes 884744 | tf_op jit(solution)/shard_map/ppermute | solution.py:18
  293.3 6.6 %fc_backward.5 = (bf16[2,32,1152]{2,1,0:T(8,128)(2,1)S(1)}, bf16[2,32,1152]{2,1,0:T(8,128)(2,1)S(1)}, bf16[2,32,1152]{2,1,0:T(8,128)(2,1)S(1)}, bf16[2,32,1152]{2,1,0:T(8,128)(2,1)S(1)}) custom-call(bf16[1152,4096]{1,0:T(8,128)(2,1)} %bitcast.201, bf16[4,32,4096]{2,1,0:T(8,128)(2,1)S(1)} %constant_dynamic-update-slice_fusion.7.own_ref, ...), custom_call_target="tpu_custom_call" | custom-call | tf_op jit(solution)/shard_map/fc_backward/pallas_call | solution.py:319
  306.4 4.5 collective-permute-start.46
  321.8 13.4 %fusion.32 = f32[3,3,384,256]{3,2,1,0:T(8,128)} fusion(bf16[13,13,32,256]{3,2,1,0:T(8,128)(2,1)S(1)} %get-tuple-element.281, bf16[1,128,13,13,384]{4,1,3,2,0:T(8,128)(2,1)} %param.12), kind=kOutput, calls=%fused_computation.50 | convolution fusion | flops 8613003264 | bytes 10461184 | tf_op jit(solution)/shard_map/conv_general_dilated | solution.py:430
  335.2 6.5 %fc_backward.6 = (bf16[2,32,1152]{2,1,0:T(8,128)(2,1)S(1)}, bf16[2,32,1152]{2,1,0:T(8,128)(2,1)S(1)}, bf16[2,32,1152]{2,1,0:T(8,128)(2,1)S(1)}, bf16[2,32,1152]{2,1,0:T(8,128)(2,1)S(1)}) custom-call(bf16[1152,4096]{1,0:T(8,128)(2,1)} %bitcast.202, bf16[4,32,4096]{2,1,0:T(8,128)(2,1)S(1)} %constant_dynamic-update-slice_fusion.12.own_ref, ...), custom_call_target="tpu_custom_call" | custom-call | tf_op jit(solution)/shard_map/fc_backward/pallas_call | solution.py:319
  349.8 14.8 %convert_dynamic-update-slice_fusion.3 = bf16[128,13,13,384]{3,0,2,1:T(8,128)(2,1)} fusion(bf16[128,13,13,384]{3,0,2,1:T(8,128)(2,1)} %bitcast.207, bf16[32,13,13,256]{3,0,2,1:T(8,128)(2,1)S(1)} %bitcast.195, bf16[1,3,3,384,256]{4,3,2,1,0:T(8,128)(2,1)S(1)} %copy-done), kind=kOutput, calls=%fused_computation.57 | convolution fusion | flops 8615079936 | bytes 8691712 | tf_op jit(solution)/shard_map/conv_general_dilated | solution.py:423
  370.7 14.2 %fusion.28 = f32[3,3,384,256]{3,2,1,0:T(8,128)} fusion(bf16[13,13,32,256]{3,2,1,0:T(8,128)(2,1)S(1)} %get-tuple-element.295, bf16[1,128,13,13,384]{4,1,3,2,0:T(8,128)(2,1)} %param.12), kind=kOutput, calls=%fused_computation.46 | convolution fusion | flops 8613003264 | bytes 10461184 | tf_op jit(solution)/shard_map/conv_general_dilated | solution.py:430
  386.1 6.7 %fc_backward.7 = (bf16[2,32,1152]{2,1,0:T(8,128)(2,1)S(1)}, bf16[2,32,1152]{2,1,0:T(8,128)(2,1)S(1)}, bf16[2,32,1152]{2,1,0:T(8,128)(2,1)S(1)}, bf16[2,32,1152]{2,1,0:T(8,128)(2,1)S(1)}) custom-call(bf16[1152,4096]{1,0:T(8,128)(2,1)} %bitcast.203, bf16[4,32,4096]{2,1,0:T(8,128)(2,1)S(1)} %constant_dynamic-update-slice_fusion.17.own_ref, ...), custom_call_target="tpu_custom_call" | custom-call | tf_op jit(solution)/shard_map/fc_backward/pallas_call | solution.py:319
  393.9 9.6 %convolution_convert_fusion = bf16[576,4096]{1,0:T(8,128)(2,1)} fusion(bf16[1024,4096]{1,0:T(8,128)(2,1)} %constant_dynamic-update-slice_fusion.24, pred[]{:T(512)S(6)} %eq.28, bf16[1024,1152]{1,0:T(8,128)(2,1)S(1)} %copy-done.57), kind=kOutput, calls=%fused_computation.5 | convolution fusion | flops 4834787328 | bytes 15728641 | tf_op jit(solution)/shard_map/dot_general | solution.py:620
  407.0 15.8 %collective-permute-start.65 = (bf16[576,4096]{1,0:T(8,128)(2,1)}, bf16[576,4096]{1,0:T(8,128)(2,1)}, u32[]{:S(2)}, u32[]{:S(2)}) collective-permute-start(bf16[576,4096]{1,0:T(8,128)(2,1)} %convolution_convert_fusion), channel_id=1, source_target_pairs={{0,1},{1,0},{2,3},{3,2},{4,5},{5,4},{6,7},{7,6},{8,9},{9,8},{10,11... | collective-permute-start | bytes 14155784 | tf_op jit(solution)/shard_map/ppermute | solution.py:22
  425.6 14.4 %fusion.24 = f32[3,3,384,256]{3,2,1,0:T(8,128)} fusion(bf16[13,13,32,256]{3,2,1,0:T(8,128)(2,1)S(1)} %get-tuple-element.308, bf16[1,128,13,13,384]{4,1,3,2,0:T(8,128)(2,1)} %param.12), kind=kOutput, calls=%fused_computation.42 | convolution fusion | flops 8613003264 | bytes 10461184 | tf_op jit(solution)/shard_map/conv_general_dilated | solution.py:430
  441.4 9.4 %convert_add_fusion = f32[576,4096]{1,0:T(8,128)} fusion(bf16[576,4096]{1,0:T(8,128)(2,1)} %collective-permute-done.65, bf16[1024,576]{1,0:T(8,128)(2,1)S(1)} %broadcast_select_fusion, bf16[1024,4096]{1,0:T(8,128)(2,1)S(1)} %bitcast.206), kind=kOutput, calls=%fused_computation | convolution fusion | flops 4836556800 | bytes 23724032 | tf_op jit(solution)/shard_map/dot_general | solution.py:625
  460.1 9.1 %collective-permute-done.66.back_ref = bf16[32,9216]{1,0:T(8,128)(2,1)S(1)} collective-permute-done((bf16[32,9216]{1,0:T(8,128)(2,1)}, bf16[32,9216]{1,0:T(8,128)(2,1)S(1)}, u32[]{:S(2)}, u32[]{:S(2)}) %collective-permute-start.66) | collective-permute-done | bytes 589856 | tf_op jit(solution)/shard_map/ppermute | solution.py:31
  474.1 14.4 %add_add_fusion = f32[3,3,384,256]{3,2,1,0:T(8,128)S(1)} fusion(f32[3,3,384,256]{3,2,1,0:T(8,128)} %fusion.24, f32[3,3,384,256]{3,2,1,0:T(8,128)S(1)} %copy-done.74, f32[3,3,384,256]{3,2,1,0:T(8,128)} %fusion.28, bf16[13,13,32,256]{3,2,1,0:T(8,128)(2,1)S(1)} %get-tuple-element.322, bf16[1,128,13,13,384]{4,1,3,2,0:T(8,128)(2,1)} %param.12), kind=kOutput, calls=%fused_computation.66 | convolution fusion | flops 8615657472 | bytes 21078016 | tf_op jit(solution)/shard_map/conv_general_dilated | solution.py:430
  496.7 14.8 %convert_dynamic-update-slice_fusion.2 = bf16[128,13,13,384]{3,0,2,1:T(8,128)(2,1)} fusion(bf16[128,13,13,384]{3,0,2,1:T(8,128)(2,1)} %convert_dynamic-update-slice_fusion.3, bf16[32,13,13,256]{3,0,2,1:T(8,128)(2,1)S(1)} %bitcast.192, bf16[1,3,3,384,256]{4,3,2,1,0:T(8,128)(2,1)S(1)} %copy-done), kind=kOutput, calls=%fused_computation.56 | convolution fusion | flops 8615079936 | bytes 8691712 | tf_op jit(solution)/shard_map/conv_general_dilated | solution.py:423
  515.3 15.1 %convert_dynamic-update-slice_fusion.1 = bf16[128,13,13,384]{3,0,2,1:T(8,128)(2,1)} fusion(bf16[128,13,13,384]{3,0,2,1:T(8,128)(2,1)} %convert_dynamic-update-slice_fusion.2, bf16[32,13,13,256]{3,0,2,1:T(8,128)(2,1)S(1)} %bitcast.193, bf16[1,3,3,384,256]{4,3,2,1,0:T(8,128)(2,1)S(1)} %copy-done), kind=kOutput, calls=%fused_computation.55 | convolution fusion | flops 8615079936 | bytes 8691712 | tf_op jit(solution)/shard_map/conv_general_dilated | solution.py:423
  534.1 15.1 %convert_dynamic-update-slice_fusion = bf16[128,13,13,384]{3,0,2,1:T(8,128)(2,1)} fusion(bf16[128,13,13,384]{3,0,2,1:T(8,128)(2,1)} %convert_dynamic-update-slice_fusion.1, bf16[32,13,13,256]{3,0,2,1:T(8,128)(2,1)S(1)} %bitcast.194, bf16[1,3,3,384,256]{4,3,2,1,0:T(8,128)(2,1)S(1)} %copy-done), kind=kOutput, calls=%fused_computation.54 | convolution fusion | flops 8615079936 | bytes 8691712 | tf_op jit(solution)/shard_map/conv_general_dilated | solution.py:423
  558.4 4.6 collective-permute-done.80
  (464 shorter events, 224.0 us)
Async XLA Ops:
  7.2 85.7 %all-gather.3.cloned.1.call-start = ((), (), s32[]{:S(2)}) async-start(), calls=%async_computation | async-start | bytes 14155776 | tf_op jit(solution)/shard_map/all_gather | solution.py:495
  27.9 23.3 %collective-permute-start = (bf16[32,9216]{1,0:T(8,128)(2,1)S(1)}, bf16[32,9216]{1,0:T(8,128)(2,1)S(1)}, u32[]{:S(2)}, u32[]{:S(2)}) collective-permute-start(bf16[32,9216]{1,0:T(8,128)(2,1)S(1)} %get-tuple-element.180.pooled_ref), channel_id=1, source_target_pairs={{0,16},{16,0},{1,17},{17,1},{2,18},{18,2},{3,19},{19,3},{4,20},{20... | collective-permute-start | bytes 1769480 | tf_op jit(solution)/shard_map/ppermute | solution.py:31
  50.8 27.6 %collective-permute-start.5 = (bf16[32,9216]{1,0:T(8,128)(2,1)}, bf16[32,9216]{1,0:T(8,128)(2,1)}, u32[]{:S(2)}, u32[]{:S(2)}) collective-permute-start(bf16[32,9216]{1,0:T(8,128)(2,1)} %get-tuple-element.188.pooled_ref), channel_id=1, source_target_pairs={{0,16},{16,0},{1,17},{17,1},{2,18},{18,2},{3,19},{19,3},{4,20},{20... | collective-permute-start | bytes 1769480 | tf_op jit(solution)/shard_map/ppermute | solution.py:31
  52.1 24.7 %collective-permute-start.1 = (bf16[2,32,1152]{2,1,0:T(8,128)(2,1)S(1)}, bf16[2,32,1152]{2,1,0:T(8,128)(2,1)S(1)}, u32[]{:S(2)}, u32[]{:S(2)}) collective-permute-start(bf16[2,32,1152]{2,1,0:T(8,128)(2,1)S(1)} %get-tuple-element.185), channel_id=1, source_target_pairs={{0,8},{4,12},{8,0},{12,4},{1,9},{5,13},{9,1},{13,5},{2,10},{6,14},... | collective-permute-start | bytes 442376 | tf_op jit(solution)/shard_map/ppermute | solution.py:27
  54.6 22.2 %collective-permute-start.2 = (bf16[2,32,1152]{2,1,0:T(8,128)(2,1)S(1)}, bf16[2,32,1152]{2,1,0:T(8,128)(2,1)S(1)}, u32[]{:S(2)}, u32[]{:S(2)}) collective-permute-start(bf16[2,32,1152]{2,1,0:T(8,128)(2,1)S(1)} %get-tuple-element.186), channel_id=1, source_target_pairs={{0,4},{4,0},{8,12},{12,8},{1,5},{5,1},{9,13},{13,9},{2,6},{6,2},{1... | collective-permute-start | bytes 442376 | tf_op jit(solution)/shard_map/ppermute | solution.py:27
  55.9 21.0 %collective-permute-start.3 = (bf16[2,32,1152]{2,1,0:T(8,128)(2,1)S(1)}, bf16[2,32,1152]{2,1,0:T(8,128)(2,1)S(1)}, u32[]{:S(2)}, u32[]{:S(2)}) collective-permute-start(bf16[2,32,1152]{2,1,0:T(8,128)(2,1)S(1)} %get-tuple-element.187), channel_id=1, source_target_pairs={{0,12},{4,8},{8,4},{12,0},{1,13},{5,9},{9,5},{13,1},{2,14},{6,10},... | collective-permute-start | bytes 442376 | tf_op jit(solution)/shard_map/ppermute | solution.py:27
  75.9 29.6 %collective-permute-start.7 = (bf16[32,9216]{1,0:T(8,128)(2,1)S(1)}, bf16[32,9216]{1,0:T(8,128)(2,1)S(1)}, u32[]{:S(2)}, u32[]{:S(2)}) collective-permute-start(bf16[32,9216]{1,0:T(8,128)(2,1)S(1)} %get-tuple-element.193.pooled_ref), channel_id=1, source_target_pairs={{0,16},{16,0},{1,17},{17,1},{2,18},{18,2},{3,19},{19,3},{4,20},{20... | collective-permute-start | bytes 1769480 | tf_op jit(solution)/shard_map/ppermute | solution.py:31
  104.7 30.3 %collective-permute-start.6 = (bf16[4,32,4096]{2,1,0:T(8,128)(2,1)S(1)}, bf16[4,32,4096]{2,1,0:T(8,128)(2,1)S(1)}, u32[]{:S(2)}, u32[]{:S(2)}) collective-permute-start(bf16[4,32,4096]{2,1,0:T(8,128)(2,1)S(1)} %get-tuple-element.192), channel_id=1, source_target_pairs={{0,2},{2,0},{1,3},{3,1},{4,6},{6,4},{5,7},{7,5},{8,10},{10,8},{9,1... | collective-permute-start | bytes 3145736 | tf_op jit(solution)/shard_map/ppermute | solution.py:18
  107.5 31.1 %collective-permute-start.12 = (bf16[4,32,1152]{2,1,0:T(8,128)(2,1)S(1)}, bf16[4,32,1152]{2,1,0:T(8,128)(2,1)S(1)}, u32[]{:S(2)}, u32[]{:S(2)}) collective-permute-start(bf16[4,32,1152]{2,1,0:T(8,128)(2,1)S(1)} %pad_maximum_fusion.4), channel_id=1, source_target_pairs={{0,2},{2,0},{1,3},{3,1},{4,6},{6,4},{5,7},{7,5},{8,10},{10,8},{9,1... | collective-permute-start | bytes 884744 | tf_op jit(solution)/shard_map/ppermute | solution.py:18
  128.9 21.0 %collective-permute-start.13 = (bf16[2,32,1152]{2,1,0:T(8,128)(2,1)S(1)}, bf16[2,32,1152]{2,1,0:T(8,128)(2,1)}, u32[]{:S(2)}, u32[]{:S(2)}) collective-permute-start(bf16[2,32,1152]{2,1,0:T(8,128)(2,1)S(1)} %get-tuple-element.207), channel_id=1, source_target_pairs={{0,8},{4,12},{8,0},{12,4},{1,9},{5,13},{9,1},{13,5},{2,10},{6,14},... | collective-permute-start | bytes 442376 | tf_op jit(solution)/shard_map/ppermute | solution.py:27
  148.0 23.0 %collective-permute-start.19 = (bf16[4,32,4096]{2,1,0:T(8,128)(2,1)}, bf16[4,32,4096]{2,1,0:T(8,128)(2,1)}, u32[]{:S(2)}, u32[]{:S(2)}) collective-permute-start(bf16[4,32,4096]{2,1,0:T(8,128)(2,1)} %get-tuple-element.205), channel_id=1, source_target_pairs={{0,2},{2,0},{1,3},{3,1},{4,6},{6,4},{5,7},{7,5},{8,10},{10,8},{9,1... | collective-permute-start | bytes 3145736 | tf_op jit(solution)/shard_map/ppermute | solution.py:18
  150.0 33.8 %collective-permute-start.23 = (bf16[128,4096]{1,0:T(8,128)(2,1)}, bf16[128,4096]{1,0:T(8,128)(2,1)}, u32[]{:S(2)}, u32[]{:S(2)}) collective-permute-start(bf16[128,4096]{1,0:T(8,128)(2,1)} %multiply_convert_fusion), channel_id=1, source_target_pairs={{0,16},{16,0},{1,17},{17,1},{2,18},{18,2},{3,19},{19,3},{4,20},{20... | collective-permute-start | bytes 3145736 | tf_op jit(solution)/shard_map/ppermute | solution.py:31
  183.3 21.3 %collective-permute-start.26 = (bf16[4,32,4096]{2,1,0:T(8,128)(2,1)S(1)}, bf16[4,32,4096]{2,1,0:T(8,128)(2,1)S(1)}, u32[]{:S(2)}, u32[]{:S(2)}) collective-permute-start(bf16[4,32,4096]{2,1,0:T(8,128)(2,1)S(1)} %get-tuple-element.223), channel_id=1, source_target_pairs={{0,2},{2,0},{1,3},{3,1},{4,6},{6,4},{5,7},{7,5},{8,10},{10,8},{9,1... | collective-permute-start | bytes 3145736 | tf_op jit(solution)/shard_map/ppermute | solution.py:18
  197.7 29.4 %collective-permute-start.33 = (bf16[4,32,4096]{2,1,0:T(8,128)(2,1)S(1)}, bf16[4,32,4096]{2,1,0:T(8,128)(2,1)S(1)}, u32[]{:S(2)}, u32[]{:S(2)}) collective-permute-start(bf16[4,32,4096]{2,1,0:T(8,128)(2,1)S(1)} %get-tuple-element.233), channel_id=1, source_target_pairs={{0,2},{2,0},{1,3},{3,1},{4,6},{6,4},{5,7},{7,5},{8,10},{10,8},{9,1... | collective-permute-start | bytes 3145736 | tf_op jit(solution)/shard_map/ppermute | solution.py:18
  213.8 35.8 %collective-permute-start.35 = (bf16[4,32,4096]{2,1,0:T(8,128)(2,1)S(1)}, bf16[4,32,4096]{2,1,0:T(8,128)(2,1)S(1)}, u32[]{:S(2)}, u32[]{:S(2)}) collective-permute-start(bf16[4,32,4096]{2,1,0:T(8,128)(2,1)S(1)} %constant_dynamic-update-slice_fusion.2.own_ref), channel_id=1, source_target_pairs={{0,2},{2,0},{1,3},{3,1},{4,6},{6,4},{5,7},{7,5},{8,10},{10,8},{9,1... | collective-permute-start | bytes 3145736 | tf_op jit(solution)/shard_map/ppermute | solution.py:18
  227.8 28.3 %collective-permute-start.34 = (bf16[2,32,4096]{2,1,0:T(8,128)(2,1)S(1)}, bf16[2,32,4096]{2,1,0:T(8,128)(2,1)S(1)}, u32[]{:S(2)}, u32[]{:S(2)}) collective-permute-start(bf16[2,32,4096]{2,1,0:T(8,128)(2,1)S(1)} %get-tuple-element.377), channel_id=1, source_target_pairs={{0,4},{4,0},{8,12},{12,8},{1,5},{5,1},{9,13},{13,9},{2,6},{6,2},{1... | collective-permute-start | bytes 1572872 | tf_op jit(solution)/shard_map/ppermute | solution.py:27
  232.6 23.5 %collective-permute-start.31 = (bf16[1,32,4096]{2,1,0:T(8,128)(2,1)S(1)}, bf16[1,32,4096]{2,1,0:T(8,128)(2,1)S(1)}, u32[]{:S(2)}, u32[]{:S(2)}) collective-permute-start(bf16[1,32,4096]{2,1,0:T(8,128)(2,1)S(1)} %get-tuple-element.244), channel_id=1, source_target_pairs={{0,8},{4,12},{8,0},{12,4},{1,9},{5,13},{9,1},{13,5},{2,10},{6,14},... | collective-permute-start | bytes 786440 | tf_op jit(solution)/shard_map/ppermute | solution.py:27
  243.5 27.8 %collective-permute-start.37 = (bf16[1,32,4096]{2,1,0:T(8,128)(2,1)S(1)}, bf16[1,32,4096]{2,1,0:T(8,128)(2,1)S(1)}, u32[]{:S(2)}, u32[]{:S(2)}) collective-permute-start(bf16[1,32,4096]{2,1,0:T(8,128)(2,1)S(1)} %get-tuple-element.251), channel_id=1, source_target_pairs={{0,8},{4,12},{8,0},{12,4},{1,9},{5,13},{9,1},{13,5},{2,10},{6,14},... | collective-permute-start | bytes 786440 | tf_op jit(solution)/shard_map/ppermute | solution.py:27
  263.3 27.5 %collective-permute-start.39 = (bf16[1,32,4096]{2,1,0:T(8,128)(2,1)S(1)}, bf16[1,32,4096]{2,1,0:T(8,128)(2,1)S(1)}, u32[]{:S(2)}, u32[]{:S(2)}) collective-permute-start(bf16[1,32,4096]{2,1,0:T(8,128)(2,1)S(1)} %get-tuple-element.258), channel_id=1, source_target_pairs={{0,8},{4,12},{8,0},{12,4},{1,9},{5,13},{9,1},{13,5},{2,10},{6,14},... | collective-permute-start | bytes 786440 | tf_op jit(solution)/shard_map/ppermute | solution.py:27
  267.4 25.9 %collective-permute-start.38 = (bf16[4,32,4096]{2,1,0:T(8,128)(2,1)S(1)}, bf16[4,32,4096]{2,1,0:T(8,128)(2,1)S(1)}, u32[]{:S(2)}, u32[]{:S(2)}) collective-permute-start(bf16[4,32,4096]{2,1,0:T(8,128)(2,1)S(1)} %constant_dynamic-update-slice_fusion.7.own_ref), channel_id=1, source_target_pairs={{0,2},{2,0},{1,3},{3,1},{4,6},{6,4},{5,7},{7,5},{8,10},{10,8},{9,1... | collective-permute-start | bytes 3145736 | tf_op jit(solution)/shard_map/ppermute | solution.py:18
  273.6 32.8 %collective-permute-start.43 = (bf16[1,32,4096]{2,1,0:T(8,128)(2,1)S(1)}, bf16[1,32,4096]{2,1,0:T(8,128)(2,1)S(1)}, u32[]{:S(2)}, u32[]{:S(2)}) collective-permute-start(bf16[1,32,4096]{2,1,0:T(8,128)(2,1)S(1)} %get-tuple-element.261), channel_id=1, source_target_pairs={{0,8},{4,12},{8,0},{12,4},{1,9},{5,13},{9,1},{13,5},{2,10},{6,14},... | collective-permute-start | bytes 786440 | tf_op jit(solution)/shard_map/ppermute | solution.py:27
  273.8 26.1 %collective-permute-start.45 = (bf16[4,32,1152]{2,1,0:T(8,128)(2,1)S(1)}, bf16[4,32,1152]{2,1,0:T(8,128)(2,1)S(1)}, u32[]{:S(2)}, u32[]{:S(2)}) collective-permute-start(bf16[4,32,1152]{2,1,0:T(8,128)(2,1)S(1)} %pad_maximum_fusion.7), channel_id=1, source_target_pairs={{0,2},{2,0},{1,3},{3,1},{4,6},{6,4},{5,7},{7,5},{8,10},{10,8},{9,1... | collective-permute-start | bytes 884744 | tf_op jit(solution)/shard_map/ppermute | solution.py:18
  305.5 29.8 %collective-permute-start.52 = (bf16[4,32,4096]{2,1,0:T(8,128)(2,1)S(1)}, bf16[4,32,4096]{2,1,0:T(8,128)(2,1)S(1)}, u32[]{:S(2)}, u32[]{:S(2)}) collective-permute-start(bf16[4,32,4096]{2,1,0:T(8,128)(2,1)S(1)} %constant_dynamic-update-slice_fusion.12.own_ref), channel_id=1, source_target_pairs={{0,2},{2,0},{1,3},{3,1},{4,6},{6,4},{5,7},{7,5},{8,10},{10,8},{9,1... | collective-permute-start | bytes 3145736 | tf_op jit(solution)/shard_map/ppermute | solution.py:18
  315.9 29.2 %collective-permute-start.50 = (bf16[2,32,4096]{2,1,0:T(8,128)(2,1)}, bf16[2,32,4096]{2,1,0:T(8,128)(2,1)S(1)}, u32[]{:S(2)}, u32[]{:S(2)}) collective-permute-start(bf16[2,32,4096]{2,1,0:T(8,128)(2,1)} %get-tuple-element.369), channel_id=1, source_target_pairs={{0,4},{4,0},{8,12},{12,8},{1,5},{5,1},{9,13},{13,9},{2,6},{6,2},{1... | collective-permute-start | bytes 1572872 | tf_op jit(solution)/shard_map/ppermute | solution.py:27
  318.8 22.9 %collective-permute-start.51 = (bf16[4,32,1152]{2,1,0:T(8,128)(2,1)S(1)}, bf16[4,32,1152]{2,1,0:T(8,128)(2,1)S(1)}, u32[]{:S(2)}, u32[]{:S(2)}) collective-permute-start(bf16[4,32,1152]{2,1,0:T(8,128)(2,1)S(1)} %pad_maximum_fusion.8), channel_id=1, source_target_pairs={{0,2},{2,0},{1,3},{3,1},{4,6},{6,4},{5,7},{7,5},{8,10},{10,8},{9,1... | collective-permute-start | bytes 884744 | tf_op jit(solution)/shard_map/ppermute | solution.py:18
  319.0 137.4 %collective-permute-start.49 = (bf16[128,4096]{1,0:T(8,128)(2,1)}, bf16[128,4096]{1,0:T(8,128)(2,1)}, u32[]{:S(2)}, u32[]{:S(2)}) collective-permute-start(bf16[128,4096]{1,0:T(8,128)(2,1)} %pad_maximum_fusion), channel_id=1, source_target_pairs={{0,16},{16,0},{1,17},{17,1},{2,18},{18,2},{3,19},{19,3},{4,20},{20... | collective-permute-start | bytes 3145736 | tf_op jit(solution)/shard_map/ppermute | solution.py:31
  343.6 23.9 %collective-permute-start.59 = (bf16[32,9216]{1,0:T(8,128)(2,1)S(1)}, bf16[32,9216]{1,0:T(8,128)(2,1)S(1)}, u32[]{:S(2)}, u32[]{:S(2)}) collective-permute-start(bf16[32,9216]{1,0:T(8,128)(2,1)S(1)} %get-tuple-element.285), channel_id=1, source_target_pairs={{0,16},{16,0},{1,17},{17,1},{2,18},{18,2},{3,19},{19,3},{4,20},{20... | collective-permute-start | bytes 1769480 | tf_op jit(solution)/shard_map/ppermute | solution.py:31
  403.4 36.6 %collective-permute-start.61 = (bf16[2,32,1152]{2,1,0:T(8,128)(2,1)S(1)}, bf16[2,32,1152]{2,1,0:T(8,128)(2,1)S(1)}, u32[]{:S(2)}, u32[]{:S(2)}) collective-permute-start(bf16[2,32,1152]{2,1,0:T(8,128)(2,1)S(1)} %get-tuple-element.310), channel_id=1, source_target_pairs={{0,8},{4,12},{8,0},{12,4},{1,9},{5,13},{9,1},{13,5},{2,10},{6,14},... | collective-permute-start | bytes 442376 | tf_op jit(solution)/shard_map/ppermute | solution.py:27
  404.6 35.5 %collective-permute-start.62 = (bf16[2,32,1152]{2,1,0:T(8,128)(2,1)S(1)}, bf16[2,32,1152]{2,1,0:T(8,128)(2,1)S(1)}, u32[]{:S(2)}, u32[]{:S(2)}) collective-permute-start(bf16[2,32,1152]{2,1,0:T(8,128)(2,1)S(1)} %get-tuple-element.311), channel_id=1, source_target_pairs={{0,4},{4,0},{8,12},{12,8},{1,5},{5,1},{9,13},{13,9},{2,6},{6,2},{1... | collective-permute-start | bytes 442376 | tf_op jit(solution)/shard_map/ppermute | solution.py:27
  405.8 34.3 %collective-permute-start.63 = (bf16[2,32,1152]{2,1,0:T(8,128)(2,1)S(1)}, bf16[2,32,1152]{2,1,0:T(8,128)(2,1)S(1)}, u32[]{:S(2)}, u32[]{:S(2)}) collective-permute-start(bf16[2,32,1152]{2,1,0:T(8,128)(2,1)S(1)} %get-tuple-element.312), channel_id=1, source_target_pairs={{0,12},{4,8},{8,4},{12,0},{1,13},{5,9},{9,5},{13,1},{2,14},{6,10},... | collective-permute-start | bytes 442376 | tf_op jit(solution)/shard_map/ppermute | solution.py:27
  407.0 34.4 %collective-permute-start.65 = (bf16[576,4096]{1,0:T(8,128)(2,1)}, bf16[576,4096]{1,0:T(8,128)(2,1)}, u32[]{:S(2)}, u32[]{:S(2)}) collective-permute-start(bf16[576,4096]{1,0:T(8,128)(2,1)} %convolution_convert_fusion), channel_id=1, source_target_pairs={{0,1},{1,0},{2,3},{3,2},{4,5},{5,4},{6,7},{7,6},{8,9},{9,8},{10,11... | collective-permute-start | bytes 14155784 | tf_op jit(solution)/shard_map/ppermute | solution.py:22
  492.5 58.1 %collective-permute-start.77 = (f32[1,13056]{1,0:T(1,128)S(1)}, f32[1,13056]{1,0:T(1,128)S(1)}, u32[]{:S(2)}, u32[]{:S(2)}) collective-permute-start(f32[1,13056]{1,0:T(1,128)S(1)} %broadcast_in_dim.16), channel_id=1, source_target_pairs={{0,2},{2,0},{1,3},{3,1},{4,6},{6,4},{5,7},{7,5},{8,10},{10,8},{9,1... | collective-permute-start | bytes 156680 | tf_op jit(solution)/shard_map/ppermute | solution.py:18
  (129 other events, 1551.8 us)
Sparse Core Ops, SparseCore 0:
  9.6 24.2 all-gather.2

commit v6 on v5

--- a/solution.py
+++ b/solution.py
@@ -471,8 +471,10 @@
         got = swap(rows)
         yield
         got = after(got)
+        if swap is swap_mid:
+            rows, got = rows.astype(F32), got.astype(F32)
         rows = jnp.where(side == 0, jnp.concatenate([rows, got]), jnp.concatenate([got, rows]))
-    stage["kernel"] = rows.astype(F32)
+    stage["kernel"] = rows
 
 
 def body(

time: 593 us -> 589 us (level)
    unnamed x188 -> x178, local copies, waits for them, and re-layouts: 36.1 us -> 33.9 us
where the time goes in v6:
time: 589 us; the launch traced here: 579 us
  matrix products  207 us (35%)
  starting transfers between devices  125 us (21%)
  Pallas kernels  98.1 us (17%)
  waiting for transfers between devices  71.7 us (12%)
  local copies, waits for them, and re-layouts  44.1 us (7%)
  other arithmetic  17.2 us (3%)
  between operations  16 us (3%)
    conv_general_dilated x4, matrix products, conv_forward(): lax.conv_general_dilated(inputs, kernel, (1, 1), ((1, 1), (1, 1)), dimens...  72.6 us
    ppermute x48, starting transfers between devices, swap_outer(): return lax.ppermute(block, 'outer', [(i, i ^ mask) for i in range(count)])  65.2 us
    conv_general_dilated x4, matrix products, conv_grad_inputs(): lax.conv_general_dilated(grad_pre, turned, (1, 1), ((1, 1), (1, 1)), dime...  60 us
    conv_general_dilated x4, matrix products, conv_grad_kernel(): lax.conv_general_dilated(inputs, grad_pre, (1, 1), ((1, 1), (1, 1)), dime...  56 us
    ppermute x48, waiting for transfers between devices, swap_outer(): return lax.ppermute(block, 'outer', [(i, i ^ mask) for i in range(count)])  47.3 us
    ppermute x19, starting transfers between devices, swap_core(): return lax.ppermute(block, 'core', [(0, 1), (1, 0)])  35 us
    unnamed x178, local copies, waits for them, and re-layouts  33.9 us
    pallas_call x4, Pallas kernels, fc_backward(): pl.pallas_call(functools.partial(fc_back_kernel, count), grid=(depth // t...  26.3 us
  transfers between devices with their start and end apart: 82, of which 21 were waited for; matrix products, arithmetic and copies ran while one was open for 40% of the time, Pallas kernels for 16%

profile of v6, /device:TPU:1, one launch (start us, length us, event | category | flops | bytes accessed | tf_op | source)
XLA Modules:
  0.0 579.2 jit_solution(8728333781928503678)
XLA Ops:
  8.7 18.3 %fusion.3 = (bf16[13,13,32,256]{3,2,1,0:T(8,128)(2,1)}, bf16[13,13,32,256]{3,2,1,0:T(8,128)(2,1)S(1)}) fusion(f32[256]{0:T(256)S(1)} %bitcast.227, bf16[1,3,3,384,256]{4,3,2,1,0:T(8,128)(2,1)S(1)} %copy-done, bf16[1,128,13,13,384]{4,1,3,2,0:T(8,128)(2,1)} %param.12), kind=kOutput, calls=%fused_computation.9 | convolution fusion | flops 8639307776 | bytes 11461632 | tf_op jit(solution)/shard_map/conv_general_dilated | solution.py:413
  30.0 18.1 %fusion.7 = (bf16[13,13,32,256]{3,2,1,0:T(8,128)(2,1)}, bf16[13,13,32,256]{3,2,1,0:T(8,128)(2,1)S(1)}) fusion(f32[256]{0:T(256)S(1)} %bitcast.228, bf16[1,3,3,384,256]{4,3,2,1,0:T(8,128)(2,1)S(1)} %copy-done, bf16[1,128,13,13,384]{4,1,3,2,0:T(8,128)(2,1)} %param.12), kind=kOutput, calls=%fused_computation.13 | convolution fusion | flops 8639307776 | bytes 11461632 | tf_op jit(solution)/shard_map/conv_general_dilated | solution.py:413
  56.0 18.1 %fusion.11 = (bf16[13,13,32,256]{3,2,1,0:T(8,128)(2,1)}, bf16[13,13,32,256]{3,2,1,0:T(8,128)(2,1)S(1)}) fusion(f32[256]{0:T(256)S(1)} %bitcast.229, bf16[1,3,3,384,256]{4,3,2,1,0:T(8,128)(2,1)S(1)} %copy-done, bf16[1,128,13,13,384]{4,1,3,2,0:T(8,128)(2,1)} %param.12), kind=kOutput, calls=%fused_computation.17 | convolution fusion | flops 8639307776 | bytes 11461632 | tf_op jit(solution)/shard_map/conv_general_dilated | solution.py:413
  97.5 6.3 %fc_forward.4 = (f32[4,32,4096]{2,1,0:T(8,128)S(1)}, bf16[4,32,4096]{2,1,0:T(8,128)(2,1)S(1)}, bf16[256,1152]{1,0:T(8,128)(2,1)S(1)}) custom-call(bf16[1152,4096]{1,0:T(8,128)(2,1)} %bitcast.195, bf16[4,32,1152]{2,1,0:T(8,128)(2,1)S(1)} %copy-done.44, bf16[2,32,1152]{2,1,0:T(8,128)(2,1)S(1)} %copy-done.36, bf16[2,32,1152]{2,1,0:T(8,128)(2,1)S(1)} %copy-done.38, ...), custom_call_target="tpu_custom_call" | custom-call | tf_op jit(solution)/shard_map/fc_forward/pallas_call | solution.py:272
  108.1 18.1 %fusion.15 = (bf16[13,13,32,256]{3,2,1,0:T(8,128)(2,1)}, bf16[13,13,32,256]{3,2,1,0:T(8,128)(2,1)S(1)}) fusion(f32[256]{0:T(256)S(1)} %bitcast.230, bf16[1,3,3,384,256]{4,3,2,1,0:T(8,128)(2,1)S(1)} %copy-done, bf16[1,128,13,13,384]{4,1,3,2,0:T(8,128)(2,1)} %param.12), kind=kOutput, calls=%fused_computation.21 | convolution fusion | flops 8639307776 | bytes 11461632 | tf_op jit(solution)/shard_map/conv_general_dilated | solution.py:413
  128.9 4.3 collective-permute-start.13
  138.6 7.1 %fc_forward.5 = (f32[4,32,4096]{2,1,0:T(8,128)S(1)}, bf16[4,32,4096]{2,1,0:T(8,128)(2,1)}, bf16[256,1152]{1,0:T(8,128)(2,1)S(1)}) custom-call(bf16[1152,4096]{1,0:T(8,128)(2,1)} %bitcast.196, bf16[4,32,1152]{2,1,0:T(8,128)(2,1)S(1)} %collective-permute-done.12.got_ref, bf16[2,32,1152]{2,1,0:T(8,128)(2,1)S(1)} %copy-done.28, ...), custom_call_target="tpu_custom_call" | custom-call | tf_op jit(solution)/shard_map/fc_forward/pallas_call | solution.py:272
  176.7 6.5 %fc_forward.6 = (f32[4,32,4096]{2,1,0:T(8,128)S(1)}, bf16[4,32,4096]{2,1,0:T(8,128)(2,1)S(1)}, bf16[256,1152]{1,0:T(8,128)(2,1)S(1)}) custom-call(bf16[1152,4096]{1,0:T(8,128)(2,1)} %bitcast.197, bf16[4,32,1152]{2,1,0:T(8,128)(2,1)S(1)} %collective-permute-done.18.got_ref, bf16[2,32,1152]{2,1,0:T(8,128)(2,1)S(1)} %copy-done.26, ...), custom_call_target="tpu_custom_call" | custom-call | tf_op jit(solution)/shard_map/fc_forward/pallas_call | solution.py:272
  191.3 6.2 %fc_forward.7 = (f32[4,32,4096]{2,1,0:T(8,128)S(1)}, bf16[4,32,4096]{2,1,0:T(8,128)(2,1)S(1)}, bf16[256,1152]{1,0:T(8,128)(2,1)S(1)}) custom-call(bf16[1152,4096]{1,0:T(8,128)(2,1)} %bitcast.198, bf16[4,32,1152]{2,1,0:T(8,128)(2,1)S(1)} %collective-permute-done.28.got_ref, bf16[2,32,1152]{2,1,0:T(8,128)(2,1)S(1)} %get-tuple-element.218.refs_0_, ...), custom_call_target="tpu_custom_call" | custom-call | tf_op jit(solution)/shard_map/fc_forward/pallas_call | solution.py:272
  208.4 4.1 collective-permute-start.32
  214.9 10.7 %collective-permute-done.29.came_ref = bf16[2,32,4096]{2,1,0:T(8,128)(2,1)S(1)} collective-permute-done((bf16[2,32,4096]{2,1,0:T(8,128)(2,1)S(1)}, bf16[2,32,4096]{2,1,0:T(8,128)(2,1)S(1)}, u32[]{:S(2)}, u32[]{:S(2)}) %collective-permute-start.29) | collective-permute-done | bytes 524320 | tf_op jit(solution)/shard_map/ppermute | solution.py:27
  235.7 7.3 %collective-permute-done.36.came_ref = bf16[2,32,4096]{2,1,0:T(8,128)(2,1)S(1)} collective-permute-done((bf16[2,32,4096]{2,1,0:T(8,128)(2,1)S(1)}, bf16[2,32,4096]{2,1,0:T(8,128)(2,1)S(1)}, u32[]{:S(2)}, u32[]{:S(2)}) %collective-permute-start.36) | collective-permute-done | bytes 524320 | tf_op jit(solution)/shard_map/ppermute | solution.py:27
  245.3 4.1 collective-permute-done.35.came_ref
  249.4 6.5 %fc_backward.4 = (bf16[2,32,1152]{2,1,0:T(8,128)(2,1)S(1)}, bf16[2,32,1152]{2,1,0:T(8,128)(2,1)S(1)}, bf16[2,32,1152]{2,1,0:T(8,128)(2,1)S(1)}, bf16[2,32,1152]{2,1,0:T(8,128)(2,1)S(1)}) custom-call(bf16[1152,4096]{1,0:T(8,128)(2,1)} %bitcast.199, bf16[4,32,4096]{2,1,0:T(8,128)(2,1)S(1)} %constant_dynamic-update-slice_fusion.2.own_ref, ...), custom_call_target="tpu_custom_call" | custom-call | tf_op jit(solution)/shard_map/fc_backward/pallas_call | solution.py:319
  273.6 17.4 %collective-permute-start.45 = (bf16[4,32,1152]{2,1,0:T(8,128)(2,1)S(1)}, bf16[4,32,1152]{2,1,0:T(8,128)(2,1)S(1)}, u32[]{:S(2)}, u32[]{:S(2)}) collective-permute-start(bf16[4,32,1152]{2,1,0:T(8,128)(2,1)S(1)} %pad_maximum_fusion.7), channel_id=1, source_target_pairs={{0,2},{2,0},{1,3},{3,1},{4,6},{6,4},{5,7},{7,5},{8,10},{10,8},{9,1... | collective-permute-start | bytes 884744 | tf_op jit(solution)/shard_map/ppermute | solution.py:18
  293.5 6.6 %fc_backward.5 = (bf16[2,32,1152]{2,1,0:T(8,128)(2,1)S(1)}, bf16[2,32,1152]{2,1,0:T(8,128)(2,1)S(1)}, bf16[2,32,1152]{2,1,0:T(8,128)(2,1)S(1)}, bf16[2,32,1152]{2,1,0:T(8,128)(2,1)S(1)}) custom-call(bf16[1152,4096]{1,0:T(8,128)(2,1)} %bitcast.200, bf16[4,32,4096]{2,1,0:T(8,128)(2,1)S(1)} %constant_dynamic-update-slice_fusion.7.own_ref, ...), custom_call_target="tpu_custom_call" | custom-call | tf_op jit(solution)/shard_map/fc_backward/pallas_call | solution.py:319
  301.7 3.9 collective-permute-done.44
  309.3 4.0 collective-permute-start.46
  325.4 13.4 %fusion.32 = f32[3,3,384,256]{3,2,1,0:T(8,128)} fusion(bf16[13,13,32,256]{3,2,1,0:T(8,128)(2,1)S(1)} %get-tuple-element.281, bf16[1,128,13,13,384]{4,1,3,2,0:T(8,128)(2,1)} %param.12), kind=kOutput, calls=%fused_computation.50 | convolution fusion | flops 8613003264 | bytes 10461184 | tf_op jit(solution)/shard_map/conv_general_dilated | solution.py:430
  338.8 6.5 %fc_backward.6 = (bf16[2,32,1152]{2,1,0:T(8,128)(2,1)S(1)}, bf16[2,32,1152]{2,1,0:T(8,128)(2,1)S(1)}, bf16[2,32,1152]{2,1,0:T(8,128)(2,1)S(1)}, bf16[2,32,1152]{2,1,0:T(8,128)(2,1)S(1)}) custom-call(bf16[1152,4096]{1,0:T(8,128)(2,1)} %bitcast.201, bf16[4,32,4096]{2,1,0:T(8,128)(2,1)S(1)} %constant_dynamic-update-slice_fusion.12.own_ref, ...), custom_call_target="tpu_custom_call" | custom-call | tf_op jit(solution)/shard_map/fc_backward/pallas_call | solution.py:319
  354.4 14.9 %convert_dynamic-update-slice_fusion.3 = bf16[128,13,13,384]{3,0,2,1:T(8,128)(2,1)} fusion(bf16[128,13,13,384]{3,0,2,1:T(8,128)(2,1)} %bitcast.206, bf16[32,13,13,256]{3,0,2,1:T(8,128)(2,1)S(1)} %bitcast.194, bf16[1,3,3,384,256]{4,3,2,1,0:T(8,128)(2,1)S(1)} %copy-done), kind=kOutput, calls=%fused_computation.57 | convolution fusion | flops 8615079936 | bytes 8691712 | tf_op jit(solution)/shard_map/conv_general_dilated | solution.py:423
  375.3 14.2 %fusion.28 = f32[3,3,384,256]{3,2,1,0:T(8,128)} fusion(bf16[13,13,32,256]{3,2,1,0:T(8,128)(2,1)S(1)} %get-tuple-element.295, bf16[1,128,13,13,384]{4,1,3,2,0:T(8,128)(2,1)} %param.12), kind=kOutput, calls=%fused_computation.46 | convolution fusion | flops 8613003264 | bytes 10461184 | tf_op jit(solution)/shard_map/conv_general_dilated | solution.py:430
  393.3 6.7 %fc_backward.7 = (bf16[2,32,1152]{2,1,0:T(8,128)(2,1)S(1)}, bf16[2,32,1152]{2,1,0:T(8,128)(2,1)S(1)}, bf16[2,32,1152]{2,1,0:T(8,128)(2,1)S(1)}, bf16[2,32,1152]{2,1,0:T(8,128)(2,1)S(1)}) custom-call(bf16[1152,4096]{1,0:T(8,128)(2,1)} %bitcast.202, bf16[4,32,4096]{2,1,0:T(8,128)(2,1)S(1)} %constant_dynamic-update-slice_fusion.17.own_ref, ...), custom_call_target="tpu_custom_call" | custom-call | tf_op jit(solution)/shard_map/fc_backward/pallas_call | solution.py:319
  401.0 9.4 %convolution_convert_fusion = bf16[576,4096]{1,0:T(8,128)(2,1)} fusion(bf16[1024,4096]{1,0:T(8,128)(2,1)} %constant_dynamic-update-slice_fusion.24, pred[]{:T(512)S(6)} %eq.28, bf16[1024,1152]{1,0:T(8,128)(2,1)S(1)} %copy-done.53), kind=kOutput, calls=%fused_computation.5 | convolution fusion | flops 4834787328 | bytes 15728641 | tf_op jit(solution)/shard_map/dot_general | solution.py:622
  415.1 10.4 %collective-permute-start.65 = (bf16[576,4096]{1,0:T(8,128)(2,1)}, bf16[576,4096]{1,0:T(8,128)(2,1)}, u32[]{:S(2)}, u32[]{:S(2)}) collective-permute-start(bf16[576,4096]{1,0:T(8,128)(2,1)} %convolution_convert_fusion), channel_id=1, source_target_pairs={{0,1},{1,0},{2,3},{3,2},{4,5},{5,4},{6,7},{7,6},{8,9},{9,8},{10,11... | collective-permute-start | bytes 14155784 | tf_op jit(solution)/shard_map/ppermute | solution.py:22
  428.3 14.4 %fusion.24 = f32[3,3,384,256]{3,2,1,0:T(8,128)} fusion(bf16[13,13,32,256]{3,2,1,0:T(8,128)(2,1)S(1)} %get-tuple-element.308, bf16[1,128,13,13,384]{4,1,3,2,0:T(8,128)(2,1)} %param.12), kind=kOutput, calls=%fused_computation.42 | convolution fusion | flops 8613003264 | bytes 10461184 | tf_op jit(solution)/shard_map/conv_general_dilated | solution.py:430
  444.2 9.3 %convert_add_fusion = f32[576,4096]{1,0:T(8,128)} fusion(bf16[576,4096]{1,0:T(8,128)(2,1)} %collective-permute-done.65, bf16[1024,576]{1,0:T(8,128)(2,1)S(1)} %broadcast_select_fusion, bf16[1024,4096]{1,0:T(8,128)(2,1)S(1)} %bitcast.205), kind=kOutput, calls=%fused_computation | convolution fusion | flops 4836556800 | bytes 23724032 | tf_op jit(solution)/shard_map/dot_general | solution.py:627
  461.7 9.4 %collective-permute-done.66.back_ref = bf16[32,9216]{1,0:T(8,128)(2,1)} collective-permute-done((bf16[32,9216]{1,0:T(8,128)(2,1)}, bf16[32,9216]{1,0:T(8,128)(2,1)}, u32[]{:S(2)}, u32[]{:S(2)}) %collective-permute-start.66) | collective-permute-done | bytes 589856 | tf_op jit(solution)/shard_map/ppermute | solution.py:31
  474.0 14.0 %add_add_fusion = f32[3,3,384,256]{3,2,1,0:T(8,128)S(1)} fusion(f32[3,3,384,256]{3,2,1,0:T(8,128)} %fusion.24, f32[3,3,384,256]{3,2,1,0:T(8,128)S(1)} %copy-done.69, f32[3,3,384,256]{3,2,1,0:T(8,128)} %fusion.28, bf16[13,13,32,256]{3,2,1,0:T(8,128)(2,1)S(1)} %get-tuple-element.322, bf16[1,128,13,13,384]{4,1,3,2,0:T(8,128)(2,1)} %param.12), kind=kOutput, calls=%fused_computation.67 | convolution fusion | flops 8615657472 | bytes 21078016 | tf_op jit(solution)/shard_map/conv_general_dilated | solution.py:430
  496.1 14.9 %convert_dynamic-update-slice_fusion.2 = bf16[128,13,13,384]{3,0,2,1:T(8,128)(2,1)} fusion(bf16[128,13,13,384]{3,0,2,1:T(8,128)(2,1)} %convert_dynamic-update-slice_fusion.3, bf16[32,13,13,256]{3,0,2,1:T(8,128)(2,1)S(1)} %bitcast.191, bf16[1,3,3,384,256]{4,3,2,1,0:T(8,128)(2,1)S(1)} %copy-done), kind=kOutput, calls=%fused_computation.56 | convolution fusion | flops 8615079936 | bytes 8691712 | tf_op jit(solution)/shard_map/conv_general_dilated | solution.py:423
  514.8 15.1 %convert_dynamic-update-slice_fusion.1 = bf16[128,13,13,384]{3,0,2,1:T(8,128)(2,1)} fusion(bf16[128,13,13,384]{3,0,2,1:T(8,128)(2,1)} %convert_dynamic-update-slice_fusion.2, bf16[32,13,13,256]{3,0,2,1:T(8,128)(2,1)S(1)} %bitcast.192, bf16[1,3,3,384,256]{4,3,2,1,0:T(8,128)(2,1)S(1)} %copy-done), kind=kOutput, calls=%fused_computation.55 | convolution fusion | flops 8615079936 | bytes 8691712 | tf_op jit(solution)/shard_map/conv_general_dilated | solution.py:423
  533.6 15.2 %convert_dynamic-update-slice_fusion = bf16[128,13,13,384]{3,0,2,1:T(8,128)(2,1)} fusion(bf16[128,13,13,384]{3,0,2,1:T(8,128)(2,1)} %convert_dynamic-update-slice_fusion.1, bf16[32,13,13,256]{3,0,2,1:T(8,128)(2,1)S(1)} %bitcast.193, bf16[1,3,3,384,256]{4,3,2,1,0:T(8,128)(2,1)S(1)} %copy-done), kind=kOutput, calls=%fused_computation.54 | convolution fusion | flops 8615079936 | bytes 8691712 | tf_op jit(solution)/shard_map/conv_general_dilated | solution.py:423
  (454 shorter events, 227.9 us)
Async XLA Ops:
  7.2 85.7 %all-gather.3.cloned.1.call-start = ((), (), s32[]{:S(2)}) async-start(), calls=%async_computation | async-start | bytes 14155776 | tf_op jit(solution)/shard_map/all_gather | solution.py:497
  27.9 23.3 %collective-permute-start = (bf16[32,9216]{1,0:T(8,128)(2,1)S(1)}, bf16[32,9216]{1,0:T(8,128)(2,1)S(1)}, u32[]{:S(2)}, u32[]{:S(2)}) collective-permute-start(bf16[32,9216]{1,0:T(8,128)(2,1)S(1)} %get-tuple-element.180.pooled_ref), channel_id=1, source_target_pairs={{0,16},{16,0},{1,17},{17,1},{2,18},{18,2},{3,19},{19,3},{4,20},{20... | collective-permute-start | bytes 1769480 | tf_op jit(solution)/shard_map/ppermute | solution.py:31
  50.8 27.5 %collective-permute-start.5 = (bf16[32,9216]{1,0:T(8,128)(2,1)}, bf16[32,9216]{1,0:T(8,128)(2,1)}, u32[]{:S(2)}, u32[]{:S(2)}) collective-permute-start(bf16[32,9216]{1,0:T(8,128)(2,1)} %get-tuple-element.188.pooled_ref), channel_id=1, source_target_pairs={{0,16},{16,0},{1,17},{17,1},{2,18},{18,2},{3,19},{19,3},{4,20},{20... | collective-permute-start | bytes 1769480 | tf_op jit(solution)/shard_map/ppermute | solution.py:31
  52.1 24.7 %collective-permute-start.1 = (bf16[2,32,1152]{2,1,0:T(8,128)(2,1)S(1)}, bf16[2,32,1152]{2,1,0:T(8,128)(2,1)S(1)}, u32[]{:S(2)}, u32[]{:S(2)}) collective-permute-start(bf16[2,32,1152]{2,1,0:T(8,128)(2,1)S(1)} %get-tuple-element.185), channel_id=1, source_target_pairs={{0,8},{4,12},{8,0},{12,4},{1,9},{5,13},{9,1},{13,5},{2,10},{6,14},... | collective-permute-start | bytes 442376 | tf_op jit(solution)/shard_map/ppermute | solution.py:27
  54.6 22.2 %collective-permute-start.2 = (bf16[2,32,1152]{2,1,0:T(8,128)(2,1)S(1)}, bf16[2,32,1152]{2,1,0:T(8,128)(2,1)S(1)}, u32[]{:S(2)}, u32[]{:S(2)}) collective-permute-start(bf16[2,32,1152]{2,1,0:T(8,128)(2,1)S(1)} %get-tuple-element.186), channel_id=1, source_target_pairs={{0,4},{4,0},{8,12},{12,8},{1,5},{5,1},{9,13},{13,9},{2,6},{6,2},{1... | collective-permute-start | bytes 442376 | tf_op jit(solution)/shard_map/ppermute | solution.py:27
  75.9 29.6 %collective-permute-start.7 = (bf16[32,9216]{1,0:T(8,128)(2,1)S(1)}, bf16[32,9216]{1,0:T(8,128)(2,1)S(1)}, u32[]{:S(2)}, u32[]{:S(2)}) collective-permute-start(bf16[32,9216]{1,0:T(8,128)(2,1)S(1)} %get-tuple-element.193.pooled_ref), channel_id=1, source_target_pairs={{0,16},{16,0},{1,17},{17,1},{2,18},{18,2},{3,19},{19,3},{4,20},{20... | collective-permute-start | bytes 1769480 | tf_op jit(solution)/shard_map/ppermute | solution.py:31
  104.7 30.3 %collective-permute-start.6 = (bf16[4,32,4096]{2,1,0:T(8,128)(2,1)S(1)}, bf16[4,32,4096]{2,1,0:T(8,128)(2,1)S(1)}, u32[]{:S(2)}, u32[]{:S(2)}) collective-permute-start(bf16[4,32,4096]{2,1,0:T(8,128)(2,1)S(1)} %get-tuple-element.192), channel_id=1, source_target_pairs={{0,2},{2,0},{1,3},{3,1},{4,6},{6,4},{5,7},{7,5},{8,10},{10,8},{9,1... | collective-permute-start | bytes 3145736 | tf_op jit(solution)/shard_map/ppermute | solution.py:18
  107.5 31.1 %collective-permute-start.12 = (bf16[4,32,1152]{2,1,0:T(8,128)(2,1)S(1)}, bf16[4,32,1152]{2,1,0:T(8,128)(2,1)S(1)}, u32[]{:S(2)}, u32[]{:S(2)}) collective-permute-start(bf16[4,32,1152]{2,1,0:T(8,128)(2,1)S(1)} %pad_maximum_fusion.4), channel_id=1, source_target_pairs={{0,2},{2,0},{1,3},{3,1},{4,6},{6,4},{5,7},{7,5},{8,10},{10,8},{9,1... | collective-permute-start | bytes 884744 | tf_op jit(solution)/shard_map/ppermute | solution.py:18
  147.9 23.0 %collective-permute-start.19 = (bf16[4,32,4096]{2,1,0:T(8,128)(2,1)}, bf16[4,32,4096]{2,1,0:T(8,128)(2,1)}, u32[]{:S(2)}, u32[]{:S(2)}) collective-permute-start(bf16[4,32,4096]{2,1,0:T(8,128)(2,1)} %get-tuple-element.205), channel_id=1, source_target_pairs={{0,2},{2,0},{1,3},{3,1},{4,6},{6,4},{5,7},{7,5},{8,10},{10,8},{9,1... | collective-permute-start | bytes 3145736 | tf_op jit(solution)/shard_map/ppermute | solution.py:18
  149.9 33.8 %collective-permute-start.23 = (bf16[128,4096]{1,0:T(8,128)(2,1)}, bf16[128,4096]{1,0:T(8,128)(2,1)}, u32[]{:S(2)}, u32[]{:S(2)}) collective-permute-start(bf16[128,4096]{1,0:T(8,128)(2,1)} %multiply_convert_fusion), channel_id=1, source_target_pairs={{0,16},{16,0},{1,17},{17,1},{2,18},{18,2},{3,19},{19,3},{4,20},{20... | collective-permute-start | bytes 3145736 | tf_op jit(solution)/shard_map/ppermute | solution.py:31
  197.6 29.4 %collective-permute-start.33 = (bf16[4,32,4096]{2,1,0:T(8,128)(2,1)S(1)}, bf16[4,32,4096]{2,1,0:T(8,128)(2,1)S(1)}, u32[]{:S(2)}, u32[]{:S(2)}) collective-permute-start(bf16[4,32,4096]{2,1,0:T(8,128)(2,1)S(1)} %get-tuple-element.233), channel_id=1, source_target_pairs={{0,2},{2,0},{1,3},{3,1},{4,6},{6,4},{5,7},{7,5},{8,10},{10,8},{9,1... | collective-permute-start | bytes 3145736 | tf_op jit(solution)/shard_map/ppermute | solution.py:18
  214.4 35.1 %collective-permute-start.35 = (bf16[4,32,4096]{2,1,0:T(8,128)(2,1)S(1)}, bf16[4,32,4096]{2,1,0:T(8,128)(2,1)S(1)}, u32[]{:S(2)}, u32[]{:S(2)}) collective-permute-start(bf16[4,32,4096]{2,1,0:T(8,128)(2,1)S(1)} %constant_dynamic-update-slice_fusion.2.own_ref), channel_id=1, source_target_pairs={{0,2},{2,0},{1,3},{3,1},{4,6},{6,4},{5,7},{7,5},{8,10},{10,8},{9,1... | collective-permute-start | bytes 3145736 | tf_op jit(solution)/shard_map/ppermute | solution.py:18
  228.3 27.6 %collective-permute-start.34 = (bf16[2,32,4096]{2,1,0:T(8,128)(2,1)}, bf16[2,32,4096]{2,1,0:T(8,128)(2,1)S(1)}, u32[]{:S(2)}, u32[]{:S(2)}) collective-permute-start(bf16[2,32,4096]{2,1,0:T(8,128)(2,1)} %get-tuple-element.379), channel_id=1, source_target_pairs={{0,4},{4,0},{8,12},{12,8},{1,5},{5,1},{9,13},{13,9},{2,6},{6,2},{1... | collective-permute-start | bytes 1572872 | tf_op jit(solution)/shard_map/ppermute | solution.py:27
  233.0 22.9 %collective-permute-start.31 = (bf16[1,32,4096]{2,1,0:T(8,128)(2,1)S(1)}, bf16[1,32,4096]{2,1,0:T(8,128)(2,1)S(1)}, u32[]{:S(2)}, u32[]{:S(2)}) collective-permute-start(bf16[1,32,4096]{2,1,0:T(8,128)(2,1)S(1)} %get-tuple-element.244), channel_id=1, source_target_pairs={{0,8},{4,12},{8,0},{12,4},{1,9},{5,13},{9,1},{13,5},{2,10},{6,14},... | collective-permute-start | bytes 786440 | tf_op jit(solution)/shard_map/ppermute | solution.py:27
  243.4 27.8 %collective-permute-start.37 = (bf16[1,32,4096]{2,1,0:T(8,128)(2,1)S(1)}, bf16[1,32,4096]{2,1,0:T(8,128)(2,1)S(1)}, u32[]{:S(2)}, u32[]{:S(2)}) collective-permute-start(bf16[1,32,4096]{2,1,0:T(8,128)(2,1)S(1)} %get-tuple-element.251), channel_id=1, source_target_pairs={{0,8},{4,12},{8,0},{12,4},{1,9},{5,13},{9,1},{13,5},{2,10},{6,14},... | collective-permute-start | bytes 786440 | tf_op jit(solution)/shard_map/ppermute | solution.py:27
  263.2 27.8 %collective-permute-start.39 = (bf16[1,32,4096]{2,1,0:T(8,128)(2,1)S(1)}, bf16[1,32,4096]{2,1,0:T(8,128)(2,1)S(1)}, u32[]{:S(2)}, u32[]{:S(2)}) collective-permute-start(bf16[1,32,4096]{2,1,0:T(8,128)(2,1)S(1)} %get-tuple-element.258), channel_id=1, source_target_pairs={{0,8},{4,12},{8,0},{12,4},{1,9},{5,13},{9,1},{13,5},{2,10},{6,14},... | collective-permute-start | bytes 786440 | tf_op jit(solution)/shard_map/ppermute | solution.py:27
  267.3 26.3 %collective-permute-start.38 = (bf16[4,32,4096]{2,1,0:T(8,128)(2,1)S(1)}, bf16[4,32,4096]{2,1,0:T(8,128)(2,1)S(1)}, u32[]{:S(2)}, u32[]{:S(2)}) collective-permute-start(bf16[4,32,4096]{2,1,0:T(8,128)(2,1)S(1)} %constant_dynamic-update-slice_fusion.7.own_ref), channel_id=1, source_target_pairs={{0,2},{2,0},{1,3},{3,1},{4,6},{6,4},{5,7},{7,5},{8,10},{10,8},{9,1... | collective-permute-start | bytes 3145736 | tf_op jit(solution)/shard_map/ppermute | solution.py:18
  273.5 35.8 %collective-permute-start.43 = (bf16[1,32,4096]{2,1,0:T(8,128)(2,1)S(1)}, bf16[1,32,4096]{2,1,0:T(8,128)(2,1)S(1)}, u32[]{:S(2)}, u32[]{:S(2)}) collective-permute-start(bf16[1,32,4096]{2,1,0:T(8,128)(2,1)S(1)} %get-tuple-element.261), channel_id=1, source_target_pairs={{0,8},{4,12},{8,0},{12,4},{1,9},{5,13},{9,1},{13,5},{2,10},{6,14},... | collective-permute-start | bytes 786440 | tf_op jit(solution)/shard_map/ppermute | solution.py:27
  273.6 26.5 %collective-permute-start.45 = (bf16[4,32,1152]{2,1,0:T(8,128)(2,1)S(1)}, bf16[4,32,1152]{2,1,0:T(8,128)(2,1)S(1)}, u32[]{:S(2)}, u32[]{:S(2)}) collective-permute-start(bf16[4,32,1152]{2,1,0:T(8,128)(2,1)S(1)} %pad_maximum_fusion.7), channel_id=1, source_target_pairs={{0,2},{2,0},{1,3},{3,1},{4,6},{6,4},{5,7},{7,5},{8,10},{10,8},{9,1... | collective-permute-start | bytes 884744 | tf_op jit(solution)/shard_map/ppermute | solution.py:18
  305.7 33.1 %collective-permute-start.52 = (bf16[4,32,4096]{2,1,0:T(8,128)(2,1)S(1)}, bf16[4,32,4096]{2,1,0:T(8,128)(2,1)S(1)}, u32[]{:S(2)}, u32[]{:S(2)}) collective-permute-start(bf16[4,32,4096]{2,1,0:T(8,128)(2,1)S(1)} %constant_dynamic-update-slice_fusion.12.own_ref), channel_id=1, source_target_pairs={{0,2},{2,0},{1,3},{3,1},{4,6},{6,4},{5,7},{7,5},{8,10},{10,8},{9,1... | collective-permute-start | bytes 3145736 | tf_op jit(solution)/shard_map/ppermute | solution.py:18
  318.3 30.3 %collective-permute-start.50 = (bf16[2,32,4096]{2,1,0:T(8,128)(2,1)}, bf16[2,32,4096]{2,1,0:T(8,128)(2,1)S(1)}, u32[]{:S(2)}, u32[]{:S(2)}) collective-permute-start(bf16[2,32,4096]{2,1,0:T(8,128)(2,1)} %get-tuple-element.371), channel_id=1, source_target_pairs={{0,4},{4,0},{8,12},{12,8},{1,5},{5,1},{9,13},{13,9},{2,6},{6,2},{1... | collective-permute-start | bytes 1572872 | tf_op jit(solution)/shard_map/ppermute | solution.py:27
  322.4 22.9 %collective-permute-start.51 = (bf16[4,32,1152]{2,1,0:T(8,128)(2,1)S(1)}, bf16[4,32,1152]{2,1,0:T(8,128)(2,1)S(1)}, u32[]{:S(2)}, u32[]{:S(2)}) collective-permute-start(bf16[4,32,1152]{2,1,0:T(8,128)(2,1)S(1)} %pad_maximum_fusion.8), channel_id=1, source_target_pairs={{0,2},{2,0},{1,3},{3,1},{4,6},{6,4},{5,7},{7,5},{8,10},{10,8},{9,1... | collective-permute-start | bytes 884744 | tf_op jit(solution)/shard_map/ppermute | solution.py:18
  322.5 135.6 %collective-permute-start.49 = (bf16[128,4096]{1,0:T(8,128)(2,1)}, bf16[128,4096]{1,0:T(8,128)(2,1)}, u32[]{:S(2)}, u32[]{:S(2)}) collective-permute-start(bf16[128,4096]{1,0:T(8,128)(2,1)} %pad_maximum_fusion), channel_id=1, source_target_pairs={{0,16},{16,0},{1,17},{17,1},{2,18},{18,2},{3,19},{19,3},{4,20},{20... | collective-permute-start | bytes 3145736 | tf_op jit(solution)/shard_map/ppermute | solution.py:31
  347.1 24.9 %collective-permute-start.59 = (bf16[32,9216]{1,0:T(8,128)(2,1)S(1)}, bf16[32,9216]{1,0:T(8,128)(2,1)S(1)}, u32[]{:S(2)}, u32[]{:S(2)}) collective-permute-start(bf16[32,9216]{1,0:T(8,128)(2,1)S(1)} %get-tuple-element.285), channel_id=1, source_target_pairs={{0,16},{16,0},{1,17},{17,1},{2,18},{18,2},{3,19},{19,3},{4,20},{20... | collective-permute-start | bytes 1769480 | tf_op jit(solution)/shard_map/ppermute | solution.py:31
  348.7 21.7 %collective-permute-start.55 = (bf16[2,32,1152]{2,1,0:T(8,128)(2,1)S(1)}, bf16[2,32,1152]{2,1,0:T(8,128)(2,1)S(1)}, u32[]{:S(2)}, u32[]{:S(2)}) collective-permute-start(bf16[2,32,1152]{2,1,0:T(8,128)(2,1)S(1)} %get-tuple-element.289), channel_id=1, source_target_pairs={{0,8},{4,12},{8,0},{12,4},{1,9},{5,13},{9,1},{13,5},{2,10},{6,14},... | collective-permute-start | bytes 442376 | tf_op jit(solution)/shard_map/ppermute | solution.py:27
  370.3 22.9 %collective-permute-start.54 = (bf16[4,32,4096]{2,1,0:T(8,128)(2,1)S(1)}, bf16[4,32,4096]{2,1,0:T(8,128)(2,1)S(1)}, u32[]{:S(2)}, u32[]{:S(2)}) collective-permute-start(bf16[4,32,4096]{2,1,0:T(8,128)(2,1)S(1)} %constant_dynamic-update-slice_fusion.17.own_ref), channel_id=1, source_target_pairs={{0,2},{2,0},{1,3},{3,1},{4,6},{6,4},{5,7},{7,5},{8,10},{10,8},{9,1... | collective-permute-start | bytes 3145736 | tf_op jit(solution)/shard_map/ppermute | solution.py:18
  393.2 21.9 %collective-permute-start.60 = (bf16[32,9216]{1,0:T(8,128)(2,1)S(1)}, bf16[32,9216]{1,0:T(8,128)(2,1)S(1)}, u32[]{:S(2)}, u32[]{:S(2)}) collective-permute-start(bf16[32,9216]{1,0:T(8,128)(2,1)S(1)} %get-tuple-element.297), channel_id=1, source_target_pairs={{0,16},{16,0},{1,17},{17,1},{2,18},{18,2},{3,19},{19,3},{4,20},{20... | collective-permute-start | bytes 1769480 | tf_op jit(solution)/shard_map/ppermute | solution.py:31
  410.4 32.2 %collective-permute-start.61 = (bf16[2,32,1152]{2,1,0:T(8,128)(2,1)S(1)}, bf16[2,32,1152]{2,1,0:T(8,128)(2,1)S(1)}, u32[]{:S(2)}, u32[]{:S(2)}) collective-permute-start(bf16[2,32,1152]{2,1,0:T(8,128)(2,1)S(1)} %get-tuple-element.310), channel_id=1, source_target_pairs={{0,8},{4,12},{8,0},{12,4},{1,9},{5,13},{9,1},{13,5},{2,10},{6,14},... | collective-permute-start | bytes 442376 | tf_op jit(solution)/shard_map/ppermute | solution.py:27
  413.9 28.8 %collective-permute-start.62 = (bf16[2,32,1152]{2,1,0:T(8,128)(2,1)S(1)}, bf16[2,32,1152]{2,1,0:T(8,128)(2,1)S(1)}, u32[]{:S(2)}, u32[]{:S(2)}) collective-permute-start(bf16[2,32,1152]{2,1,0:T(8,128)(2,1)S(1)} %get-tuple-element.311), channel_id=1, source_target_pairs={{0,4},{4,0},{8,12},{12,8},{1,5},{5,1},{9,13},{13,9},{2,6},{6,2},{1... | collective-permute-start | bytes 442376 | tf_op jit(solution)/shard_map/ppermute | solution.py:27
  413.9 28.8 %collective-permute-start.63 = (bf16[2,32,1152]{2,1,0:T(8,128)(2,1)S(1)}, bf16[2,32,1152]{2,1,0:T(8,128)(2,1)S(1)}, u32[]{:S(2)}, u32[]{:S(2)}) collective-permute-start(bf16[2,32,1152]{2,1,0:T(8,128)(2,1)S(1)} %get-tuple-element.312), channel_id=1, source_target_pairs={{0,12},{4,8},{8,4},{12,0},{1,13},{5,9},{9,5},{13,1},{2,14},{6,10},... | collective-permute-start | bytes 442376 | tf_op jit(solution)/shard_map/ppermute | solution.py:27
  415.1 29.2 %collective-permute-start.65 = (bf16[576,4096]{1,0:T(8,128)(2,1)}, bf16[576,4096]{1,0:T(8,128)(2,1)}, u32[]{:S(2)}, u32[]{:S(2)}) collective-permute-start(bf16[576,4096]{1,0:T(8,128)(2,1)} %convolution_convert_fusion), channel_id=1, source_target_pairs={{0,1},{1,0},{2,3},{3,2},{4,5},{5,4},{6,7},{7,6},{8,9},{9,8},{10,11... | collective-permute-start | bytes 14155784 | tf_op jit(solution)/shard_map/ppermute | solution.py:22
  492.2 58.3 %collective-permute-start.77 = (f32[1,13056]{1,0:T(1,128)S(1)}, f32[1,13056]{1,0:T(1,128)S(1)}, u32[]{:S(2)}, u32[]{:S(2)}) collective-permute-start(f32[1,13056]{1,0:T(1,128)S(1)} %broadcast_in_dim.16), channel_id=1, source_target_pairs={{0,2},{2,0},{1,3},{3,1},{4,6},{6,4},{5,7},{7,5},{8,10},{10,8},{9,1... | collective-permute-start | bytes 156680 | tf_op jit(solution)/shard_map/ppermute | solution.py:18
  (124 other events, 1565.8 us)
Sparse Core Ops, SparseCore 0:
  9.6 24.2 all-gather.2
